TPU v7x, 256 devices: a whole 4x4x8 slice. The times are simulated.
256 devices in a mesh: gx: 16 (over y, x_hi, core), gy: 16 (over x_lo, z).
Axes of the slice: x: 4 (x_hi: 2, x_lo: 2; x = x_hi * 2 + x_lo), y: 4, z: 8, core: 2. Of those that a mesh axis runs over, the one named last changes fastest.
Arguments:
- noise: float32 [16, 2048, 2048], P(None, 'gx', 'gy'), may hold values from -6 to 6
- biofilm: int32 [16, 2048, 2048], P(None, 'gx', 'gy'), may hold values from 0 to 15
- source: float32 [16, 2048, 2048], P(None, 'gx', 'gy'), may hold values from -8 to 8
Outputs:
- pressure: float32 [16, 2048, 2048], P(None, 'gx', 'gy')
- residual: float32 [16, 2048, 2048], P(None, 'gx', 'gy')
All inputs are finite; a program needn't handle non-finite values.
Results may differ from a plain program's by a relative error of at most 0.02.
Values sent between devices are 32-bit elements; how exact they have to be, the bound alone decides.
No kernel may reach another device: no remote copies, remote signals or barrier semaphores. Data moves between devices by JAX's collectives and lax.ppermute only.
A program may use at most 64 MiB of HBM per device.

v0:
```python
import jax
import jax.numpy as jnp
from jax import lax
from jax.sharding import PartitionSpec as P

R = 64
ITERS = 3


def padded_2(block, sides, width):
    for axis, dim in sides:
        count = lax.axis_size(axis)
        forward = [(i, i + 1) for i in range(count - 1)]
        forward.append((count - 1, 0))
        backward = [(target, source) for source, target in forward]
        low = lax.ppermute(
            lax.slice_in_dim(block, block.shape[dim] - width, None, axis=dim), axis, forward
        )
        high = lax.ppermute(lax.slice_in_dim(block, 0, width, axis=dim), axis, backward)
        block = jnp.concatenate([low, block, high], axis=dim)
    return block


def band_matrix(length_in, length_out):
    rows = lax.broadcasted_iota(jnp.int32, (length_in, length_out), 0)
    cols = lax.broadcasted_iota(jnp.int32, (length_in, length_out), 1)
    offset = rows - cols
    inside = (offset >= 0) & (offset <= 2 * R)
    return jnp.where(inside, 1.0 / float(2 * R + 1) ** 0.5, 0.0).astype(jnp.float32)


def smooth_first(field, length_out):
    weights = band_matrix(field.shape[1], length_out)
    return jnp.einsum("zxy,xo->zoy", field, weights, precision=lax.Precision.HIGHEST)


def smooth_second(field, length_out):
    weights = band_matrix(field.shape[2], length_out)
    return jnp.einsum("zxy,yo->zxo", field, weights, precision=lax.Precision.HIGHEST)


def kozeny(biofilm):
    fraction = 0.06 * biofilm.astype(jnp.float32)
    porosity = 0.35 * (1.0 - fraction)
    ratio = (1.0 - 0.35) / (1.0 - porosity)
    return (1.0 - fraction) ** 3 * ratio * ratio


def harmonic(left, right):
    return 2.0 * left * right / (left + right)


def operate(field, trans_x, trans_y, trans_z):
    padded = padded_2(field, (("gx", 1), ("gy", 2)), 1)
    flux_x = trans_x * (padded[:, 1:, 1:-1] - padded[:, :-1, 1:-1])
    flux_y = trans_y * (padded[:, 1:-1, 1:] - padded[:, 1:-1, :-1])
    flux_z = trans_z * (field[1:] - field[:-1])
    zeros = jnp.zeros_like(field[:1])
    result = 0.5 * field + flux_x[:, :-1, :] - flux_x[:, 1:, :]
    result = result + flux_y[:, :, :-1] - flux_y[:, :, 1:]
    result = result + jnp.concatenate([zeros, flux_z], 0) - jnp.concatenate([flux_z, zeros], 0)
    return result


def squares(residual):
    return lax.psum(jnp.sum(residual * residual), ("gx", "gy"))


def local(noise, biofilm, source):
    cells_x = noise.shape[1]
    cells_y = noise.shape[2]
    extended = padded_2(noise, (("gx", 1), ("gy", 2)), R)
    smooth_x = smooth_first(extended, cells_x)
    logperm = smooth_second(smooth_x, cells_y)
    perm = jnp.exp(logperm) * kozeny(biofilm)
    perm_pad = padded_2(perm, (("gx", 1), ("gy", 2)), 1)
    trans_x = harmonic(perm_pad[:, :-1, 1:-1], perm_pad[:, 1:, 1:-1])
    trans_y = harmonic(perm_pad[:, 1:-1, :-1], perm_pad[:, 1:-1, 1:])
    trans_z = harmonic(perm[:-1], perm[1:])
    pressure = jnp.zeros_like(source)
    residual = source
    direction = source
    norm_now = squares(residual)
    for step in range(ITERS):
        image = operate(direction, trans_x, trans_y, trans_z)
        alpha = norm_now / lax.psum(jnp.sum(direction * image), ("gx", "gy"))
        pressure = pressure + alpha * direction
        residual = residual - alpha * image
        norm_next = squares(residual)
        direction = residual + norm_next / norm_now * direction
        norm_now = norm_next
    return (pressure, residual)


def solution(mesh):
    in_specs = (P(None, "gx", "gy"), P(None, "gx", "gy"), P(None, "gx", "gy"))
    out_specs = (P(None, "gx", "gy"), P(None, "gx", "gy"))
    return jax.shard_map(local, mesh=mesh, in_specs=in_specs, out_specs=out_specs, check_vma=False)
```

profile of v0, /device:TPU:1, one launch (start us, length us, event | category | flops | bytes accessed | tf_op | source)
XLA Modules:
  0.0 561.5 jit_solution(11432851373501475404)
XLA Ops:
  2.0 4.2 collective-permute-start
  6.3 7.0 %collective-permute-done = f32[16,64,128]{2,1,0:T(8,128)S(1)} collective-permute-done((f32[16,64,128]{2,1,0:T(8,128)S(1)}, f32[16,64,128]{2,1,0:T(8,128)S(1)}, u32[]{:S(2)}, u32[]{:S(2)}) %collective-permute-start) | collective-permute-done | bytes 524320 | tf_op jit(solution)/shard_map/ppermute | solution.py:16
  13.4 6.6 %collective-permute-done.1 = f32[16,64,128]{2,1,0:T(8,128)S(1)} collective-permute-done((f32[16,64,128]{2,1,0:T(8,128)S(1)}, f32[16,64,128]{2,1,0:T(8,128)S(1)}, u32[]{:S(2)}, u32[]{:S(2)}) %collective-permute-start.1) | collective-permute-done | bytes 524320 | tf_op jit(solution)/shard_map/ppermute | solution.py:19
  20.0 2.7 fusion.56
  22.7 3.1 copy.25
  25.9 6.2 %collective-permute-start.3 = (f32[16,256,64]{1,2,0:T(8,128)}, f32[16,256,64]{1,2,0:T(8,128)}, u32[]{:S(2)}, u32[]{:S(2)}) collective-permute-start(f32[16,256,64]{1,2,0:T(8,128)} %copy.25), channel_id=1, source_target_pairs={{1,0},{2,1},{3,2},{4,3},{5,4},{6,5},{7,6},{8,7},{9,8},{10,9},{11,1... | collective-permute-start | bytes 3145736 | tf_op jit(solution)/shard_map/ppermute | solution.py:19
  32.1 3.1 copy.24
  35.4 3.2 collective-permute-start.7
  38.6 2.5 collective-permute-done.6
  46.7 3.8 collective-permute-start.10
  50.5 12.1 %collective-permute-done.11 = f32[16,130,1]{1,0,2:T(8,128)S(1)} collective-permute-done((f32[16,130,1]{1,0,2:T(8,128)S(1)}, f32[16,130,1]{1,0,2:T(8,128)S(1)}, u32[]{:S(2)}, u32[]{:S(2)}) %collective-permute-start.11) | collective-permute-done | bytes 8352 | tf_op jit(solution)/shard_map/ppermute | solution.py:16
  65.5 3.2 copy.27
  68.6 3.2 copy.26
  71.8 5.8 %fusion = f32[128,16,256]{2,0,1:T(8,128)S(1)} fusion(f32[16,256,64]{2,1,0:T(8,128)} %copy.27, f32[16,256,128]{2,1,0:T(8,128)S(1)} %constant_dynamic-update-slice_fusion, f32[16,256,64]{2,1,0:T(8,128)} %copy.26), kind=kOutput, calls=%fused_computation | convolution fusion | flops 1612873728 | bytes 6291456 | tf_op jit(solution)/shard_map/zxy,xo->zoy/dot_general | solution.py:34
  79.5 5.8 %collective-permute-start.5 = (f32[16,1,128]{2,1,0:T(1,128)S(1)}, f32[16,1,128]{2,1,0:T(1,128)S(1)}, u32[]{:S(2)}, u32[]{:S(2)}) collective-permute-start(f32[16,1,128]{2,1,0:T(1,128)S(1)} %get-tuple-element.28), channel_id=1, source_target_pairs={{16,0},{32,16},{48,32},{64,48},{80,64},{96,80},{112,96},{128,112},... | collective-permute-start | bytes 24584 | tf_op jit(solution)/shard_map/ppermute | solution.py:19
  86.5 7.0 %collective-permute-done.4 = f32[16,1,128]{2,1,0:T(1,128)S(1)} collective-permute-done((f32[16,1,128]{2,1,0:T(1,128)S(1)}, f32[16,1,128]{2,1,0:T(1,128)S(1)}, u32[]{:S(2)}, u32[]{:S(2)}) %collective-permute-start.4) | collective-permute-done | bytes 8224 | tf_op jit(solution)/shard_map/ppermute | solution.py:16
  96.8 2.7 collective-permute-start.9
  102.3 2.8 collective-permute-done.8
  106.5 3.4 fusion.11
  112.1 80.8 %all-reduce.6 = (f32[]{:T(128)}, f32[]{:T(128)}) all-reduce(f32[]{:T(128)} %get-tuple-element.3, f32[]{:T(128)} %get-tuple-element.2), channel_id=1, replica_groups=mesh['gx'=16,'gy'=16] {'gx','gy'}, use_global_device_ids=true, to_apply=%region_1.2 | all-reduce | flops 2 | bytes 16 | tf_op jit(solution)/shard_map/psum | solution.py:66
  196.4 73.4 %psum.44 = f32[]{:T(128)} all-reduce(f32[]{:T(128)} %multiply_reduce_fusion.3), channel_id=1, replica_groups=mesh['gx'=16,'gy'=16] {'gx','gy'}, use_global_device_ids=true, to_apply=%region_5.6 | all-reduce | flops 1 | bytes 8 | tf_op jit(solution)/shard_map/psum | solution.py:66
  273.3 2.6 collective-permute-start.13
  283.6 2.8 collective-permute-start.14
  290.7 3.6 fusion.9
  296.5 77.6 %psum.45 = f32[]{:T(128)} all-reduce(f32[]{:T(128)} %get-tuple-element.10), channel_id=1, replica_groups=mesh['gx'=16,'gy'=16] {'gx','gy'}, use_global_device_ids=true, to_apply=%region_7.8 | all-reduce | flops 1 | bytes 8 | tf_op jit(solution)/shard_map/psum | solution.py:86
  375.4 3.5 multiply_reduce_fusion.1
  378.9 72.8 %psum.46 = f32[]{:T(128)} all-reduce(f32[]{:T(128)} %get-tuple-element.8), channel_id=1, replica_groups=mesh['gx'=16,'gy'=16] {'gx','gy'}, use_global_device_ids=true, to_apply=%region_9.10 | all-reduce | flops 1 | bytes 8 | tf_op jit(solution)/shard_map/psum | solution.py:66
  455.0 2.6 collective-permute-start.17
  468.1 3.0 fusion.22
  474.0 3.9 fusion.7
  480.0 76.4 %psum.47 = f32[]{:T(128)} all-reduce(f32[]{:T(128)} %get-tuple-element.6), channel_id=1, replica_groups=mesh['gx'=16,'gy'=16] {'gx','gy'}, use_global_device_ids=true, to_apply=%region_11.12 | all-reduce | flops 1 | bytes 8 | tf_op jit(solution)/shard_map/psum | solution.py:86
  557.8 3.3 multiply_subtract_fusion
  (95 shorter events, 58.8 us)
Async XLA Ops:
  0.6 12.7 %copy-start.8 = (f32[16,128,128]{2,1,0:T(8,128)S(1)}, f32[16,128,128]{2,1,0:T(8,128)}, u32[]{:S(2)}) copy-start(f32[16,128,128]{2,1,0:T(8,128)} %param.3) | copy-start | bytes 3145732
  2.0 11.2 %collective-permute-start = (f32[16,64,128]{2,1,0:T(8,128)S(1)}, f32[16,64,128]{2,1,0:T(8,128)S(1)}, u32[]{:S(2)}, u32[]{:S(2)}) collective-permute-start(f32[16,64,128]{2,1,0:T(8,128)S(1)} %get-tuple-element.32), channel_id=1, source_target_pairs={{0,16},{16,32},{32,48},{48,64},{64,80},{80,96},{96,112},{112,128},... | collective-permute-start | bytes 1572872 | tf_op jit(solution)/shard_map/ppermute | solution.py:16
  6.3 13.7 %collective-permute-start.1 = (f32[16,64,128]{2,1,0:T(8,128)S(1)}, f32[16,64,128]{2,1,0:T(8,128)S(1)}, u32[]{:S(2)}, u32[]{:S(2)}) collective-permute-start(f32[16,64,128]{2,1,0:T(8,128)S(1)} %get-tuple-element.31), channel_id=1, source_target_pairs={{16,0},{32,16},{48,32},{64,48},{80,64},{96,80},{112,96},{128,112},... | collective-permute-start | bytes 1572872 | tf_op jit(solution)/shard_map/ppermute | solution.py:19
  25.9 9.4 %copy-start = (f32[16,128,128]{2,1,0:T(8,128)S(1)}, f32[16,128,128]{2,1,0:T(8,128)}, u32[]{:S(2)}) copy-start(f32[16,128,128]{2,1,0:T(8,128)} %param.5) | copy-start | bytes 3145732
  25.9 39.6 %collective-permute-start.3 = (f32[16,256,64]{1,2,0:T(8,128)}, f32[16,256,64]{1,2,0:T(8,128)}, u32[]{:S(2)}, u32[]{:S(2)}) collective-permute-start(f32[16,256,64]{1,2,0:T(8,128)} %copy.25), channel_id=1, source_target_pairs={{1,0},{2,1},{3,2},{4,3},{5,4},{6,5},{7,6},{8,7},{9,8},{10,9},{11,1... | collective-permute-start | bytes 3145736 | tf_op jit(solution)/shard_map/ppermute | solution.py:19
  35.2 33.4 %collective-permute-start.2 = (f32[16,256,64]{1,2,0:T(8,128)}, f32[16,256,64]{1,2,0:T(8,128)}, u32[]{:S(2)}, u32[]{:S(2)}) collective-permute-start(f32[16,256,64]{1,2,0:T(8,128)} %copy.24), channel_id=1, source_target_pairs={{0,1},{1,2},{2,3},{3,4},{4,5},{5,6},{6,7},{7,8},{8,9},{9,10},{10,1... | collective-permute-start | bytes 3145736 | tf_op jit(solution)/shard_map/ppermute | solution.py:16
  35.3 5.9 %collective-permute-start.6 = (f32[16,1,128]{2,1,0:T(1,128)S(1)}, f32[16,1,128]{2,1,0:T(1,128)S(1)}, u32[]{:S(2)}, u32[]{:S(2)}) collective-permute-start(f32[16,1,128]{2,1,0:T(1,128)S(1)} %get-tuple-element.30), channel_id=1, source_target_pairs={{16,0},{32,16},{48,32},{64,48},{80,64},{96,80},{112,96},{128,112},... | collective-permute-start | bytes 24584 | tf_op jit(solution)/shard_map/ppermute | solution.py:19
  35.4 5.8 %collective-permute-start.7 = (f32[16,1,128]{2,1,0:T(1,128)S(1)}, f32[16,1,128]{2,1,0:T(1,128)S(1)}, u32[]{:S(2)}, u32[]{:S(2)}) collective-permute-start(f32[16,1,128]{2,1,0:T(1,128)S(1)} %get-tuple-element.29), channel_id=1, source_target_pairs={{0,16},{16,32},{32,48},{48,64},{64,80},{80,96},{96,112},{112,128},... | collective-permute-start | bytes 24584 | tf_op jit(solution)/shard_map/ppermute | solution.py:16
  44.8 17.8 %collective-permute-start.11 = (f32[16,130,1]{1,0,2:T(8,128)S(1)}, f32[16,130,1]{1,0,2:T(8,128)S(1)}, u32[]{:S(2)}, u32[]{:S(2)}) collective-permute-start(f32[16,130,1]{1,0,2:T(8,128)S(1)} %copy.35), channel_id=1, source_target_pairs={{0,1},{1,2},{2,3},{3,4},{4,5},{5,6},{6,7},{7,8},{8,9},{9,10},{10,1... | collective-permute-start | bytes 24968 | tf_op jit(solution)/shard_map/ppermute | solution.py:16
  46.7 17.3 %collective-permute-start.10 = (f32[16,130,1]{1,0,2:T(8,128)S(1)}, f32[16,130,1]{1,0,2:T(8,128)S(1)}, u32[]{:S(2)}, u32[]{:S(2)}) collective-permute-start(f32[16,130,1]{1,0,2:T(8,128)S(1)} %copy.33), channel_id=1, source_target_pairs={{1,0},{2,1},{3,2},{4,3},{5,4},{6,5},{7,6},{8,7},{9,8},{10,9},{11,1... | collective-permute-start | bytes 24968 | tf_op jit(solution)/shard_map/ppermute | solution.py:19
  71.8 5.8 %copy-start.12 = (s32[16,128,128]{2,1,0:T(8,128)S(1)}, s32[16,128,128]{2,1,0:T(8,128)}, u32[]{:S(2)}) copy-start(s32[16,128,128]{2,1,0:T(8,128)} %param.4) | copy-start | bytes 3145732
  79.5 7.0 %collective-permute-start.5 = (f32[16,1,128]{2,1,0:T(1,128)S(1)}, f32[16,1,128]{2,1,0:T(1,128)S(1)}, u32[]{:S(2)}, u32[]{:S(2)}) collective-permute-start(f32[16,1,128]{2,1,0:T(1,128)S(1)} %get-tuple-element.28), channel_id=1, source_target_pairs={{16,0},{32,16},{48,32},{64,48},{80,64},{96,80},{112,96},{128,112},... | collective-permute-start | bytes 24584 | tf_op jit(solution)/shard_map/ppermute | solution.py:19
  85.3 8.2 %collective-permute-start.4 = (f32[16,1,128]{2,1,0:T(1,128)S(1)}, f32[16,1,128]{2,1,0:T(1,128)S(1)}, u32[]{:S(2)}, u32[]{:S(2)}) collective-permute-start(f32[16,1,128]{2,1,0:T(1,128)S(1)} %get-tuple-element.27), channel_id=1, source_target_pairs={{0,16},{16,32},{32,48},{48,64},{64,80},{80,96},{96,112},{112,128},... | collective-permute-start | bytes 24584 | tf_op jit(solution)/shard_map/ppermute | solution.py:16
  96.8 5.0 collective-permute-start.9
  100.1 5.0 collective-permute-start.8
  102.3 7.7 %copy-start.4 = (f32[16,130,1]{2,1,0:T(8,128)}, f32[16,130,1]{2,1,0:T(8,128)S(1)}, u32[]{:S(2)}) copy-start(f32[16,130,1]{2,1,0:T(8,128)S(1)} %copy.32) | copy-start | bytes 24964
  106.5 3.5 copy-start.11
  272.5 4.7 collective-permute-start.12
  273.3 3.9 collective-permute-start.13
  280.9 6.9 %collective-permute-start.15 = (f32[16,130,1]{1,0,2:T(8,128)S(1)}, f32[16,130,1]{1,0,2:T(8,128)S(1)}, u32[]{:S(2)}, u32[]{:S(2)}) collective-permute-start(f32[16,130,1]{1,0,2:T(8,128)S(1)} %copy.39), channel_id=1, source_target_pairs={{0,1},{1,2},{2,3},{3,4},{4,5},{5,6},{6,7},{7,8},{8,9},{9,10},{10,1... | collective-permute-start | bytes 24968 | tf_op jit(solution)/shard_map/ppermute | solution.py:16
  283.6 5.6 %collective-permute-start.14 = (f32[16,130,1]{1,0,2:T(8,128)S(1)}, f32[16,130,1]{1,0,2:T(8,128)S(1)}, u32[]{:S(2)}, u32[]{:S(2)}) collective-permute-start(f32[16,130,1]{1,0,2:T(8,128)S(1)} %copy.37), channel_id=1, source_target_pairs={{1,0},{2,1},{3,2},{4,3},{5,4},{6,5},{7,6},{8,7},{9,8},{10,9},{11,1... | collective-permute-start | bytes 24968 | tf_op jit(solution)/shard_map/ppermute | solution.py:19
  290.7 3.6 copy-start.6
  290.7 3.6 copy-start.10
  454.2 4.7 copy-start.1
  454.3 4.7 collective-permute-start.16
  455.0 3.9 collective-permute-start.17
  462.6 8.5 %collective-permute-start.19 = (f32[16,130,1]{1,0,2:T(8,128)S(1)}, f32[16,130,1]{1,0,2:T(8,128)S(1)}, u32[]{:S(2)}, u32[]{:S(2)}) collective-permute-start(f32[16,130,1]{1,0,2:T(8,128)S(1)} %copy.43), channel_id=1, source_target_pairs={{0,1},{1,2},{2,3},{3,4},{4,5},{5,6},{6,7},{7,8},{8,9},{9,10},{10,1... | collective-permute-start | bytes 24968 | tf_op jit(solution)/shard_map/ppermute | solution.py:16
  466.3 6.2 %collective-permute-start.18 = (f32[16,130,1]{1,0,2:T(8,128)S(1)}, f32[16,130,1]{1,0,2:T(8,128)S(1)}, u32[]{:S(2)}, u32[]{:S(2)}) collective-permute-start(f32[16,130,1]{1,0,2:T(8,128)S(1)} %copy.41), channel_id=1, source_target_pairs={{1,0},{2,1},{3,2},{4,3},{5,4},{6,5},{7,6},{8,7},{9,8},{10,9},{11,1... | collective-permute-start | bytes 24968 | tf_op jit(solution)/shard_map/ppermute | solution.py:19
  474.0 4.0 copy-start.2
  474.0 4.0 copy-start.5
  474.0 4.0 copy-start.9
  478.0 79.8 %copy-start.3 = (f32[16,128,128]{2,1,0:T(8,128)S(1)}, f32[16,128,128]{2,1,0:T(8,128)}, u32[]{:S(2)}) copy-start(f32[16,128,128]{2,1,0:T(8,128)} %copy-done.1) | copy-start | bytes 3145732
  (1 other events, 3.4 us)
where the time goes:
time: 569 us; the launch traced here: 562 us
  blocking collectives  381 us (67%)
  local copies, waits for them, and re-layouts  47.6 us (8%)
  starting transfers between devices  40.4 us (7%)
  other arithmetic  38.6 us (7%)
  waiting for transfers between devices  38.4 us (7%)
  between operations  7.97 us (1%)
  matrix products  7.63 us (1%)
    psum x3, blocking collectives, squares(): return lax.psum(jnp.sum(residual * residual), ('gx', 'gy'))  227 us
    psum x2, blocking collectives, local(): alpha = norm_now / lax.psum(jnp.sum(direction * image), ('gx', 'gy'))  154 us
    ppermute x10, waiting for transfers between devices, padded_2(): lax.ppermute(lax.slice_in_dim(block, block.shape[dim] - width, None, axis...  29 us
    ppermute x10, starting transfers between devices, padded_2(): lax.ppermute(lax.slice_in_dim(block, 0, width, axis=dim), axis, backward)  24.7 us
    slice x9, local copies, waits for them, and re-layouts, padded_2(): lax.slice_in_dim(block, 0, width, axis=dim)  17.1 us
    ppermute x10, starting transfers between devices, padded_2(): lax.ppermute(lax.slice_in_dim(block, block.shape[dim] - width, None, axis...  15.7 us
    slice x11, local copies, waits for them, and re-layouts, padded_2(): lax.slice_in_dim(block, block.shape[dim] - width, None, axis=dim)  13.4 us
  transfers between devices with their start and end apart: 20, of which 8 were waited for; matrix products, arithmetic and copies ran while one was open for 6% of the time, Pallas kernels for 0%

commit v1 on v0

v1 whole, which is shorter than its diff:
```python
import jax
import jax.numpy as jnp
from jax import lax
from jax.experimental import pallas as pl
from jax.experimental.pallas import tpu as pltpu
from jax.sharding import PartitionSpec as P

R = 64
WIDTH = 2 * R + 1
NZ = 16
N = 128
F32 = jnp.float32
BF16 = jnp.bfloat16

MSG_Y = 8 * N + N + 16
MSG_X = 17 * 72 + 24
ROWS = 160
OWN = 16
HUGE = 1e30


def iota(shape, dim):
    return lax.broadcasted_iota(jnp.int32, shape, dim)


def roll(x, shift, axis):
    if isinstance(shift, int):
        shift = shift % x.shape[axis]
        if shift == 0:
            return x
    return pltpu.roll(x, shift, axis)


def split3(x):
    high = x.astype(BF16)
    rest = x - high.astype(F32)
    middle = rest.astype(BF16)
    low = (rest - middle.astype(F32)).astype(BF16)
    return high, middle, low


def dot(a, b):
    return lax.dot_general(a, b, (((1,), (0,)), ((), ())), preferred_element_type=F32)


def weights(mask):
    return jnp.where(mask, 1.0, 0.0).astype(BF16)


def pack_columns(noise, source, biofilm, to_right, to_left):
    lane = iota((16, N), 1)
    slot = lane % 8
    group = lane // 8
    low = lane < 64

    third_right = jnp.zeros((16, N), F32)
    third_left = jnp.zeros((16, N), F32)
    for g in range(8):
        rows = slice(16 * g, 16 * g + 16)
        zero = jnp.zeros((16, N), F32)
        nr, sr, nl, sl = zero, zero, zero, zero
        br = jnp.zeros((16, N), jnp.int32)
        bl = br
        for q in range(8):
            even = noise[2 * q, rows, :]
            odd = noise[2 * q + 1, rows, :]
            to_right[q * N + 16 * g : q * N + 16 * g + 16, :] = jnp.where(low, roll(even, 64, 1), odd)
            to_left[q * N + 16 * g : q * N + 16 * g + 16, :] = jnp.where(low, even, roll(odd, 64, 1))
            for z, n in ((2 * q, even), (2 * q + 1, odd)):
                here = group == z
                s = source[z, rows, :]
                b = biofilm[z, rows, :]
                nr = jnp.where(here, roll(n, 8 * z - 61, 1), nr)
                nl = jnp.where(here, roll(n, 8 * z + 5 - 64, 1), nl)
                sr = jnp.where(here, roll(s, 8 * z + 8, 1), sr)
                sl = jnp.where(here, roll(s, 8 * z, 1), sl)
                br = jnp.where(here, roll(b, 8 * z + 8, 1), br)
                bl = jnp.where(here, roll(b, 8 * z, 1), bl)
        br = br.astype(F32)
        bl = bl.astype(F32)
        to_right[8 * N + 16 * g : 8 * N + 16 * g + 16, :] = jnp.where(
            slot < 3, nr, jnp.where(slot < 5, roll(br, -3, 1), sr)
        )
        to_left[8 * N + 16 * g : 8 * N + 16 * g + 16, :] = jnp.where(
            slot < 3, sl, jnp.where(slot < 5, roll(bl, 3, 1), nl)
        )
        third_right = third_right + roll(jnp.where(slot == 5, br, 0.0), g, 1)
        third_left = third_left + roll(jnp.where(slot == 2, bl, 0.0), g, 1)
    to_right[9 * N :, :] = third_right
    to_left[9 * N :, :] = third_left


def column_weights():
    m = iota((N, 2 * N), 0)
    o = iota((N, 2 * N), 1)
    s = o - N
    own = ((o < N) & (m - o <= R) & (o - m <= R)) | ((o >= N) & (s <= 2) & (m >= s + 64)) | (
        (s >= 5) & (s <= 7) & (m <= s + 56)
    )
    lane = iota((N, 3 * N), 0)
    o = iota((N, 3 * N), 1)
    half = lane // 64
    m = lane % 64
    e = o - 2 * N
    same = (o < 2 * N) & (o // N == half)
    edge = (e >= 0) & (e < 16) & (e // 8 == half)
    left = (same & (m >= o % N)) | (edge & (o % 8 >= 5))
    right = (same & (m + 64 <= o % N)) | (edge & (o % 8 <= 2))
    a = iota((N, N), 0)
    b = iota((N, N), 1)
    together = a // 8 == b // 8
    t = a % 8
    s = b % 8
    left_extra = together & (t <= 2) & (s >= 5) & (t >= s - 5)
    right_extra = together & (t >= 5) & (s <= 2) & (t - 5 <= s)
    return [weights(w) for w in (own, left, right, left_extra, right_extra)]


def smooth_columns(
    noise, source, biofilm, from_left, from_right, middle, edge, edge_source, edge_biofilm, to_down, to_up
):
    own, left, right, left_extra, right_extra = column_weights()
    slot = iota((N, N), 1) % 8

    def times(x, w):
        high, mid, low = split3(x)
        return dot(high, w) + dot(mid, w) + dot(low, w)

    extra_left = from_left[8 * N : 9 * N, :]
    extra_right = from_right[8 * N : 9 * N, :]
    total = times(extra_left, left_extra) + times(extra_right, right_extra)
    for q in range(8):
        halo = times(from_left[q * N : q * N + N, :], left) + times(from_right[q * N : q * N + N, :], right)
        total = total + roll(halo[:, 2 * N :], 16 * q, 1)
        for z in (2 * q, 2 * q + 1):
            out = times(noise[z], own)
            total = total + roll(out[:, N:], 8 * z, 1)
            field = out[:, :N] + halo[:, (z % 2) * N : (z % 2) * N + N]
            middle[z] = field
            to_down[z * 72 : z * 72 + 72, :] = field[56:, :]
            to_up[z * 72 : z * 72 + 72, :] = field[:72, :]
    edge[...] = total
    to_down[16 * 72 : 17 * 72, :] = total[56:, :]
    to_up[16 * 72 : 17 * 72, :] = total[:72, :]

    edge_source[...] = jnp.where(slot >= 5, extra_left, jnp.where(slot <= 2, extra_right, 0.0))
    third_left = from_left[9 * N :, :]
    third_right = from_right[9 * N :, :]
    levels = jnp.where(slot >= 6, roll(extra_left, 3, 1), jnp.where(slot <= 1, roll(extra_right, -3, 1), 0.0))
    slot16 = iota((16, N), 1) % 8
    for g in range(8):
        rows = slice(16 * g, 16 * g + 16)
        edge_biofilm[rows, :] = jnp.where(
            slot16 == 5, roll(third_left, -g, 1), jnp.where(slot16 == 2, roll(third_right, -g, 1), levels[rows, :])
        )

    to_down[17 * 72 :, :] = jnp.zeros((24, N), F32)
    to_up[17 * 72 :, :] = jnp.zeros((24, N), F32)
    for z in range(17):
        s = source.at[z] if z < 16 else edge_source
        b = biofilm.at[z] if z < 16 else edge_biofilm
        to_down[z * 72 : z * 72 + 3, :] = s[125:128, :]
        to_down[z * 72 + 3 : z * 72 + 5, :] = b[126:128, :].astype(F32)
        to_down[17 * 72 + z : 17 * 72 + z + 1, :] = b[125:126, :].astype(F32)
        to_up[z * 72 + 67 : z * 72 + 70, :] = s[0:3, :]
        to_up[z * 72 + 70 : z * 72 + 72, :] = b[0:2, :].astype(F32)
        to_up[17 * 72 + z : 17 * 72 + z + 1, :] = b[2:3, :].astype(F32)


def row_weights():
    r = iota((144, N), 0) - 8
    m = iota((144, N), 1)
    inside = (r >= -3) & (r <= 130)
    own = inside & (m >= r - R) & (m <= r + R)
    r = iota((144, 72), 0) - 8
    m = iota((144, 72), 1)
    inside = (r >= -3) & (r <= 130)
    up = inside & (m >= 5) & (m >= r + 8)
    down = inside & (m <= 66) & (m <= r - R)
    return [weights(w) for w in (own, up, down)]


def resistance(logperm, biofilm, top):
    open_part = 1.0 - 0.06 * biofilm
    solid = (1.0 - 0.35 * open_part) * (1.0 / (1.0 - 0.35))
    value = jnp.exp(top - logperm) * (0.5 * solid * solid) / (open_part * open_part * open_part)
    return jnp.minimum(value, HUGE)


def chunks():
    return [(8, 48), (56, 48), (104, 48)]


def operate_powers(
    middle, edge, edge_source, edge_biofilm, source, biofilm, from_up, from_down,
    power1, power2, power3, table,
    resist, across_x, across_y, across_z, edge_right, field0, field1, field2, field3,
):
    lane = iota((8, N), 1)
    row8 = iota((8, N), 0)

    own, up, down = row_weights()
    edge_lane = (iota((144, N), 1) % 8 <= 2) | (iota((144, N), 1) % 8 >= 5)
    row144 = iota((144, N), 0)
    real_row = (row144 >= 5) & (row144 <= 138)

    def plane_logperm(data, z, real):
        total = jnp.zeros((144, N), F32)
        first = pl.multiple_of(z * 72, 8)
        for w, part in ((own, data), (up, from_up[pl.ds(first, 72), :]), (down, from_down[pl.ds(first, 72), :])):
            for piece in split3(part):
                total = total + dot(w, piece)
        total = total * (1.0 / WIDTH)
        resist[z, 8:152, :] = total
        return jnp.max(jnp.where(real, total, -HUGE).reshape(18, 8, N), axis=0)

    def smooth(z, largest):
        return jnp.maximum(largest, plane_logperm(middle[z], z, real_row))

    largest = plane_logperm(edge[...], 16, real_row & edge_lane)
    largest = lax.fori_loop(0, 16, smooth, largest)
    top = jnp.max(jnp.max(largest, axis=0, keepdims=True), axis=1, keepdims=True)
    top = jnp.maximum(top, -60.0)

    def halo_tiles(z):
        first = pl.multiple_of(z * 72, 8)
        above = from_up[pl.ds(first, 8), :]
        below = from_down[pl.ds(first + 64, 8), :]
        third_above = from_up[pl.ds(17 * 72 + z, 1), :]
        third_below = from_down[pl.ds(17 * 72 + z, 1), :]
        source_above = jnp.where(row8 >= 5, roll(above, 5, 0), 0.0)
        source_below = jnp.where(row8 <= 2, roll(below, 5, 0), 0.0)
        biofilm_above = jnp.where(row8 == 5, third_above, jnp.where(row8 >= 6, roll(above, 3, 0), 0.0))
        biofilm_below = jnp.where(row8 == 2, third_below, jnp.where(row8 <= 1, roll(below, 2, 0), 0.0))
        return source_above, source_below, biofilm_above, biofilm_below

    def prepare(z, own_source, own_biofilm, real8, real):
        source_above, source_below, biofilm_above, biofilm_below = halo_tiles(z)
        field0[z, 8:16, :] = source_above
        field0[z, 16:144, :] = own_source
        field0[z, 144:152, :] = source_below
        resist[z, 8:16, :] = jnp.where(
            real8 & (row8 >= 5), resistance(resist[z, 8:16, :], biofilm_above, top), HUGE
        )
        resist[z, 144:152, :] = jnp.where(
            real8 & (row8 <= 2), resistance(resist[z, 144:152, :], biofilm_below, top), HUGE
        )
        value = resistance(resist[z, 16:144, :], own_biofilm, top)
        resist[z, 16:144, :] = value if real is None else jnp.where(real, value, HUGE)
        empty = jnp.full((8, N), HUGE, F32)
        resist[z, 0:8, :] = empty
        resist[z, 152:160, :] = empty
        none = jnp.zeros((8, N), F32)
        for f in (field0, field1, field2):
            f[z, 0:8, :] = none
            f[z, 152:160, :] = none

    def prepare_layer(z, carry):
        prepare(z, source[z], biofilm[z].astype(F32), row8 >= 0, None)
        return carry

    slot128 = iota((N, N), 1) % 8
    slot8 = lane % 8
    prepare(
        16, edge_source[...], edge_biofilm[...],
        (slot8 <= 2) | (slot8 >= 5), (slot128 <= 2) | (slot128 >= 5),
    )
    lax.fori_loop(0, 16, prepare_layer, 0)

    lane48 = iota((48, N), 1)
    slot48 = lane48 % 8

    def block_ends(field, start, size):
        ends = jnp.zeros((size, N), F32)
        for z in range(16):
            ends = jnp.where(lane48 >= 8 * z, roll(field[z, start : start + size, :], 8 * z + 1, 1), ends)
        return ends

    def edge_neighbours(field, start, size):
        ends = block_ends(field, start, size)
        here = field[16, start : start + size, :]
        left = jnp.where(slot48 == 0, ends, roll(here, 1, 1))
        right = jnp.where(slot48 == 7, roll(ends, 6, 1), roll(here, -1, 1))
        return here, left, right

    for start, size in chunks():
        here, left, right = edge_neighbours(resist, start, size)
        before = resist[16, start - 1 : start - 1 + size, :]
        across_x[16, start : start + size, :] = 1.0 / (here + before)
        across_y[16, start : start + size, :] = 1.0 / (here + left)
        edge_right[start : start + size, :] = 1.0 / (here + right)
        across_z[16, start : start + size, :] = jnp.where(
            lane48 < 120, 1.0 / (here + roll(here, -8, 1)), 0.0
        )
    across_x[16, 152:160, :] = jnp.zeros((8, N), F32)

    def faces(z, carry):
        across_x[z, 152:160, :] = jnp.zeros((8, N), F32)
        for start, size in chunks():
            rows = slice(start, start + size)
            here = resist[z, rows, :]
            before = resist[z, start - 1 : start - 1 + size, :]
            outer = resist[16, rows, :]
            left = jnp.where(lane48 == 0, roll(outer, 121 - 8 * z, 1), roll(here, 1, 1))
            across_x[z, rows, :] = 1.0 / (here + before)
            across_y[z, rows, :] = 1.0 / (here + left)
            above = resist[jnp.maximum(z - 1, 0), rows, :]
            across_z[z, rows, :] = jnp.where(z > 0, 1.0 / (here + above), 0.0)
        return carry

    lax.fori_loop(0, 16, faces, 0)

    def apply(field, image, flux):
        for start, size in chunks():
            rows = slice(start, start + size)
            here, left, right = edge_neighbours(field, start, size)
            inward = across_y[16, rows, :] * (here - left)
            flux[rows, :] = inward
            value = inward - edge_right[rows, :] * (right - here)
            value = value + across_x[16, rows, :] * (here - field[16, start - 1 : start - 1 + size, :])
            value = value - across_x[16, start + 1 : start + 1 + size, :] * (
                field[16, start + 1 : start + 1 + size, :] - here
            )
            through = across_z[16, rows, :] * (roll(here, -8, 1) - here)
            image[16, rows, :] = value - through + roll(through, 8, 1)

        def layer(z, carry):
            for start, size in chunks():
                rows = slice(start, start + size)
                here = field[z, rows, :]
                left = jnp.where(lane48 == 0, roll(field[16, rows, :], 121 - 8 * z, 1), roll(here, 1, 1))
                inward = across_y[z, rows, :] * (here - left)
                outward = jnp.where(lane48 == 127, roll(flux[rows, :], 127 - 8 * z, 1), roll(inward, -1, 1))
                value = inward - outward
                value = value + across_x[z, rows, :] * (here - field[z, start - 1 : start - 1 + size, :])
                value = value - across_x[z, start + 1 : start + 1 + size, :] * (
                    field[z, start + 1 : start + 1 + size, :] - here
                )
                value = value + across_z[z, rows, :] * (here - field[jnp.maximum(z - 1, 0), rows, :])
                below = jnp.where(z < 15, across_z[jnp.minimum(z + 1, 15), rows, :], 0.0)
                value = value - below * (field[jnp.minimum(z + 1, 15), rows, :] - here)
                image[z, rows, :] = value
            return carry

        lax.fori_loop(0, 16, layer, 0)

    flux = edge_flux = field3.at[16]
    apply(field0, field1, edge_flux)
    apply(field1, field2, edge_flux)

    def last(z, carry):
        return carry

    apply(field2, field3, resist.at[16])

    def gather(z, sums):
        f0 = field0[z, 16:144, :]
        f1 = field1[z, 16:144, :]
        f2 = field2[z, 16:144, :]
        f3 = field3[z, 16:144, :]
        power1[z] = f1
        power2[z] = f2
        power3[z] = f3
        terms = (f0 * f0, f0 * f1, f1 * f1, f1 * f2, f2 * f2, f2 * f3)
        return tuple(s + jnp.sum(t.reshape(16, 8, N), axis=0) for s, t in zip(sums, terms))

    sums = lax.fori_loop(0, 16, gather, tuple(jnp.zeros((8, N), F32) for _ in range(6)))
    line = jnp.where((lane[:1] >= 8) & (lane[:1] < 16), top, 0.0)
    for k, s in enumerate(sums):
        amount = jnp.sum(jnp.sum(s, axis=0, keepdims=True), axis=1, keepdims=True)
        line = jnp.where(lane[:1] == k, amount, line)
    table[...] = jnp.broadcast_to(line, table.shape)


def combine(everyone, own, source, power1, power2, power3, pressure, residual):
    n = everyone.shape[0]
    rows = everyone[...]
    lane = iota((n, N), 1)
    tops = jnp.where(lane < 8, roll(rows, -8, 1), 0.0)
    top = jnp.max(tops, axis=0, keepdims=True)
    top = jnp.max(jnp.where(lane[:1] == 0, top, -HUGE), axis=1, keepdims=True)
    factor = jnp.exp((tops - top) * lane.astype(F32))
    moments = jnp.sum(jnp.where(lane < 6, rows * factor, 0.0), axis=0, keepdims=True)
    u0, u1, u2, u3, u4, u5 = [
        jnp.sum(jnp.where(lane[:1] == k, moments, 0.0), axis=1, keepdims=True) for k in range(6)
    ]
    own_top = jnp.sum(jnp.where(lane[:1] == 8, own[0:1, :], 0.0), axis=1, keepdims=True)
    ratio = jnp.exp(own_top - top)

    def over(a, b):
        return jnp.where(b > 0.0, a / jnp.where(b > 0.0, b, 1.0), 0.0)

    l10 = over(u1, u0)
    l20 = over(u2, u0)
    d1 = u2 - l10 * u1
    s12 = u3 - l10 * u2
    l21 = over(s12, d1)
    d2 = (u4 - l20 * u2) - l21 * s12
    y1 = u4 - l10 * u3
    y2 = u5 - l20 * u3 - l21 * y1
    e2 = -over(y2, d2)
    e1 = -over(y1, d1) - l21 * e2
    e0 = -over(u3, u0) - l10 * e1 - l20 * e2

    sigma = jnp.exp(top)
    tau = jnp.minimum(1.0, 2.0 * sigma)
    kappa = jnp.minimum(1.0, 0.5 / sigma)
    at_zero = ((e0 * tau - e1 * kappa) * tau + e2 * kappa * kappa) * tau - kappa * kappa * kappa
    r_scale = tau * tau * tau / at_zero
    p_scale = -jnp.minimum(1.0 / sigma, 2.0) / at_zero
    q1 = tau * e2 - kappa
    r0 = r_scale * e0
    r1 = r_scale * e1 * ratio
    r2 = r_scale * e2 * ratio * ratio
    r3 = r_scale * ratio * ratio * ratio
    p0 = p_scale * (tau * tau * e1 - kappa * q1)
    p1 = p_scale * (tau * q1) * ratio
    p2 = p_scale * (tau * tau) * ratio * ratio
    for z in range(source.shape[0]):
        f0 = source[z]
        f1 = power1[z]
        f2 = power2[z]
        pressure[z] = p0 * f0 + p1 * f1 + p2 * f2
        residual[z] = (r0 * f0 + r1 * f1) + (r2 * f2 + r3 * power3[z])


def vmem(count):
    return [pl.BlockSpec(memory_space=pltpu.VMEM)] * count


def shape(*dims):
    return jax.ShapeDtypeStruct(dims, F32)


def call(body, out, scratch=(), inputs=0, name=None):
    return pl.pallas_call(
        body,
        out_shape=out,
        in_specs=vmem(inputs),
        out_specs=vmem(len(out)),
        scratch_shapes=list(scratch),
        compiler_params=pltpu.CompilerParams(vmem_limit_bytes=40 * 1024 * 1024),
        name=name,
    )


def exchange(to_next, to_previous, axis):
    count = lax.axis_size(axis)
    forward = [(i, (i + 1) % count) for i in range(count)]
    backward = [(target, source) for source, target in forward]
    return lax.ppermute(to_next, axis, forward), lax.ppermute(to_previous, axis, backward)


def local(noise, biofilm, source):
    to_right, to_left = call(pack_columns, [shape(MSG_Y, N)] * 2, inputs=3, name="pack")(noise, source, biofilm)
    from_left, from_right = exchange(to_right, to_left, "gy")
    middle, edge, edge_source, edge_biofilm, to_down, to_up = call(
        smooth_columns,
        [shape(NZ, N, N), shape(N, N), shape(N, N), shape(N, N), shape(MSG_X, N), shape(MSG_X, N)],
        inputs=5,
        name="columns",
    )(noise, source, biofilm, from_left, from_right)
    from_up, from_down = exchange(to_down, to_up, "gx")
    devices = lax.axis_size("gx") * lax.axis_size("gy")
    planes = [pltpu.VMEM((17, ROWS, N), F32)]
    power1, power2, power3, table = call(
        operate_powers,
        [shape(NZ, N, N)] * 3 + [shape(devices, N)],
        scratch=planes * 4 + [pltpu.VMEM((ROWS, N), F32)] + planes * 4,
        inputs=8,
        name="powers",
    )(middle, edge, edge_source, edge_biofilm, source, biofilm, from_up, from_down)
    everyone = lax.all_to_all(table, ("gx", "gy"), 0, 0, tiled=True)

    layers = 4
    block = pl.BlockSpec((layers, N, N), lambda i: (i, 0, 0))
    whole = pl.BlockSpec((devices, N), lambda i: (0, 0))
    first = pl.BlockSpec((8, N), lambda i: (0, 0))
    return tuple(
        pl.pallas_call(
            combine,
            grid=(NZ // layers,),
            out_shape=[shape(NZ, N, N)] * 2,
            in_specs=[whole, first] + [block] * 4,
            out_specs=[block] * 2,
            name="combine",
        )(everyone, table, source, power1, power2, power3)
    )


def solution(mesh):
    in_specs = (P(None, "gx", "gy"), P(None, "gx", "gy"), P(None, "gx", "gy"))
    out_specs = (P(None, "gx", "gy"), P(None, "gx", "gy"))
    return jax.shard_map(local, mesh=mesh, in_specs=in_specs, out_specs=out_specs, check_vma=False)
```

time: 569 us -> 102 us (0.18); the launches traced: 562 us -> 102 us
  blocking collectives: 381 us -> 23.3 us
  local copies, waits for them, and re-layouts: 47.6 us -> 6.61 us
  other arithmetic: 38.6 us -> 0 us
  Pallas kernels: 0 us -> 30.6 us
  starting transfers between devices: 40.4 us -> 11.2 us
  waiting for transfers between devices: 38.4 us -> 29.3 us
  matrix products: 7.63 us -> 0 us
  between operations: 7.97 us -> 0.68 us
    psum x5 -> x0, blocking collectives: 381 us -> none  [the longest x3 227 us: squares(): return lax.psum(jnp.sum(residual * residual), ('gx', 'gy'))]
    pallas_call x0 -> x4, Pallas kernels: none -> 30.6 us  [the longest x1 20.8 us: local(): call(operate_powers, [shape(NZ, N, N)] * 3 + [shape(devices, N)], scratch...]
    slice x20 -> x0, local copies, waits for them, and re-layouts: 30.5 us -> none  [the longest x9 17.1 us: padded_2(): lax.slice_in_dim(block, 0, width, axis=dim)]
    ppermute x20 -> x4, starting transfers between devices: 40.4 us -> 11.2 us  [the longest x2 6.19 us: exchange(): lax.ppermute(to_next, axis, forward)]
    all_to_all x0 -> x1, blocking collectives: none -> 23.3 us  [local(): everyone = lax.all_to_all(table, ('gx', 'gy'), 0, 0, tiled=True)]
    mul x9 -> x0, other arithmetic: 20.3 us -> none  [the longest x3 11 us: operate(): flux_y = trans_y * (padded[:, 1:-1, 1:] - padded[:, 1:-1, :-1])]
    ppermute x10 -> x0, local copies, waits for them, and re-layouts: 16.9 us -> none  [the longest x5 8.9 us: padded_2(): lax.ppermute(lax.slice_in_dim(block, block.shape[dim] - width, None, axis...]
    reduce_sum x5 -> x0, other arithmetic: 11.9 us -> none  [the longest x3 6.3 us: local(): alpha = norm_now / lax.psum(jnp.sum(direction * image), ('gx', 'gy'))]
  transfers between devices with their start and end apart: 20 -> 4, of which waited for: 8 -> 3; matrix products, arithmetic and copies ran while one was open for 6% -> 0% of each run, Pallas kernels for 0% -> 0%
where the time goes in v1:
time: 102 us
  Pallas kernels  30.6 us (30%)
  waiting for transfers between devices  29.3 us (29%)
  blocking collectives  23.3 us (23%)
  starting transfers between devices  11.2 us (11%)
  local copies, waits for them, and re-layouts  6.61 us (6%)
    ppermute x2, waiting for transfers between devices, exchange(): lax.ppermute(to_next, axis, forward)  24 us
    all_to_all x1, blocking collectives, local(): everyone = lax.all_to_all(table, ('gx', 'gy'), 0, 0, tiled=True)  23.3 us
    pallas_call x1, Pallas kernels, local(): call(operate_powers, [shape(NZ, N, N)] * 3 + [shape(devices, N)], scratch...  20.8 us
    unnamed x18, local copies, waits for them, and re-layouts  6.61 us
    ppermute x2, starting transfers between devices, exchange(): lax.ppermute(to_next, axis, forward)  6.19 us
    ppermute x2, waiting for transfers between devices, exchange(): lax.ppermute(to_previous, axis, backward)  5.24 us
    pallas_call x1, Pallas kernels, local(): pl.pallas_call(combine, grid=(NZ // layers,), out_shape=[shape(NZ, N, N)]...  4.98 us
    ppermute x2, starting transfers between devices, exchange(): lax.ppermute(to_previous, axis, backward)  4.98 us
  transfers between devices with their start and end apart: 4, of which 3 were waited for; matrix products, arithmetic and copies ran while one was open for 0% of the time, Pallas kernels for 0%

profile of v1, /device:TPU:1, one launch (start us, length us, event | category | flops | bytes accessed | tf_op | source)
XLA Modules:
  0.0 101.6 jit_solution(18246993949810834032)
XLA Ops:
  0.6 0.0 copy-start
  0.6 1.2 %copy-done = f32[16,128,128]{2,1,0:T(8,128)S(1)} copy-done((f32[16,128,128]{2,1,0:T(8,128)S(1)}, f32[16,128,128]{2,1,0:T(8,128)}, u32[]{:S(2)}) %copy-start) | copy-done | bytes 1048600
  1.9 0.0 copy-start.2
  1.9 1.2 %copy-done.2 = s32[16,128,128]{2,1,0:T(8,128)S(1)} copy-done((s32[16,128,128]{2,1,0:T(8,128)S(1)}, s32[16,128,128]{2,1,0:T(8,128)}, u32[]{:S(2)}) %copy-start.2) | copy-done | bytes 1048600
  3.1 0.0 copy-start.4
  3.1 1.2 %copy-done.4 = f32[16,128,128]{2,1,0:T(8,128)S(1)} copy-done((f32[16,128,128]{2,1,0:T(8,128)S(1)}, f32[16,128,128]{2,1,0:T(8,128)}, u32[]{:S(2)}) %copy-start.4) | copy-done | bytes 1048600
  4.3 2.4 %pack.1 = (f32[1168,128]{1,0:T(8,128)S(1)}, f32[1168,128]{1,0:T(8,128)S(1)}) custom-call(f32[16,128,128]{2,1,0:T(8,128)S(1)} %copy-done.4, f32[16,128,128]{2,1,0:T(8,128)S(1)} %copy-done, s32[16,128,128]{2,1,0:T(8,128)S(1)} %copy-done.2), custom_call_target="tpu_custom_call" | custom-call | tf_op jit(solution)/shard_map/pack/pallas_call | solution.py:455
  6.8 2.5 %collective-permute-start = (f32[1168,128]{1,0:T(8,128)S(1)}, f32[1168,128]{1,0:T(8,128)S(1)}, u32[]{:S(2)}, u32[]{:S(2)}) collective-permute-start(f32[1168,128]{1,0:T(8,128)S(1)} %get-tuple-element.14), channel_id=1, source_target_pairs={{0,1},{1,2},{2,3},{3,4},{4,5},{5,6},{6,7},{7,8},{8,9},{9,10},{10,1... | collective-permute-start | bytes 1794056 | tf_op jit(solution)/shard_map/ppermute | solution.py:451
  9.3 0.0 copy-start.1
  9.3 0.0 copy-start.3
  9.3 5.0 %collective-permute-start.1 = (f32[1168,128]{1,0:T(8,128)S(1)}, f32[1168,128]{1,0:T(8,128)S(1)}, u32[]{:S(2)}, u32[]{:S(2)}) collective-permute-start(f32[1168,128]{1,0:T(8,128)S(1)} %get-tuple-element.15), channel_id=1, source_target_pairs={{1,0},{2,1},{3,2},{4,3},{5,4},{6,5},{7,6},{8,7},{9,8},{10,9},{11,1... | collective-permute-start | bytes 1794056 | tf_op jit(solution)/shard_map/ppermute | solution.py:451
  14.3 13.1 %collective-permute-done.from_left = f32[1168,128]{1,0:T(8,128)S(1)} collective-permute-done((f32[1168,128]{1,0:T(8,128)S(1)}, f32[1168,128]{1,0:T(8,128)S(1)}, u32[]{:S(2)}, u32[]{:S(2)}) %collective-permute-start) | collective-permute-done | bytes 598048 | tf_op jit(solution)/shard_map/ppermute | solution.py:451
  27.4 0.0 collective-permute-done.1.from_right
  27.4 2.4 %columns.1 = (f32[16,128,128]{2,1,0:T(8,128)S(1)}, f32[128,128]{1,0:T(8,128)S(1)}, f32[128,128]{1,0:T(8,128)S(1)}, f32[128,128]{1,0:T(8,128)S(1)}, f32[1248,128]{1,0:T(8,128)S(1)}, /*index=5*/f32[1248,128]{1,0:T(8,128)S(1)}) custom-call(f32[16,128,128]{2,1,0:T(8,128)S(1)} %copy-done.4, f32[16,128,128]{2,1,0:T(8,128)S(1)} %copy-done, ...), custom_call_target="tpu_custom_call" | custom-call | tf_op jit(solution)/shard_map/columns/pallas_call | solution.py:457
  29.8 3.6 %collective-permute-start.2 = (f32[1248,128]{1,0:T(8,128)S(1)}, f32[1248,128]{1,0:T(8,128)S(1)}, u32[]{:S(2)}, u32[]{:S(2)}) collective-permute-start(f32[1248,128]{1,0:T(8,128)S(1)} %get-tuple-element.20), channel_id=1, source_target_pairs={{0,16},{16,32},{32,48},{48,64},{64,80},{80,96},{96,112},{112,128},... | collective-permute-start | bytes 1916936 | tf_op jit(solution)/shard_map/ppermute | solution.py:451
  33.4 0.0 collective-permute-start.3
  33.4 10.9 %collective-permute-done.2.from_up = f32[1248,128]{1,0:T(8,128)S(1)} collective-permute-done((f32[1248,128]{1,0:T(8,128)S(1)}, f32[1248,128]{1,0:T(8,128)S(1)}, u32[]{:S(2)}, u32[]{:S(2)}) %collective-permute-start.2) | collective-permute-done | bytes 639008 | tf_op jit(solution)/shard_map/ppermute | solution.py:451
  44.4 5.2 %collective-permute-done.3.from_down = f32[1248,128]{1,0:T(8,128)S(1)} collective-permute-done((f32[1248,128]{1,0:T(8,128)S(1)}, f32[1248,128]{1,0:T(8,128)S(1)}, u32[]{:S(2)}, u32[]{:S(2)}) %collective-permute-start.3) | collective-permute-done | bytes 639008 | tf_op jit(solution)/shard_map/ppermute | solution.py:451
  49.6 0.0 copy-done.1
  49.6 0.0 copy-done.3
  49.6 20.8 %powers.1 = (f32[16,128,128]{2,1,0:T(8,128)S(1)}, f32[16,128,128]{2,1,0:T(8,128)S(1)}, f32[16,128,128]{2,1,0:T(8,128)S(1)}, f32[256,128]{1,0:T(8,128)S(1)}) custom-call(f32[16,128,128]{2,1,0:T(8,128)S(1)} %get-tuple-element.16.middle, f32[128,128]{1,0:T(8,128)S(1)} %get-tuple-element.17.edge, f32[128,128]{1,0:T(8,128)S(1)} %get-tuple-element.18.edge_source, ...), custom_call_target="tpu_custom_call" | custom-call | tf_op jit(solution)/shard_map/powers/pallas_call | solution.py:466
  70.4 0.0 copy-start.5
  70.5 1.0 copy-done.5
  71.4 0.0 copy-start.6
  71.4 1.0 copy-done.6
  72.4 0.0 copy-start.7
  72.4 1.0 copy-done.7
  73.4 0.0 copy-start.8
  73.4 23.3 %all_to_all.11 = f32[256,1,128]{2,1,0:T(1,128)} all-to-all(f32[256,1,128]{2,1,0:T(1,128)S(1)} %bitcast.4), channel_id=1, replica_groups=mesh['gx'=16,'gy'=16] {'gx','gy'}, dimensions={0} | all-to-all | bytes 262144 | tf_op jit(solution)/shard_map/all_to_all | solution.py:473
  96.7 0.0 copy-done.8
  96.7 5.0 %combine.1 = (f32[16,128,128]{2,1,0:T(8,128)}, f32[16,128,128]{2,1,0:T(8,128)}) custom-call(f32[256,128]{1,0:T(8,128)} %bitcast.5, f32[256,128]{1,0:T(8,128)} %copy-done.8, f32[16,128,128]{2,1,0:T(8,128)} %source.7, f32[16,128,128]{2,1,0:T(8,128)} %copy-done.5, f32[16,128,128]{2,1,0:T(8,128)} %copy-done.6, f32[16,128,128]{2,1,0:T(8,128)} %copy-done.7), custom_call_target="tpu_custom_call" | custom-call | tf_op jit(solution)/shard_map/combine/pallas_call | solution.py:480
Async XLA Ops:
  0.6 1.2 %copy-start = (f32[16,128,128]{2,1,0:T(8,128)S(1)}, f32[16,128,128]{2,1,0:T(8,128)}, u32[]{:S(2)}) copy-start(f32[16,128,128]{2,1,0:T(8,128)} %source.7) | copy-start | bytes 3145732
  1.9 1.2 %copy-start.2 = (s32[16,128,128]{2,1,0:T(8,128)S(1)}, s32[16,128,128]{2,1,0:T(8,128)}, u32[]{:S(2)}) copy-start(s32[16,128,128]{2,1,0:T(8,128)} %biofilm.5) | copy-start | bytes 3145732
  3.1 1.2 %copy-start.4 = (f32[16,128,128]{2,1,0:T(8,128)S(1)}, f32[16,128,128]{2,1,0:T(8,128)}, u32[]{:S(2)}) copy-start(f32[16,128,128]{2,1,0:T(8,128)} %noise.3) | copy-start | bytes 3145732
  6.8 20.6 %collective-permute-start = (f32[1168,128]{1,0:T(8,128)S(1)}, f32[1168,128]{1,0:T(8,128)S(1)}, u32[]{:S(2)}, u32[]{:S(2)}) collective-permute-start(f32[1168,128]{1,0:T(8,128)S(1)} %get-tuple-element.14), channel_id=1, source_target_pairs={{0,1},{1,2},{2,3},{3,4},{4,5},{5,6},{6,7},{7,8},{8,9},{9,10},{10,1... | collective-permute-start | bytes 1794056 | tf_op jit(solution)/shard_map/ppermute | solution.py:451
  9.3 40.3 %copy-start.1 = (f32[16,128,128]{2,1,0:T(8,128)S(1)}, f32[16,128,128]{2,1,0:T(8,128)}, u32[]{:S(2)}) copy-start(f32[16,128,128]{2,1,0:T(8,128)} %source.7) | copy-start | bytes 3145732
  9.3 40.3 %copy-start.3 = (s32[16,128,128]{2,1,0:T(8,128)S(1)}, s32[16,128,128]{2,1,0:T(8,128)}, u32[]{:S(2)}) copy-start(s32[16,128,128]{2,1,0:T(8,128)} %biofilm.5) | copy-start | bytes 3145732
  9.3 18.1 %collective-permute-start.1 = (f32[1168,128]{1,0:T(8,128)S(1)}, f32[1168,128]{1,0:T(8,128)S(1)}, u32[]{:S(2)}, u32[]{:S(2)}) collective-permute-start(f32[1168,128]{1,0:T(8,128)S(1)} %get-tuple-element.15), channel_id=1, source_target_pairs={{1,0},{2,1},{3,2},{4,3},{5,4},{6,5},{7,6},{8,7},{9,8},{10,9},{11,1... | collective-permute-start | bytes 1794056 | tf_op jit(solution)/shard_map/ppermute | solution.py:451
  29.8 14.6 %collective-permute-start.2 = (f32[1248,128]{1,0:T(8,128)S(1)}, f32[1248,128]{1,0:T(8,128)S(1)}, u32[]{:S(2)}, u32[]{:S(2)}) collective-permute-start(f32[1248,128]{1,0:T(8,128)S(1)} %get-tuple-element.20), channel_id=1, source_target_pairs={{0,16},{16,32},{32,48},{48,64},{64,80},{80,96},{96,112},{112,128},... | collective-permute-start | bytes 1916936 | tf_op jit(solution)/shard_map/ppermute | solution.py:451
  33.4 16.2 %collective-permute-start.3 = (f32[1248,128]{1,0:T(8,128)S(1)}, f32[1248,128]{1,0:T(8,128)S(1)}, u32[]{:S(2)}, u32[]{:S(2)}) collective-permute-start(f32[1248,128]{1,0:T(8,128)S(1)} %get-tuple-element.21), channel_id=1, source_target_pairs={{16,0},{32,16},{48,32},{64,48},{80,64},{96,80},{112,96},{128,112},... | collective-permute-start | bytes 1916936 | tf_op jit(solution)/shard_map/ppermute | solution.py:451
  70.4 1.0 copy-start.5
  71.4 1.0 copy-start.6
  72.4 1.0 copy-start.7
  73.4 23.3 %copy-start.8 = (f32[256,128]{1,0:T(8,128)}, f32[256,128]{1,0:T(8,128)S(1)}, u32[]{:S(2)}) copy-start(f32[256,128]{1,0:T(8,128)S(1)} %get-tuple-element.22.own) | copy-start | bytes 393220

commit v2 on v1

v2 whole, which is shorter than its diff:
```python
import jax
import jax.numpy as jnp
from jax import lax
from jax.experimental import pallas as pl
from jax.experimental.pallas import tpu as pltpu
from jax.sharding import PartitionSpec as P

R = 64
WIDTH = 2 * R + 1
NZ = 16
N = 128
F32 = jnp.float32
BF16 = jnp.bfloat16

MSG_Y = 8 * N + N + 16
MSG_X = 17 * 72 + 24
ROWS = 160
OWN = 16
HUGE = 1e30
U1, U2, U3, U4, U5, U6 = 16, 4, 2, 4, 4, 2


def iota(shape, dim):
    return lax.broadcasted_iota(jnp.int32, shape, dim)


def roll(x, shift, axis):
    if isinstance(shift, int):
        shift = shift % x.shape[axis]
        if shift == 0:
            return x
    return pltpu.roll(x, shift, axis)


def split3(x):
    high = x.astype(BF16)
    rest = x - high.astype(F32)
    middle = rest.astype(BF16)
    low = (rest - middle.astype(F32)).astype(BF16)
    return high, middle, low


def split2(x):
    high = x.astype(BF16)
    return high, (x - high.astype(F32)).astype(BF16)


def dot(a, b):
    return lax.dot_general(a, b, (((1,), (0,)), ((), ())), preferred_element_type=F32)


def weights(mask):
    return jnp.where(mask, 1.0, 0.0).astype(BF16)


def pack_columns(noise_in, source_in, biofilm_in, to_right, to_left, noise, source, biofilm, arrived):
    def arrivals(g):
        rows = slice(16 * g, 16 * g + 16)
        return [
            pltpu.make_async_copy(far.at[:, rows, :], near.at[:, rows, :], arrived.at[k, g])
            for k, (far, near) in enumerate(((noise_in, noise), (source_in, source), (biofilm_in, biofilm)))
        ]

    for g in range(8):
        for copy in arrivals(g):
            copy.start()

    lane = iota((16, N), 1)
    slot = lane % 8
    group = lane // 8
    low = lane < 64

    third_right = jnp.zeros((16, N), F32)
    third_left = jnp.zeros((16, N), F32)
    for g in range(8):
        for copy in arrivals(g):
            copy.wait()
        rows = slice(16 * g, 16 * g + 16)
        zero = jnp.zeros((16, N), F32)
        nr, sr, nl, sl = zero, zero, zero, zero
        br = jnp.zeros((16, N), jnp.int32)
        bl = br
        for q in range(8):
            even = noise[2 * q, rows, :]
            odd = noise[2 * q + 1, rows, :]
            to_right[q * N + 16 * g : q * N + 16 * g + 16, :] = jnp.where(low, roll(even, 64, 1), odd)
            to_left[q * N + 16 * g : q * N + 16 * g + 16, :] = jnp.where(low, even, roll(odd, 64, 1))
            for z, n in ((2 * q, even), (2 * q + 1, odd)):
                here = group == z
                s = source[z, rows, :]
                b = biofilm[z, rows, :]
                nr = jnp.where(here, roll(n, 8 * z - 61, 1), nr)
                nl = jnp.where(here, roll(n, 8 * z + 5 - 64, 1), nl)
                sr = jnp.where(here, roll(s, 8 * z + 8, 1), sr)
                sl = jnp.where(here, roll(s, 8 * z, 1), sl)
                br = jnp.where(here, roll(b, 8 * z + 8, 1), br)
                bl = jnp.where(here, roll(b, 8 * z, 1), bl)
        br = br.astype(F32)
        bl = bl.astype(F32)
        to_right[8 * N + 16 * g : 8 * N + 16 * g + 16, :] = jnp.where(
            slot < 3, nr, jnp.where(slot < 5, roll(br, -3, 1), sr)
        )
        to_left[8 * N + 16 * g : 8 * N + 16 * g + 16, :] = jnp.where(
            slot < 3, sl, jnp.where(slot < 5, roll(bl, 3, 1), nl)
        )
        third_right = third_right + roll(jnp.where(slot == 5, br, 0.0), g, 1)
        third_left = third_left + roll(jnp.where(slot == 2, bl, 0.0), g, 1)
    to_right[9 * N :, :] = third_right
    to_left[9 * N :, :] = third_left


def column_weights():
    m = iota((N, 2 * N), 0)
    o = iota((N, 2 * N), 1)
    s = o - N
    own = ((o < N) & (m - o <= R) & (o - m <= R)) | ((o >= N) & (s <= 2) & (m >= s + 64)) | (
        (s >= 5) & (s <= 7) & (m <= s + 56)
    )
    lane = iota((N, 3 * N), 0)
    o = iota((N, 3 * N), 1)
    half = lane // 64
    m = lane % 64
    e = o - 2 * N
    same = (o < 2 * N) & (o // N == half)
    edge = (e >= 0) & (e < 16) & (e // 8 == half)
    left = (same & (m >= o % N)) | (edge & (o % 8 >= 5))
    right = (same & (m + 64 <= o % N)) | (edge & (o % 8 <= 2))
    a = iota((N, N), 0)
    b = iota((N, N), 1)
    together = a // 8 == b // 8
    t = a % 8
    s = b % 8
    left_extra = together & (t <= 2) & (s >= 5) & (t >= s - 5)
    right_extra = together & (t >= 5) & (s <= 2) & (t - 5 <= s)
    return [weights(w) for w in (own, left, right, left_extra, right_extra)]


def column_sums_own(noise, biofilm, own_middle, own_edge, factor):
    own = column_weights()[0]
    twice = jnp.concatenate([own, own], axis=0)
    total = jnp.zeros((N, N), F32)
    for z in range(16):
        out = dot(jnp.concatenate(split2(noise[z]), axis=1), twice)
        own_middle[z] = out[:, :N]
        total = total + roll(out[:, N:], 8 * z, 1)
        factor[z] = resistance_factor(biofilm[z].astype(F32))
    own_edge[...] = total


def smooth_columns(
    own_middle, own_edge, source, biofilm, from_left, from_right,
    middle, edge, edge_source, edge_biofilm, to_down, to_up,
):
    _, left, right, left_extra, right_extra = column_weights()
    both = jnp.concatenate([left, right], axis=0)
    both_extra = jnp.concatenate([left_extra, right_extra], axis=0)
    slot = iota((N, N), 1) % 8

    def times(x, y, w):
        high, low = split2(jnp.concatenate([x, y], axis=1))
        return dot(high, w) + dot(low, w)

    extra_left = from_left[8 * N : 9 * N, :]
    extra_right = from_right[8 * N : 9 * N, :]
    total = own_edge[...] + times(extra_left, extra_right, both_extra)
    for q in range(8):
        halo = times(from_left[q * N : q * N + N, :], from_right[q * N : q * N + N, :], both)
        total = total + roll(halo[:, 2 * N :], 16 * q, 1)
        for z in (2 * q, 2 * q + 1):
            field = own_middle[z] + halo[:, (z % 2) * N : (z % 2) * N + N]
            middle[z] = field
            to_down[z * 72 : z * 72 + 72, :] = field[56:, :]
            to_up[z * 72 : z * 72 + 72, :] = field[:72, :]
    edge[...] = total
    to_down[16 * 72 : 17 * 72, :] = total[56:, :]
    to_up[16 * 72 : 17 * 72, :] = total[:72, :]

    edge_source[...] = jnp.where(slot >= 5, extra_left, jnp.where(slot <= 2, extra_right, 0.0))
    third_left = from_left[9 * N :, :]
    third_right = from_right[9 * N :, :]
    levels = jnp.where(slot >= 6, roll(extra_left, 3, 1), jnp.where(slot <= 1, roll(extra_right, -3, 1), 0.0))
    slot16 = iota((16, N), 1) % 8
    for g in range(8):
        rows = slice(16 * g, 16 * g + 16)
        edge_biofilm[rows, :] = jnp.where(
            slot16 == 5, roll(third_left, -g, 1), jnp.where(slot16 == 2, roll(third_right, -g, 1), levels[rows, :])
        )

    to_down[17 * 72 :, :] = jnp.zeros((24, N), F32)
    to_up[17 * 72 :, :] = jnp.zeros((24, N), F32)
    for z in range(17):
        s = source.at[z] if z < 16 else edge_source
        b = biofilm.at[z] if z < 16 else edge_biofilm
        to_down[z * 72 : z * 72 + 3, :] = s[125:128, :]
        to_down[z * 72 + 3 : z * 72 + 5, :] = b[126:128, :].astype(F32)
        to_down[17 * 72 + z : 17 * 72 + z + 1, :] = b[125:126, :].astype(F32)
        to_up[z * 72 + 67 : z * 72 + 70, :] = s[0:3, :]
        to_up[z * 72 + 70 : z * 72 + 72, :] = b[0:2, :].astype(F32)
        to_up[17 * 72 + z : 17 * 72 + z + 1, :] = b[2:3, :].astype(F32)


def row_weights():
    r = iota((144, N), 0) - 8
    m = iota((144, N), 1)
    inside = (r >= -3) & (r <= 130)
    own = inside & (m >= r - R) & (m <= r + R)
    halo = inside & (((m < 64) & (m >= r)) | ((m >= 64) & (m <= r)))
    return weights(own), weights(halo)


def row_sums(band, *planes):
    columns = [jnp.concatenate(split2(p), axis=0) for p in planes]
    out = dot(jnp.concatenate([band, band], axis=1), jnp.concatenate(columns, axis=1))
    return [out[:, k * N : k * N + N] for k in range(len(planes))]


def row_sums_own(middle, edge, edge_biofilm, partial, factor):
    own, _ = row_weights()
    for z in range(0, 16, 2):
        partial[z], partial[z + 1] = row_sums(own, middle[z], middle[z + 1])
    partial[16] = row_sums(own, edge[...])[0]
    factor[...] = resistance_factor(edge_biofilm[...])


def resistance_factor(biofilm):
    open_part = 1.0 - 0.06 * biofilm
    solid = (1.0 - 0.35 * open_part) * (1.0 / (1.0 - 0.35))
    return (0.5 * solid * solid) / (open_part * open_part * open_part)


def resistance(logperm, factor, top):
    return jnp.minimum(jnp.exp(top - logperm) * factor, HUGE)


def reciprocal(x):
    guess = pl.reciprocal(x, approx=True)
    return guess * (2.0 - x * guess)


WIDE = ((8, 48), (56, 48), (104, 48))
OWN_ROWS = ((16, 64), (80, 64))


def operate_powers(
    partial, factor, edge_factor, edge_source, source, from_up, from_down,
    power1, power2, power3, table,
    resist, across_x, across_y, across_z, flow, field0, field1, field2, field3, plane_resist, plane_field,
    side_resist, side_x, side_y, side_z, side0, side1, side2, side_flux, done,
):
    lane = iota((8, N), 1)
    row8 = iota((8, N), 0)

    _, halo = row_weights()
    edge_lane = (iota((144, N), 1) % 8 <= 2) | (iota((144, N), 1) % 8 >= 5)
    row144 = iota((144, N), 0)
    real_row = (row144 >= 5) & (row144 <= 138)

    def halo_rows(z):
        first = pl.multiple_of(z * 72, 8)
        return jnp.concatenate([from_up[pl.ds(first + 8, 64), :], from_down[pl.ds(first, 64), :]], axis=0)

    def finish(z, out, sums, real):
        first = pl.multiple_of(z * 72, 8)
        above = jnp.where(row8 >= 5, from_up[pl.ds(first, 8), :], 0.0)
        below = jnp.where(row8 <= 2, from_down[pl.ds(first + 64, 8), :], 0.0)
        above = jnp.where(row8 >= 5, above + roll(above, 7, 0) + roll(above, 6, 0), 0.0)
        below = jnp.where(row8 <= 2, below + roll(below, 1, 0) + roll(below, 2, 0), 0.0)
        total = sums + partial[z]
        total = jnp.concatenate([total[:8] + above, total[8:136], total[136:] + below], axis=0) * (1.0 / WIDTH)
        out[8:152, :] = total
        return jnp.max(jnp.where(real, total, -HUGE).reshape(18, 8, N), axis=0)

    def smooth(k, largest):
        first, second = row_sums(halo, halo_rows(2 * k), halo_rows(2 * k + 1))
        largest = jnp.maximum(largest, finish(2 * k, resist.at[2 * k], first, real_row))
        return jnp.maximum(largest, finish(2 * k + 1, resist.at[2 * k + 1], second, real_row))

    largest = finish(16, plane_resist, row_sums(halo, halo_rows(16))[0], real_row & edge_lane)
    largest = lax.fori_loop(0, 8, smooth, largest, unroll=U4)
    top = jnp.max(jnp.max(largest, axis=0, keepdims=True), axis=1, keepdims=True)
    top = jnp.maximum(top, -60.0)

    def halo_tiles(z):
        first = pl.multiple_of(z * 72, 8)
        above = from_up[pl.ds(first, 8), :]
        below = from_down[pl.ds(first + 64, 8), :]
        third_above = from_up[pl.ds(17 * 72 + z, 1), :]
        third_below = from_down[pl.ds(17 * 72 + z, 1), :]
        source_above = jnp.where(row8 >= 5, roll(above, 5, 0), 0.0)
        source_below = jnp.where(row8 <= 2, roll(below, 5, 0), 0.0)
        biofilm_above = jnp.where(row8 == 5, third_above, jnp.where(row8 >= 6, roll(above, 3, 0), 0.0))
        biofilm_below = jnp.where(row8 == 2, third_below, jnp.where(row8 <= 1, roll(below, 2, 0), 0.0))
        return source_above, source_below, biofilm_above, biofilm_below

    def prepare(z, out, field, own_source, own_factor):
        source_above, source_below, biofilm_above, biofilm_below = halo_tiles(z)
        field[8:16, :] = source_above
        field[16:144, :] = own_source
        field[144:152, :] = source_below
        out[8:16, :] = jnp.where(row8 >= 5, resistance(out[8:16, :], resistance_factor(biofilm_above), top), HUGE)
        out[144:152, :] = jnp.where(row8 <= 2, resistance(out[144:152, :], resistance_factor(biofilm_below), top), HUGE)
        out[16:144, :] = resistance(out[16:144, :], own_factor, top)
        empty = jnp.full((8, N), HUGE, F32)
        none = jnp.zeros((8, N), F32)
        out[0:8, :] = empty
        out[152:160, :] = empty
        field[0:8, :] = none
        field[152:160, :] = none

    def prepare_layer(z, carry):
        prepare(z, resist.at[z], field0.at[z], source[z], factor[z])
        none = jnp.zeros((8, N), F32)
        for ref in (field1, field2, across_x):
            ref[z, 0:8, :] = none
            ref[z, 152:160, :] = none
        return carry

    prepare(16, plane_resist, plane_field, edge_source[...], edge_factor[...])
    lax.fori_loop(0, 16, prepare_layer, 0, unroll=U6)

    a = iota((N, 2 * N), 0)
    o = iota((N, 2 * N), 1)
    t = o % 16
    spread = weights(
        (a // 8 == o // 16)
        & (((t >= 3) & (t <= 5) & (a % 8 == t - 3)) | ((t >= 10) & (t <= 12) & (a % 8 == t - 5)))
    )
    lane160 = iota((ROWS, N), 1)
    slot160 = lane160 % 16
    for plane, field, side, fill in ((plane_resist, resist, side_resist, HUGE), (plane_field, field0, side0, 0.0)):
        high, mid, low = split3(plane[...])
        outer = dot(high, spread) + dot(mid, spread) + dot(low, spread)
        for p in range(2):
            inner = jnp.zeros((ROWS, N), F32)
            for k in range(8):
                inner = jnp.where(lane160 // 16 == k, roll(field[8 * p + k], 16 * k + 3, 1), inner)
            value = jnp.where(slot160 <= 2, inner, jnp.where(slot160 >= 13, roll(inner, 10, 1), outer[:, p * N : p * N + N]))
            side[p] = jnp.where((slot160 <= 5) | (slot160 >= 10), value, fill)
    none = jnp.zeros((8, N), F32)
    for p in range(2):
        for ref in (side1, side2, side_x):
            ref[p, 0:8, :] = none
            ref[p, 152:160, :] = none

    def next_layer(first, second):
        lanes = iota(first.shape, 1)
        return jnp.where(lanes < 112, roll(first, -16, 1), roll(second, -16, 1)), roll(second, -16, 1)

    def last_layer(first, second):
        lanes = iota(first.shape, 1)
        return (
            jnp.where(lanes >= 16, roll(first, 16, 1), 0.0),
            jnp.where(lanes >= 16, roll(second, 16, 1), roll(first, 16, 1)),
        )

    for start, size in WIDE:
        rows = slice(start, start + size)
        here = [side_resist[p, rows, :] for p in range(2)]
        after = next_layer(*here)
        for p in range(2):
            side_x[p, rows, :] = reciprocal(here[p] + side_resist[p, start - 1 : start - 1 + size, :])
            side_y[p, rows, :] = reciprocal(here[p] + roll(here[p], 1, 1))
            value = reciprocal(here[p] + after[p])
            side_z[p, rows, :] = value if p == 0 else jnp.where(iota((size, N), 1) < 112, value, 0.0)

    def faces(z, carry):
        for start, size in WIDE:
            rows = slice(start, start + size)
            here = resist[z, rows, :]
            across_x[z, rows, :] = reciprocal(here + resist[z, start - 1 : start - 1 + size, :])
            across_y[z, rows, :] = jnp.where(iota((size, N), 1) == 0, 0.0, reciprocal(here + roll(here, 1, 1)))
            above = resist[jnp.maximum(z - 1, 0), rows, :]
            across_z[z, rows, :] = jnp.where(z > 0, reciprocal(here + above), 0.0)
        return carry

    lax.fori_loop(0, 16, faces, 0, unroll=U5)
    across_z[16] = jnp.zeros((ROWS, N), F32)

    def apply_sides(field, image):
        for start, size in WIDE:
            rows = slice(start, start + size)
            slot = iota((size, N), 1) % 16
            here = [field[p, rows, :] for p in range(2)]
            inward = [side_y[p, rows, :] * (here[p] - roll(here[p], 1, 1)) for p in range(2)]
            for p in range(2):
                side_flux[p, rows, :] = jnp.where(slot == 13, inward[p], -roll(inward[p], 9, 1))
            if image is None:
                continue
            after = next_layer(*here)
            through = [side_z[p, rows, :] * (after[p] - here[p]) for p in range(2)]
            back = last_layer(*through)
            for p in range(2):
                value = inward[p] - roll(inward[p], -1, 1) - through[p] + back[p]
                value = value + side_x[p, rows, :] * (here[p] - field[p, start - 1 : start - 1 + size, :])
                value = value - side_x[p, start + 1 : start + 1 + size, :] * (
                    field[p, start + 1 : start + 1 + size, :] - here[p]
                )
                image[p, rows, :] = value

    def flow_along_y(field):
        def layer(z, carry):
            for start, size in WIDE:
                rows = slice(start, start + size)
                here = field[z, rows, :]
                flow[z, rows, :] = across_y[z, rows, :] * (here - roll(here, 1, 1))
            return carry

        lax.fori_loop(0, 16, layer, 0, unroll=U1)

    def apply_rows(field, z, start, size):
        rows = slice(start, start + size)
        lanes = iota((size, N), 1)
        here = field[z, rows, :]
        inward = flow[z, rows, :]
        value = inward - roll(inward, -1, 1)
        beside = roll(side_flux[z // 8, rows, :], 115 - 16 * (z % 8), 1)
        value = value + jnp.where((lanes == 0) | (lanes == 127), beside, 0.0)
        value = value + across_x[z, rows, :] * (here - field[z, start - 1 : start - 1 + size, :])
        value = value - across_x[z, start + 1 : start + 1 + size, :] * (
            field[z, start + 1 : start + 1 + size, :] - here
        )
        value = value + across_z[z, rows, :] * (here - field[jnp.maximum(z - 1, 0), rows, :])
        return value - across_z[z + 1, rows, :] * (field[jnp.minimum(z + 1, 15), rows, :] - here)

    def apply(field, image):
        flow_along_y(field)

        def layer(z, carry):
            for start, size in WIDE:
                image[z, start : start + size, :] = apply_rows(field, z, start, size)
            return carry

        lax.fori_loop(0, 16, layer, 0, unroll=U2)

    def hand_out(field, power, k):
        return pltpu.make_async_copy(field.at[:, 16:144, :], power, done.at[k])

    apply_sides(side0, side1)
    apply(field0, field1)
    hand_out(field1, power1, 0).start()
    apply_sides(side1, side2)
    apply(field1, field2)
    hand_out(field2, power2, 1).start()
    apply_sides(side2, None)
    flow_along_y(field2)

    def last(z, sums):
        for start, size in OWN_ROWS:
            rows = slice(start, start + size)
            f3 = apply_rows(field2, z, start, size)
            field3[z, start - 16 : start - 16 + size, :] = f3
            f0 = field0[z, rows, :]
            f1 = field1[z, rows, :]
            f2 = field2[z, rows, :]
            terms = (f0 * f0, f0 * f1, f1 * f1, f1 * f2, f2 * f2, f2 * f3)
            sums = tuple(s + jnp.sum(t.reshape(size // 8, 8, N), axis=0) for s, t in zip(sums, terms))
        pltpu.make_async_copy(field3.at[z], power3.at[z], done.at[2]).start()
        return sums

    sums = lax.fori_loop(0, 16, last, tuple(jnp.zeros((8, N), F32) for _ in range(6)), unroll=U3)
    line = jnp.where((lane[:1] >= 8) & (lane[:1] < 16), top, 0.0)
    for k, s in enumerate(sums):
        amount = jnp.sum(jnp.sum(s, axis=0, keepdims=True), axis=1, keepdims=True)
        line = jnp.where(lane[:1] == k, amount, line)
    table[...] = jnp.broadcast_to(line, table.shape)
    hand_out(field1, power1, 0).wait()
    hand_out(field2, power2, 1).wait()
    pltpu.make_async_copy(field3, power3, done.at[2]).wait()


def coefficients(everyone, own):
    n = everyone.shape[0]
    rows = everyone[...]
    lane = iota((n, N), 1)
    tops = jnp.where(lane < 8, roll(rows, -8, 1), 0.0)
    top = jnp.max(tops, axis=0, keepdims=True)
    top = jnp.max(jnp.where(lane[:1] == 0, top, -HUGE), axis=1, keepdims=True)
    factor = jnp.exp((tops - top) * lane.astype(F32))
    moments = jnp.sum(jnp.where(lane < 6, rows * factor, 0.0), axis=0, keepdims=True)
    u0, u1, u2, u3, u4, u5 = [
        jnp.sum(jnp.where(lane[:1] == k, moments, 0.0), axis=1, keepdims=True) for k in range(6)
    ]
    own_top = jnp.sum(jnp.where(lane[:1] == 8, own[0:1, :], 0.0), axis=1, keepdims=True)
    ratio = jnp.exp(own_top - top)

    def over(a, b):
        return jnp.where(b > 0.0, a / jnp.where(b > 0.0, b, 1.0), 0.0)

    l10 = over(u1, u0)
    l20 = over(u2, u0)
    d1 = u2 - l10 * u1
    s12 = u3 - l10 * u2
    l21 = over(s12, d1)
    d2 = (u4 - l20 * u2) - l21 * s12
    y1 = u4 - l10 * u3
    y2 = u5 - l20 * u3 - l21 * y1
    e2 = -over(y2, d2)
    e1 = -over(y1, d1) - l21 * e2
    e0 = -over(u3, u0) - l10 * e1 - l20 * e2

    sigma = jnp.exp(top)
    tau = jnp.minimum(1.0, 2.0 * sigma)
    kappa = jnp.minimum(1.0, 0.5 / sigma)
    at_zero = ((e0 * tau - e1 * kappa) * tau + e2 * kappa * kappa) * tau - kappa * kappa * kappa
    r_scale = tau * tau * tau / at_zero
    p_scale = -jnp.minimum(1.0 / sigma, 2.0) / at_zero
    q1 = tau * e2 - kappa
    r0 = r_scale * e0
    r1 = r_scale * e1 * ratio
    r2 = r_scale * e2 * ratio * ratio
    r3 = r_scale * ratio * ratio * ratio
    p0 = p_scale * (tau * tau * e1 - kappa * q1)
    p1 = p_scale * (tau * q1) * ratio
    p2 = p_scale * (tau * tau) * ratio * ratio
    return p0, p1, p2, r0, r1, r2, r3


def combine(
    everyone, own, source_in, power1_in, power2_in, power3_in, pressure_out, residual_out,
    source, power1, power2, power3, pressure, residual, arrived, left,
):
    def arrivals(g):
        part = slice(4 * g, 4 * g + 4)
        pairs = ((source_in, source), (power1_in, power1), (power2_in, power2), (power3_in, power3))
        return [
            pltpu.make_async_copy(far.at[part], near.at[part], arrived.at[k, g]) for k, (far, near) in enumerate(pairs)
        ]

    def departures(g):
        part = slice(4 * g, 4 * g + 4)
        return [
            pltpu.make_async_copy(near.at[part], far.at[part], left.at[k, g])
            for k, (near, far) in enumerate(((pressure, pressure_out), (residual, residual_out)))
        ]

    for g in range(4):
        for copy in arrivals(g):
            copy.start()
    p0, p1, p2, r0, r1, r2, r3 = coefficients(everyone, own)
    for g in range(4):
        for copy in arrivals(g):
            copy.wait()
        for z in range(4 * g, 4 * g + 4):
            f0 = source[z]
            f1 = power1[z]
            f2 = power2[z]
            pressure[z] = p0 * f0 + p1 * f1 + p2 * f2
            residual[z] = (r0 * f0 + r1 * f1) + (r2 * f2 + r3 * power3[z])
        for copy in departures(g):
            copy.start()
    for g in range(4):
        for copy in departures(g):
            copy.wait()


def vmem(count):
    return [pl.BlockSpec(memory_space=pltpu.VMEM)] * count


def shape(*dims):
    return jax.ShapeDtypeStruct(dims, F32)


def hbm(count):
    return [pl.BlockSpec(memory_space=pltpu.HBM)] * count


def in_hbm(x):
    return pltpu.with_memory_space_constraint(x, pltpu.HBM)


def call(body, inputs, out, out_specs, scratch=(), name=None, cost=1e6):
    return pl.pallas_call(
        body,
        out_shape=out,
        in_specs=inputs,
        out_specs=out_specs,
        scratch_shapes=list(scratch),
        compiler_params=pltpu.CompilerParams(vmem_limit_bytes=40 * 1024 * 1024),
        cost_estimate=pl.CostEstimate(flops=int(cost), bytes_accessed=int(cost), transcendentals=0),
        name=name,
    )


def exchange(to_next, to_previous, axis):
    count = lax.axis_size(axis)
    forward = [(i, (i + 1) % count) for i in range(count)]
    backward = [(target, source) for source, target in forward]
    return lax.ppermute(to_next, axis, forward), lax.ppermute(to_previous, axis, backward)


def local(noise, biofilm, source):
    block = pltpu.VMEM((NZ, N, N), F32)
    to_right, to_left = call(
        pack_columns,
        hbm(3),
        [shape(MSG_Y, N)] * 2,
        vmem(2),
        [block, block, pltpu.VMEM((NZ, N, N), jnp.int32), pltpu.SemaphoreType.DMA((3, 8))],
        name="pack",
    )(in_hbm(noise), in_hbm(source), in_hbm(biofilm))
    from_left, from_right = exchange(to_right, to_left, "gy")
    own_middle, own_edge, factor = call(
        column_sums_own,
        vmem(2),
        [shape(NZ, N, N), shape(N, N), shape(NZ, N, N)],
        vmem(3),
        name="columns_own",
    )(noise, biofilm)
    middle, edge, edge_source, edge_biofilm, to_down, to_up = call(
        smooth_columns,
        vmem(6),
        [shape(NZ, N, N), shape(N, N), shape(N, N), shape(N, N), shape(MSG_X, N), shape(MSG_X, N)],
        vmem(6),
        name="columns",
    )(own_middle, own_edge, source, biofilm, from_left, from_right)
    from_up, from_down = exchange(to_down, to_up, "gx")
    partial, edge_factor = call(
        row_sums_own,
        vmem(3),
        [shape(NZ + 1, 144, N), shape(N, N)],
        vmem(2),
        name="rows_own",
    )(middle, edge, edge_biofilm)
    devices = lax.axis_size("gx") * lax.axis_size("gy")
    layers = pltpu.VMEM((NZ, ROWS, N), F32)
    plane = pltpu.VMEM((ROWS, N), F32)
    sides = pltpu.VMEM((2, ROWS, N), F32)
    power1, power2, power3, table = call(
        operate_powers,
        vmem(7),
        [pltpu.HBM((NZ, N, N), F32)] * 3 + [shape(devices, N)],
        hbm(3) + vmem(1),
        [layers] * 3
        + [pltpu.VMEM((NZ + 1, ROWS, N), F32)]
        + [layers] * 4
        + [block, plane, plane]
        + [sides] * 8
        + [pltpu.SemaphoreType.DMA((3,))],
        name="powers",
    )(partial, factor, edge_factor, edge_source, source, from_up, from_down)
    everyone = lax.all_to_all(table, ("gx", "gy"), 0, 0, tiled=True)
    return tuple(
        call(
            combine,
            vmem(2) + hbm(4),
            [pltpu.HBM((NZ, N, N), F32)] * 2,
            hbm(2),
            [block] * 6 + [pltpu.SemaphoreType.DMA((4, 4)), pltpu.SemaphoreType.DMA((2, 4))],
            name="combine",
        )(everyone, table, *[in_hbm(x) for x in (source, power1, power2, power3)])
    )


def solution(mesh):
    in_specs = (P(None, "gx", "gy"), P(None, "gx", "gy"), P(None, "gx", "gy"))
    out_specs = (P(None, "gx", "gy"), P(None, "gx", "gy"))
    return jax.shard_map(local, mesh=mesh, in_specs=in_specs, out_specs=out_specs, check_vma=False)
```

time: 102 us -> 81.5 us (0.80)
  Pallas kernels: 30.6 us -> 18.4 us
  local copies, waits for them, and re-layouts: 6.61 us -> 0.01 us
  waiting for transfers between devices: 29.3 us -> 28.1 us
    pallas_call x4 -> x6, Pallas kernels: 30.6 us -> 18.4 us  [the longest x1 9.08 us: local(): call(operate_powers, vmem(7), [pltpu.HBM((NZ, N, N), F32)] * 3 + [shape(d...]
    unnamed x18 -> x6, local copies, waits for them, and re-layouts: 6.61 us -> 0.01 us
    ppermute x2, waiting for transfers between devices: 24 us -> 22.8 us  [exchange(): lax.ppermute(to_next, axis, forward)]
  transfers between devices with their start and end apart: 4 -> 4, of which waited for: 3 -> 3; matrix products, arithmetic and copies ran while one was open for 0% -> 0% of each run, Pallas kernels for 0% -> 1%
where the time goes in v2:
time: 81.5 us; the launch traced here: 81.4 us
  waiting for transfers between devices  28.1 us (34%)
  blocking collectives  23 us (28%)
  Pallas kernels  18.4 us (23%)
  starting transfers between devices  11.1 us (14%)
    all_to_all x1, blocking collectives, local(): everyone = lax.all_to_all(table, ('gx', 'gy'), 0, 0, tiled=True)  23 us
    ppermute x2, waiting for transfers between devices, exchange(): lax.ppermute(to_next, axis, forward)  22.8 us
    pallas_call x1, Pallas kernels, local(): call(operate_powers, vmem(7), [pltpu.HBM((NZ, N, N), F32)] * 3 + [shape(d...  9.08 us
    ppermute x2, starting transfers between devices, exchange(): lax.ppermute(to_next, axis, forward)  6.19 us
    ppermute x2, waiting for transfers between devices, exchange(): lax.ppermute(to_previous, axis, backward)  5.25 us
    ppermute x2, starting transfers between devices, exchange(): lax.ppermute(to_previous, axis, backward)  4.96 us
    pallas_call x1, Pallas kernels, local(): call(pack_columns, hbm(3), [shape(MSG_Y, N)] * 2, vmem(2), [block, block,...  4.04 us
    pallas_call x1, Pallas kernels, local(): call(combine, vmem(2) + hbm(4), [pltpu.HBM((NZ, N, N), F32)] * 2, hbm(2),...  3.25 us
  transfers between devices with their start and end apart: 4, of which 3 were waited for; matrix products, arithmetic and copies ran while one was open for 0% of the time, Pallas kernels for 1%

profile of v2, /device:TPU:1, one launch (start us, length us, event | category | flops | bytes accessed | tf_op | source)
XLA Modules:
  0.0 81.4 jit_solution(3957943324564308920)
XLA Ops:
  0.6 0.0 copy-start.1
  0.6 0.0 copy-start.2
  0.6 4.0 %pack.1 = (f32[1168,128]{1,0:T(8,128)S(1)}, f32[1168,128]{1,0:T(8,128)S(1)}) custom-call(f32[16,128,128]{2,1,0:T(8,128)} %noise_in.1, f32[16,128,128]{2,1,0:T(8,128)} %source_in.3, s32[16,128,128]{2,1,0:T(8,128)} %biofilm.3), custom_call_target="tpu_custom_call" | custom-call | flops 1000000 | bytes 1000000 | tf_op jit(solution)/shard_map/pack/pallas_call | solution.py:594
  4.7 0.0 copy-start
  4.7 2.5 %collective-permute-start = (f32[1168,128]{1,0:T(8,128)S(1)}, f32[1168,128]{1,0:T(8,128)S(1)}, u32[]{:S(2)}, u32[]{:S(2)}) collective-permute-start(f32[1168,128]{1,0:T(8,128)S(1)} %get-tuple-element.21), channel_id=1, source_target_pairs={{0,1},{1,2},{2,3},{3,4},{4,5},{5,6},{6,7},{7,8},{8,9},{9,10},{10,1... | collective-permute-start | bytes 1794056 | tf_op jit(solution)/shard_map/ppermute | solution.py:589
  7.3 5.0 %collective-permute-start.1 = (f32[1168,128]{1,0:T(8,128)S(1)}, f32[1168,128]{1,0:T(8,128)S(1)}, u32[]{:S(2)}, u32[]{:S(2)}) collective-permute-start(f32[1168,128]{1,0:T(8,128)S(1)} %get-tuple-element.22), channel_id=1, source_target_pairs={{1,0},{2,1},{3,2},{4,3},{5,4},{6,5},{7,6},{8,7},{9,8},{10,9},{11,1... | collective-permute-start | bytes 1794056 | tf_op jit(solution)/shard_map/ppermute | solution.py:589
  12.2 0.0 copy-done.1
  12.2 0.0 copy-done.2
  12.2 0.9 %columns_own.1 = (f32[16,128,128]{2,1,0:T(8,128)S(1)}, f32[128,128]{1,0:T(8,128)S(1)}, f32[16,128,128]{2,1,0:T(8,128)S(1)}) custom-call(f32[16,128,128]{2,1,0:T(8,128)S(1)} %copy-done.2, s32[16,128,128]{2,1,0:T(8,128)S(1)} %copy-done.1), custom_call_target="tpu_custom_call" | custom-call | flops 1000000 | bytes 1000000 | tf_op jit(solution)/shard_map/columns_own/pallas_call | solution.py:603
  13.1 12.3 %collective-permute-done.from_left = f32[1168,128]{1,0:T(8,128)S(1)} collective-permute-done((f32[1168,128]{1,0:T(8,128)S(1)}, f32[1168,128]{1,0:T(8,128)S(1)}, u32[]{:S(2)}, u32[]{:S(2)}) %collective-permute-start) | collective-permute-done | bytes 598048 | tf_op jit(solution)/shard_map/ppermute | solution.py:589
  25.3 0.0 collective-permute-done.1.from_right
  25.4 0.0 copy-done
  25.4 0.9 %columns.1 = (f32[16,128,128]{2,1,0:T(8,128)S(1)}, f32[128,128]{1,0:T(8,128)S(1)}, f32[128,128]{1,0:T(8,128)S(1)}, f32[128,128]{1,0:T(8,128)S(1)}, f32[1248,128]{1,0:T(8,128)S(1)}, /*index=5*/f32[1248,128]{1,0:T(8,128)S(1)}) custom-call(f32[16,128,128]{2,1,0:T(8,128)S(1)} %get-tuple-element.19.own_middle, f32[128,128]{1,0:T(8,128)S(1)} %get-tuple-element.20.own_edge, ...), custom_call_target="tpu_custom_call" | custom-call | flops 1000000 | bytes 1000000 | tf_op jit(solution)/shard_map/columns/pallas_call | solution.py:610
  26.2 3.6 %collective-permute-start.2 = (f32[1248,128]{1,0:T(8,128)S(1)}, f32[1248,128]{1,0:T(8,128)S(1)}, u32[]{:S(2)}, u32[]{:S(2)}) collective-permute-start(f32[1248,128]{1,0:T(8,128)S(1)} %get-tuple-element.30), channel_id=1, source_target_pairs={{0,16},{16,32},{32,48},{48,64},{64,80},{80,96},{96,112},{112,128},... | collective-permute-start | bytes 1916936 | tf_op jit(solution)/shard_map/ppermute | solution.py:589
  29.9 0.0 collective-permute-start.3
  29.9 0.3 rows_own.1
  30.2 10.6 %collective-permute-done.2.from_up = f32[1248,128]{1,0:T(8,128)S(1)} collective-permute-done((f32[1248,128]{1,0:T(8,128)S(1)}, f32[1248,128]{1,0:T(8,128)S(1)}, u32[]{:S(2)}, u32[]{:S(2)}) %collective-permute-start.2) | collective-permute-done | bytes 639008 | tf_op jit(solution)/shard_map/ppermute | solution.py:589
  40.8 5.2 %collective-permute-done.3.from_down = f32[1248,128]{1,0:T(8,128)S(1)} collective-permute-done((f32[1248,128]{1,0:T(8,128)S(1)}, f32[1248,128]{1,0:T(8,128)S(1)}, u32[]{:S(2)}, u32[]{:S(2)}) %collective-permute-start.3) | collective-permute-done | bytes 639008 | tf_op jit(solution)/shard_map/ppermute | solution.py:589
  46.0 9.1 %powers.1 = (f32[16,128,128]{2,1,0:T(8,128)}, f32[16,128,128]{2,1,0:T(8,128)}, f32[16,128,128]{2,1,0:T(8,128)}, f32[256,128]{1,0:T(8,128)S(1)}) custom-call(f32[17,144,128]{2,1,0:T(8,128)S(1)} %get-tuple-element.26.partial, f32[16,128,128]{2,1,0:T(8,128)S(1)} %get-tuple-element.27.factor, f32[128,128]{1,0:T(8,128)S(1)} %get-tuple-element.28.edge_factor, ...), custom_call_target="tpu_custom_call" | custom-call | flops 1000000 | bytes 1000000 | tf_op jit(solution)/shard_map/powers/pallas_call | solution.py:629
  55.1 23.0 %all_to_all.11 = f32[256,1,128]{2,1,0:T(1,128)S(1)} all-to-all(f32[256,1,128]{2,1,0:T(1,128)S(1)} %bitcast.4), channel_id=1, replica_groups=mesh['gx'=16,'gy'=16] {'gx','gy'}, dimensions={0} | all-to-all | bytes 262144 | tf_op jit(solution)/shard_map/all_to_all | solution.py:642
  78.1 3.3 %combine.1 = (f32[16,128,128]{2,1,0:T(8,128)}, f32[16,128,128]{2,1,0:T(8,128)}) custom-call(f32[256,128]{1,0:T(8,128)S(1)} %bitcast.5, f32[256,128]{1,0:T(8,128)S(1)} %get-tuple-element.32.own, f32[16,128,128]{2,1,0:T(8,128)} %source_in.3, f32[16,128,128]{2,1,0:T(8,128)} %get-tuple-element.33.power1_in, f32[16,128,128]{2,1,0:T(8,128)} %get-tuple-element.34.power2_in, ...), custom_call_target="tpu_custom_call" | custom-call | flops 1000000 | bytes 1000000 | tf_op jit(solution)/shard_map/combine/pallas_call | solution.py:644
Async XLA Ops:
  0.6 11.6 %copy-start.1 = (s32[16,128,128]{2,1,0:T(8,128)S(1)}, s32[16,128,128]{2,1,0:T(8,128)}, u32[]{:S(2)}) copy-start(s32[16,128,128]{2,1,0:T(8,128)} %biofilm.3) | copy-start | bytes 3145732
  0.6 11.6 %copy-start.2 = (f32[16,128,128]{2,1,0:T(8,128)S(1)}, f32[16,128,128]{2,1,0:T(8,128)}, u32[]{:S(2)}) copy-start(f32[16,128,128]{2,1,0:T(8,128)} %noise_in.1) | copy-start | bytes 3145732
  4.7 20.7 %copy-start = (f32[16,128,128]{2,1,0:T(8,128)S(1)}, f32[16,128,128]{2,1,0:T(8,128)}, u32[]{:S(2)}) copy-start(f32[16,128,128]{2,1,0:T(8,128)} %source_in.3) | copy-start | bytes 3145732
  4.7 20.6 %collective-permute-start = (f32[1168,128]{1,0:T(8,128)S(1)}, f32[1168,128]{1,0:T(8,128)S(1)}, u32[]{:S(2)}, u32[]{:S(2)}) collective-permute-start(f32[1168,128]{1,0:T(8,128)S(1)} %get-tuple-element.21), channel_id=1, source_target_pairs={{0,1},{1,2},{2,3},{3,4},{4,5},{5,6},{6,7},{7,8},{8,9},{9,10},{10,1... | collective-permute-start | bytes 1794056 | tf_op jit(solution)/shard_map/ppermute | solution.py:589
  7.3 18.1 %collective-permute-start.1 = (f32[1168,128]{1,0:T(8,128)S(1)}, f32[1168,128]{1,0:T(8,128)S(1)}, u32[]{:S(2)}, u32[]{:S(2)}) collective-permute-start(f32[1168,128]{1,0:T(8,128)S(1)} %get-tuple-element.22), channel_id=1, source_target_pairs={{1,0},{2,1},{3,2},{4,3},{5,4},{6,5},{7,6},{8,7},{9,8},{10,9},{11,1... | collective-permute-start | bytes 1794056 | tf_op jit(solution)/shard_map/ppermute | solution.py:589
  26.2 14.6 %collective-permute-start.2 = (f32[1248,128]{1,0:T(8,128)S(1)}, f32[1248,128]{1,0:T(8,128)S(1)}, u32[]{:S(2)}, u32[]{:S(2)}) collective-permute-start(f32[1248,128]{1,0:T(8,128)S(1)} %get-tuple-element.30), channel_id=1, source_target_pairs={{0,16},{16,32},{32,48},{48,64},{64,80},{80,96},{96,112},{112,128},... | collective-permute-start | bytes 1916936 | tf_op jit(solution)/shard_map/ppermute | solution.py:589
  29.9 16.2 %collective-permute-start.3 = (f32[1248,128]{1,0:T(8,128)S(1)}, f32[1248,128]{1,0:T(8,128)S(1)}, u32[]{:S(2)}, u32[]{:S(2)}) collective-permute-start(f32[1248,128]{1,0:T(8,128)S(1)} %get-tuple-element.31), channel_id=1, source_target_pairs={{16,0},{32,16},{48,32},{64,48},{80,64},{96,80},{112,96},{128,112},... | collective-permute-start | bytes 1916936 | tf_op jit(solution)/shard_map/ppermute | solution.py:589

commit v3 on v2

--- a/solution.py
+++ b/solution.py
@@ -12,12 +12,12 @@
 F32 = jnp.float32
 BF16 = jnp.bfloat16
 
-MSG_Y = 8 * N + N + 16
-MSG_X = 17 * 72 + 24
+Y_ROWS = (4 * N, 4 * N + N + 16)
+X_ROWS = (8 * 72 + 8, 9 * 72 + 16)
 ROWS = 160
 OWN = 16
 HUGE = 1e30
-U1, U2, U3, U4, U5, U6 = 16, 4, 2, 4, 4, 2
+U1, U2, U3, U5, U6 = 16, 4, 2, 4, 2
 
 
 def iota(shape, dim):
@@ -53,7 +53,23 @@
     return jnp.where(mask, 1.0, 0.0).astype(BF16)
 
 
-def pack_columns(noise_in, source_in, biofilm_in, to_right, to_left, noise, source, biofilm, arrived):
+def pack_first(noise_in, to_right, to_left, noise, arrived):
+    low = iota((N, N), 1) < 64
+    copies = [
+        pltpu.make_async_copy(noise_in.at[2 * q : 2 * q + 2], noise.at[2 * q : 2 * q + 2], arrived.at[q])
+        for q in range(4)
+    ]
+    for copy in copies:
+        copy.start()
+    for q in range(4):
+        copies[q].wait()
+        even = noise[2 * q]
+        odd = noise[2 * q + 1]
+        to_right[q * N : q * N + N, :] = jnp.where(low, roll(even, 64, 1), odd)
+        to_left[q * N : q * N + N, :] = jnp.where(low, even, roll(odd, 64, 1))
+
+
+def pack_second(noise_in, source_in, biofilm_in, to_right, to_left, noise, source, biofilm, arrived):
     def arrivals(g):
         rows = slice(16 * g, 16 * g + 16)
         return [
@@ -83,8 +99,10 @@
         for q in range(8):
             even = noise[2 * q, rows, :]
             odd = noise[2 * q + 1, rows, :]
-            to_right[q * N + 16 * g : q * N + 16 * g + 16, :] = jnp.where(low, roll(even, 64, 1), odd)
-            to_left[q * N + 16 * g : q * N + 16 * g + 16, :] = jnp.where(low, even, roll(odd, 64, 1))
+            if q >= 4:
+                first = (q - 4) * N + 16 * g
+                to_right[first : first + 16, :] = jnp.where(low, roll(even, 64, 1), odd)
+                to_left[first : first + 16, :] = jnp.where(low, even, roll(odd, 64, 1))
             for z, n in ((2 * q, even), (2 * q + 1, odd)):
                 here = group == z
                 s = source[z, rows, :]
@@ -97,16 +115,13 @@
                 bl = jnp.where(here, roll(b, 8 * z, 1), bl)
         br = br.astype(F32)
         bl = bl.astype(F32)
-        to_right[8 * N + 16 * g : 8 * N + 16 * g + 16, :] = jnp.where(
-            slot < 3, nr, jnp.where(slot < 5, roll(br, -3, 1), sr)
-        )
-        to_left[8 * N + 16 * g : 8 * N + 16 * g + 16, :] = jnp.where(
-            slot < 3, sl, jnp.where(slot < 5, roll(bl, 3, 1), nl)
-        )
+        first = 4 * N + 16 * g
+        to_right[first : first + 16, :] = jnp.where(slot < 3, nr, jnp.where(slot < 5, roll(br, -3, 1), sr))
+        to_left[first : first + 16, :] = jnp.where(slot < 3, sl, jnp.where(slot < 5, roll(bl, 3, 1), nl))
         third_right = third_right + roll(jnp.where(slot == 5, br, 0.0), g, 1)
         third_left = third_left + roll(jnp.where(slot == 2, bl, 0.0), g, 1)
-    to_right[9 * N :, :] = third_right
-    to_left[9 * N :, :] = third_left
+    to_right[5 * N :, :] = third_right
+    to_left[5 * N :, :] = third_left
 
 
 def column_weights():
@@ -147,37 +162,61 @@
     own_edge[...] = total
 
 
-def smooth_columns(
-    own_middle, own_edge, source, biofilm, from_left, from_right,
-    middle, edge, edge_source, edge_biofilm, to_down, to_up,
-):
-    _, left, right, left_extra, right_extra = column_weights()
+def sums_beside(x, y, w):
+    high, low = split2(jnp.concatenate([x, y], axis=1))
+    return dot(high, w) + dot(low, w)
+
+
+def half_columns(first_layer, own_middle, from_left, from_right, middle, to_down, to_up):
+    _, left, right, _, _ = column_weights()
     both = jnp.concatenate([left, right], axis=0)
-    both_extra = jnp.concatenate([left_extra, right_extra], axis=0)
-    slot = iota((N, N), 1) % 8
-
-    def times(x, y, w):
-        high, low = split2(jnp.concatenate([x, y], axis=1))
-        return dot(high, w) + dot(low, w)
-
-    extra_left = from_left[8 * N : 9 * N, :]
-    extra_right = from_right[8 * N : 9 * N, :]
-    total = own_edge[...] + times(extra_left, extra_right, both_extra)
-    for q in range(8):
-        halo = times(from_left[q * N : q * N + N, :], from_right[q * N : q * N + N, :], both)
-        total = total + roll(halo[:, 2 * N :], 16 * q, 1)
-        for z in (2 * q, 2 * q + 1):
-            field = own_middle[z] + halo[:, (z % 2) * N : (z % 2) * N + N]
+    total = jnp.zeros((N, N), F32)
+    for q in range(4):
+        rows = slice(q * N, q * N + N)
+        halo = sums_beside(from_left[rows, :], from_right[rows, :], both)
+        total = total + roll(halo[:, 2 * N :], 8 * first_layer + 16 * q, 1)
+        for k in (0, 1):
+            z = 2 * q + k
+            field = own_middle[first_layer + z] + halo[:, k * N : k * N + N]
             middle[z] = field
             to_down[z * 72 : z * 72 + 72, :] = field[56:, :]
             to_up[z * 72 : z * 72 + 72, :] = field[:72, :]
+    return total
+
+
+def outer_rows(to_down, to_up, z, tail, s, b):
+    to_down[z * 72 : z * 72 + 3, :] = s[125:128, :]
+    to_down[z * 72 + 3 : z * 72 + 5, :] = b[126:128, :].astype(F32)
+    to_down[tail + z : tail + z + 1, :] = b[125:126, :].astype(F32)
+    to_up[z * 72 + 67 : z * 72 + 70, :] = s[0:3, :]
+    to_up[z * 72 + 70 : z * 72 + 72, :] = b[0:2, :].astype(F32)
+    to_up[tail + z : tail + z + 1, :] = b[2:3, :].astype(F32)
+
+
+def columns_first(own_middle, source, biofilm, from_left, from_right, middle, edge, to_down, to_up):
+    edge[...] = half_columns(0, own_middle, from_left, from_right, middle, to_down, to_up)
+    for z in range(8):
+        outer_rows(to_down, to_up, z, 8 * 72, source.at[z], biofilm.at[z])
+
+
+def columns_second(
+    own_middle, own_edge, first_edge, source, biofilm, from_left, from_right,
+    middle, edge, edge_source, edge_biofilm, to_down, to_up,
+):
+    _, _, _, left_extra, right_extra = column_weights()
+    slot = iota((N, N), 1) % 8
+    extra_left = from_left[4 * N : 5 * N, :]
+    extra_right = from_right[4 * N : 5 * N, :]
+    total = own_edge[...] + first_edge[...]
+    total = total + sums_beside(extra_left, extra_right, jnp.concatenate([left_extra, right_extra], axis=0))
+    total = total + half_columns(8, own_middle, from_left, from_right, middle, to_down, to_up)
     edge[...] = total
-    to_down[16 * 72 : 17 * 72, :] = total[56:, :]
-    to_up[16 * 72 : 17 * 72, :] = total[:72, :]
+    to_down[8 * 72 : 9 * 72, :] = total[56:, :]
+    to_up[8 * 72 : 9 * 72, :] = total[:72, :]
 
     edge_source[...] = jnp.where(slot >= 5, extra_left, jnp.where(slot <= 2, extra_right, 0.0))
-    third_left = from_left[9 * N :, :]
-    third_right = from_right[9 * N :, :]
+    third_left = from_left[5 * N :, :]
+    third_right = from_right[5 * N :, :]
     levels = jnp.where(slot >= 6, roll(extra_left, 3, 1), jnp.where(slot <= 1, roll(extra_right, -3, 1), 0.0))
     slot16 = iota((16, N), 1) % 8
     for g in range(8):
@@ -186,17 +225,11 @@
             slot16 == 5, roll(third_left, -g, 1), jnp.where(slot16 == 2, roll(third_right, -g, 1), levels[rows, :])
         )
 
-    to_down[17 * 72 :, :] = jnp.zeros((24, N), F32)
-    to_up[17 * 72 :, :] = jnp.zeros((24, N), F32)
-    for z in range(17):
-        s = source.at[z] if z < 16 else edge_source
-        b = biofilm.at[z] if z < 16 else edge_biofilm
-        to_down[z * 72 : z * 72 + 3, :] = s[125:128, :]
-        to_down[z * 72 + 3 : z * 72 + 5, :] = b[126:128, :].astype(F32)
-        to_down[17 * 72 + z : 17 * 72 + z + 1, :] = b[125:126, :].astype(F32)
-        to_up[z * 72 + 67 : z * 72 + 70, :] = s[0:3, :]
-        to_up[z * 72 + 70 : z * 72 + 72, :] = b[0:2, :].astype(F32)
-        to_up[17 * 72 + z : 17 * 72 + z + 1, :] = b[2:3, :].astype(F32)
+    to_down[9 * 72 :, :] = jnp.zeros((16, N), F32)
+    to_up[9 * 72 :, :] = jnp.zeros((16, N), F32)
+    for z in range(8):
+        outer_rows(to_down, to_up, z, 9 * 72, source.at[8 + z], biofilm.at[8 + z])
+    outer_rows(to_down, to_up, 8, 9 * 72, edge_source, edge_biofilm)
 
 
 def row_weights():
@@ -214,11 +247,45 @@
     return [out[:, k * N : k * N + N] for k in range(len(planes))]
 
 
+def halo_rows(from_up, from_down, z):
+    first = pl.multiple_of(z * 72, 8)
+    return jnp.concatenate([from_up[pl.ds(first + 8, 64), :], from_down[pl.ds(first, 64), :]], axis=0)
+
+
+def finish_sums(from_up, from_down, z, sums, out, lanes=None):
+    row8 = iota((8, N), 0)
+    row144 = iota((144, N), 0)
+    first = pl.multiple_of(z * 72, 8)
+    above = jnp.where(row8 >= 5, from_up[pl.ds(first, 8), :], 0.0)
+    below = jnp.where(row8 <= 2, from_down[pl.ds(first + 64, 8), :], 0.0)
+    above = jnp.where(row8 >= 5, above + roll(above, 7, 0) + roll(above, 6, 0), 0.0)
+    below = jnp.where(row8 <= 2, below + roll(below, 1, 0) + roll(below, 2, 0), 0.0)
+    total = jnp.concatenate([sums[:8] + above, sums[8:136], sums[136:] + below], axis=0) * (1.0 / WIDTH)
+    out[...] = total
+    real = (row144 >= 5) & (row144 <= 138)
+    if lanes is not None:
+        real = real & lanes
+    return jnp.max(jnp.where(real, total, -HUGE).reshape(18, 8, N), axis=0)
+
+
+def rows_first(middle, from_up, from_down, logperm, largest):
+    own, halo = row_weights()
+    most = jnp.full((8, N), -HUGE, F32)
+    for z in range(0, 8, 2):
+        inner = row_sums(own, middle[z], middle[z + 1])
+        outer = row_sums(halo, *[halo_rows(from_up, from_down, z + i) for i in (0, 1)])
+        for i in (0, 1):
+            most = jnp.maximum(
+                most, finish_sums(from_up, from_down, z + i, inner[i] + outer[i], logperm.at[z + i])
+            )
+    largest[...] = most
+
+
 def row_sums_own(middle, edge, edge_biofilm, partial, factor):
     own, _ = row_weights()
-    for z in range(0, 16, 2):
+    for z in range(0, 8, 2):
         partial[z], partial[z + 1] = row_sums(own, middle[z], middle[z + 1])
-    partial[16] = row_sums(own, edge[...])[0]
+    partial[8] = row_sums(own, edge[...])[0]
     factor[...] = resistance_factor(edge_biofilm[...])
 
 
@@ -242,9 +309,9 @@
 
 
 def operate_powers(
-    partial, factor, edge_factor, edge_source, source, from_up, from_down,
+    logperm1, largest1, partial, factor, edge_factor, edge_source, source, from_up1, from_down1, from_up2, from_down2,
     power1, power2, power3, table,
-    resist, across_x, across_y, across_z, flow, field0, field1, field2, field3, plane_resist, plane_field,
+    resist, across_x, across_y, across_z, flow, field0, field1, field2, field3, logperm2, plane_resist, plane_field,
     side_resist, side_x, side_y, side_z, side0, side1, side2, side_flux, done,
 ):
     lane = iota((8, N), 1)
@@ -252,54 +319,42 @@
 
     _, halo = row_weights()
     edge_lane = (iota((144, N), 1) % 8 <= 2) | (iota((144, N), 1) % 8 >= 5)
-    row144 = iota((144, N), 0)
-    real_row = (row144 >= 5) & (row144 <= 138)
-
-    def halo_rows(z):
-        first = pl.multiple_of(z * 72, 8)
-        return jnp.concatenate([from_up[pl.ds(first + 8, 64), :], from_down[pl.ds(first, 64), :]], axis=0)
-
-    def finish(z, out, sums, real):
-        first = pl.multiple_of(z * 72, 8)
-        above = jnp.where(row8 >= 5, from_up[pl.ds(first, 8), :], 0.0)
-        below = jnp.where(row8 <= 2, from_down[pl.ds(first + 64, 8), :], 0.0)
-        above = jnp.where(row8 >= 5, above + roll(above, 7, 0) + roll(above, 6, 0), 0.0)
-        below = jnp.where(row8 <= 2, below + roll(below, 1, 0) + roll(below, 2, 0), 0.0)
-        total = sums + partial[z]
-        total = jnp.concatenate([total[:8] + above, total[8:136], total[136:] + below], axis=0) * (1.0 / WIDTH)
-        out[8:152, :] = total
-        return jnp.max(jnp.where(real, total, -HUGE).reshape(18, 8, N), axis=0)
-
-    def smooth(k, largest):
-        first, second = row_sums(halo, halo_rows(2 * k), halo_rows(2 * k + 1))
-        largest = jnp.maximum(largest, finish(2 * k, resist.at[2 * k], first, real_row))
-        return jnp.maximum(largest, finish(2 * k + 1, resist.at[2 * k + 1], second, real_row))
-
-    largest = finish(16, plane_resist, row_sums(halo, halo_rows(16))[0], real_row & edge_lane)
-    largest = lax.fori_loop(0, 8, smooth, largest, unroll=U4)
+    second = (from_up2, from_down2)
+    largest = largest1[...]
+    for z in (0, 2, 4, 6):
+        pair = row_sums(halo, halo_rows(*second, z), halo_rows(*second, z + 1))
+        for i in (0, 1):
+            sums = partial[z + i] + pair[i]
+            largest = jnp.maximum(largest, finish_sums(*second, z + i, sums, logperm2.at[z + i]))
+    sums = partial[8] + row_sums(halo, halo_rows(*second, 8))[0]
+    largest = jnp.maximum(largest, finish_sums(*second, 8, sums, logperm2.at[8], edge_lane))
     top = jnp.max(jnp.max(largest, axis=0, keepdims=True), axis=1, keepdims=True)
     top = jnp.maximum(top, -60.0)
 
-    def halo_tiles(z):
+    def halo_tiles(half, z):
+        from_up, from_down, tail = half
         first = pl.multiple_of(z * 72, 8)
         above = from_up[pl.ds(first, 8), :]
         below = from_down[pl.ds(first + 64, 8), :]
-        third_above = from_up[pl.ds(17 * 72 + z, 1), :]
-        third_below = from_down[pl.ds(17 * 72 + z, 1), :]
+        third_above = from_up[pl.ds(tail + z, 1), :]
+        third_below = from_down[pl.ds(tail + z, 1), :]
         source_above = jnp.where(row8 >= 5, roll(above, 5, 0), 0.0)
         source_below = jnp.where(row8 <= 2, roll(below, 5, 0), 0.0)
         biofilm_above = jnp.where(row8 == 5, third_above, jnp.where(row8 >= 6, roll(above, 3, 0), 0.0))
         biofilm_below = jnp.where(row8 == 2, third_below, jnp.where(row8 <= 1, roll(below, 2, 0), 0.0))
         return source_above, source_below, biofilm_above, biofilm_below
 
-    def prepare(z, out, field, own_source, own_factor):
-        source_above, source_below, biofilm_above, biofilm_below = halo_tiles(z)
+    first_half = (from_up1, from_down1, 8 * 72)
+    second_half = (from_up2, from_down2, 9 * 72)
+
+    def prepare(half, z, logperm, out, field, own_source, own_factor):
+        source_above, source_below, biofilm_above, biofilm_below = halo_tiles(half, z)
         field[8:16, :] = source_above
         field[16:144, :] = own_source
         field[144:152, :] = source_below
-        out[8:16, :] = jnp.where(row8 >= 5, resistance(out[8:16, :], resistance_factor(biofilm_above), top), HUGE)
-        out[144:152, :] = jnp.where(row8 <= 2, resistance(out[144:152, :], resistance_factor(biofilm_below), top), HUGE)
-        out[16:144, :] = resistance(out[16:144, :], own_factor, top)
+        out[8:16, :] = jnp.where(row8 >= 5, resistance(logperm[0:8, :], resistance_factor(biofilm_above), top), HUGE)
+        out[144:152, :] = jnp.where(row8 <= 2, resistance(logperm[136:144, :], resistance_factor(biofilm_below), top), HUGE)
+        out[16:144, :] = resistance(logperm[8:136, :], own_factor, top)
         empty = jnp.full((8, N), HUGE, F32)
         none = jnp.zeros((8, N), F32)
         out[0:8, :] = empty
@@ -307,16 +362,19 @@
         field[0:8, :] = none
         field[152:160, :] = none
 
-    def prepare_layer(z, carry):
-        prepare(z, resist.at[z], field0.at[z], source[z], factor[z])
-        none = jnp.zeros((8, N), F32)
-        for ref in (field1, field2, across_x):
-            ref[z, 0:8, :] = none
-            ref[z, 152:160, :] = none
-        return carry
-
-    prepare(16, plane_resist, plane_field, edge_source[...], edge_factor[...])
-    lax.fori_loop(0, 16, prepare_layer, 0, unroll=U6)
+    prepare(second_half, 8, logperm2.at[8], plane_resist, plane_field, edge_source[...], edge_factor[...])
+    for base, half, logperm in ((0, first_half, logperm1), (8, second_half, logperm2)):
+
+        def prepare_layer(k, carry, base=base, half=half, logperm=logperm):
+            z = base + k
+            prepare(half, k, logperm.at[k], resist.at[z], field0.at[z], source[z], factor[z])
+            none = jnp.zeros((8, N), F32)
+            for ref in (field1, field2, across_x):
+                ref[z, 0:8, :] = none
+                ref[z, 152:160, :] = none
+            return carry
+
+        lax.fori_loop(0, 8, prepare_layer, 0, unroll=U6)
 
     a = iota((N, 2 * N), 0)
     o = iota((N, 2 * N), 1)
@@ -592,53 +650,82 @@
 def local(noise, biofilm, source):
     block = pltpu.VMEM((NZ, N, N), F32)
     to_right, to_left = call(
-        pack_columns,
+        pack_first,
+        hbm(1),
+        [shape(Y_ROWS[0], N)] * 2,
+        vmem(2),
+        [pltpu.VMEM((8, N, N), F32), pltpu.SemaphoreType.DMA((4,))],
+        name="pack_first",
+    )(in_hbm(noise))
+    beside1 = exchange(to_right, to_left, "gy")
+    to_right, to_left = call(
+        pack_second,
         hbm(3),
-        [shape(MSG_Y, N)] * 2,
+        [shape(Y_ROWS[1], N)] * 2,
         vmem(2),
         [block, block, pltpu.VMEM((NZ, N, N), jnp.int32), pltpu.SemaphoreType.DMA((3, 8))],
-        name="pack",
+        name="pack_second",
+        cost=2e10,
     )(in_hbm(noise), in_hbm(source), in_hbm(biofilm))
-    from_left, from_right = exchange(to_right, to_left, "gy")
+    beside2 = exchange(to_right, to_left, "gy")
     own_middle, own_edge, factor = call(
         column_sums_own,
         vmem(2),
         [shape(NZ, N, N), shape(N, N), shape(NZ, N, N)],
         vmem(3),
         name="columns_own",
+        cost=2e10,
     )(noise, biofilm)
-    middle, edge, edge_source, edge_biofilm, to_down, to_up = call(
-        smooth_columns,
+    middle1, first_edge, to_down, to_up = call(
+        columns_first,
+        vmem(5),
+        [shape(8, N, N), shape(N, N)] + [shape(X_ROWS[0], N)] * 2,
+        vmem(4),
+        name="columns_first",
+    )(own_middle, source, biofilm, *beside1)
+    above_below1 = exchange(to_down, to_up, "gx")
+    middle2, edge, edge_source, edge_biofilm, to_down, to_up = call(
+        columns_second,
+        vmem(7),
+        [shape(8, N, N), shape(N, N), shape(N, N), shape(N, N)] + [shape(X_ROWS[1], N)] * 2,
         vmem(6),
-        [shape(NZ, N, N), shape(N, N), shape(N, N), shape(N, N), shape(MSG_X, N), shape(MSG_X, N)],
-        vmem(6),
-        name="columns",
-    )(own_middle, own_edge, source, biofilm, from_left, from_right)
-    from_up, from_down = exchange(to_down, to_up, "gx")
+        name="columns_second",
+        cost=2e10,
+    )(own_middle, own_edge, first_edge, source, biofilm, *beside2)
+    above_below2 = exchange(to_down, to_up, "gx")
     partial, edge_factor = call(
         row_sums_own,
         vmem(3),
-        [shape(NZ + 1, 144, N), shape(N, N)],
+        [shape(9, 144, N), shape(N, N)],
         vmem(2),
         name="rows_own",
-    )(middle, edge, edge_biofilm)
+        cost=1,
+    )(middle2, edge, edge_biofilm)
+    logperm1, largest1 = call(
+        rows_first,
+        vmem(3),
+        [shape(8, 144, N), shape(8, N)],
+        vmem(2),
+        name="rows_first",
+        cost=2e10,
+    )(middle1, *above_below1)
     devices = lax.axis_size("gx") * lax.axis_size("gy")
     layers = pltpu.VMEM((NZ, ROWS, N), F32)
     plane = pltpu.VMEM((ROWS, N), F32)
     sides = pltpu.VMEM((2, ROWS, N), F32)
     power1, power2, power3, table = call(
         operate_powers,
-        vmem(7),
+        vmem(11),
         [pltpu.HBM((NZ, N, N), F32)] * 3 + [shape(devices, N)],
         hbm(3) + vmem(1),
         [layers] * 3
         + [pltpu.VMEM((NZ + 1, ROWS, N), F32)]
         + [layers] * 4
-        + [block, plane, plane]
+        + [block, pltpu.VMEM((9, 144, N), F32), plane, plane]
         + [sides] * 8
         + [pltpu.SemaphoreType.DMA((3,))],
         name="powers",
-    )(partial, factor, edge_factor, edge_source, source, from_up, from_down)
+    )(logperm1, largest1, partial, factor, edge_factor, edge_source, source, *above_below1, *above_below2)
     everyone = lax.all_to_all(table, ("gx", "gy"), 0, 0, tiled=True)
     return tuple(
         call(

time: 81.5 us -> 74.4 us (0.913)
  waiting for transfers between devices: 28.1 us -> 12.7 us
  starting transfers between devices: 11.1 us -> 19.5 us
  blocking collectives: 23 us -> 21.4 us
  Pallas kernels: 18.4 us -> 19.7 us
    ppermute x2 -> x4, waiting for transfers between devices: 22.8 us -> 2.03 us  [exchange(): lax.ppermute(to_next, axis, forward)]
    ppermute x2 -> x4, waiting for transfers between devices: 5.25 us -> 10.6 us  [exchange(): lax.ppermute(to_previous, axis, backward)]
    ppermute x2 -> x4, starting transfers between devices: 6.19 us -> 10.9 us  [exchange(): lax.ppermute(to_next, axis, forward)]
    ppermute x2 -> x4, starting transfers between devices: 4.96 us -> 8.53 us  [exchange(): lax.ppermute(to_previous, axis, backward)]
    all_to_all x1, blocking collectives: 23 us -> 21.4 us  [local(): everyone = lax.all_to_all(table, ('gx', 'gy'), 0, 0, tiled=True)]
    pallas_call x4 -> x7, Pallas kernels: 14.3 us -> 15.6 us  [the longest x1 8.78 us: local(): call(operate_powers, vmem(11), [pltpu.HBM((NZ, N, N), F32)] * 3 + [shape(...]
  transfers between devices with their start and end apart: 4 -> 8, of which waited for: 3 -> 4; matrix products, arithmetic and copies ran while one was open for 0% -> 0% of each run, Pallas kernels for 1% -> 9%
where the time goes in v3:
time: 74.4 us; the launch traced here: 74.2 us
  blocking collectives  21.4 us (29%)
  Pallas kernels  19.7 us (26%)
  starting transfers between devices  19.5 us (26%)
  waiting for transfers between devices  12.7 us (17%)
  between operations  0.9 us (1%)
    all_to_all x1, blocking collectives, local(): everyone = lax.all_to_all(table, ('gx', 'gy'), 0, 0, tiled=True)  21.4 us
    ppermute x4, starting transfers between devices, exchange(): lax.ppermute(to_next, axis, forward)  10.9 us
    ppermute x4, waiting for transfers between devices, exchange(): lax.ppermute(to_previous, axis, backward)  10.6 us
    pallas_call x1, Pallas kernels, local(): call(operate_powers, vmem(11), [pltpu.HBM((NZ, N, N), F32)] * 3 + [shape(...  8.78 us
    ppermute x4, starting transfers between devices, exchange(): lax.ppermute(to_previous, axis, backward)  8.53 us
    pallas_call x1, Pallas kernels, local(): call(pack_second, hbm(3), [shape(Y_ROWS[1], N)] * 2, vmem(2), [block, blo...  3.75 us
    pallas_call x1, Pallas kernels, local(): call(combine, vmem(2) + hbm(4), [pltpu.HBM((NZ, N, N), F32)] * 2, hbm(2),...  3.25 us
    ppermute x4, waiting for transfers between devices, exchange(): lax.ppermute(to_next, axis, forward)  2.03 us
  transfers between devices with their start and end apart: 8, of which 4 were waited for; matrix products, arithmetic and copies ran while one was open for 0% of the time, Pallas kernels for 9%

profile of v3, /device:TPU:1, one launch (start us, length us, event | category | flops | bytes accessed | tf_op | source)
XLA Modules:
  0.0 74.2 jit_solution(12098181408966025556)
XLA Ops:
  0.6 1.3 %pack_first.1 = (f32[512,128]{1,0:T(8,128)S(1)}, f32[512,128]{1,0:T(8,128)S(1)}) custom-call(f32[16,128,128]{2,1,0:T(8,128)} %noise_in.3), custom_call_target="tpu_custom_call" | custom-call | flops 1000000 | bytes 1000000 | tf_op jit(solution)/shard_map/pack_first/pallas_call | solution.py:652
  2.0 2.5 %collective-permute-start = (f32[512,128]{1,0:T(8,128)S(1)}, f32[512,128]{1,0:T(8,128)S(1)}, u32[]{:S(2)}, u32[]{:S(2)}) collective-permute-start(f32[512,128]{1,0:T(8,128)S(1)} %get-tuple-element.28), channel_id=1, source_target_pairs={{0,1},{1,2},{2,3},{3,4},{4,5},{5,6},{6,7},{7,8},{8,9},{9,10},{10,1... | collective-permute-start | bytes 786440 | tf_op jit(solution)/shard_map/ppermute | solution.py:647
  4.5 0.0 copy-start.1
  4.5 0.0 copy-start.2
  4.5 5.0 %collective-permute-start.1 = (f32[512,128]{1,0:T(8,128)S(1)}, f32[512,128]{1,0:T(8,128)S(1)}, u32[]{:S(2)}, u32[]{:S(2)}) collective-permute-start(f32[512,128]{1,0:T(8,128)S(1)} %get-tuple-element.29), channel_id=1, source_target_pairs={{1,0},{2,1},{3,2},{4,3},{5,4},{6,5},{7,6},{8,7},{9,8},{10,9},{11,1... | collective-permute-start | bytes 786440 | tf_op jit(solution)/shard_map/ppermute | solution.py:647
  9.5 3.8 %pack_second.1 = (f32[656,128]{1,0:T(8,128)S(1)}, f32[656,128]{1,0:T(8,128)S(1)}) custom-call(f32[16,128,128]{2,1,0:T(8,128)} %noise_in.3, f32[16,128,128]{2,1,0:T(8,128)} %source_in.3, s32[16,128,128]{2,1,0:T(8,128)} %biofilm.5), custom_call_target="tpu_custom_call" | custom-call | flops 20000000000 | bytes 20000000000 | tf_op jit(solution)/shard_map/pack_second/pallas_call | solution.py:661
  13.3 0.1 collective-permute-start.4
  13.4 0.0 copy-start
  13.4 3.6 %collective-permute-start.5 = (f32[656,128]{1,0:T(8,128)S(1)}, f32[656,128]{1,0:T(8,128)S(1)}, u32[]{:S(2)}, u32[]{:S(2)}) collective-permute-start(f32[656,128]{1,0:T(8,128)S(1)} %get-tuple-element.38), channel_id=1, source_target_pairs={{1,0},{2,1},{3,2},{4,3},{5,4},{6,5},{7,6},{8,7},{9,8},{10,9},{11,1... | collective-permute-start | bytes 1007624 | tf_op jit(solution)/shard_map/ppermute | solution.py:647
  16.9 0.0 copy-done.1
  16.9 0.0 copy-done.2
  16.9 0.9 %columns_own.1 = (f32[16,128,128]{2,1,0:T(8,128)S(1)}, f32[128,128]{1,0:T(8,128)S(1)}, f32[16,128,128]{2,1,0:T(8,128)S(1)}) custom-call(f32[16,128,128]{2,1,0:T(8,128)S(1)} %copy-done.2, s32[16,128,128]{2,1,0:T(8,128)S(1)} %copy-done.1), custom_call_target="tpu_custom_call" | custom-call | flops 20000000000 | bytes 20000000000 | tf_op jit(solution)/shard_map/columns_own/pallas_call | solution.py:671
  17.8 0.0 collective-permute-done.from_left
  17.8 0.0 collective-permute-done.1.from_right
  17.8 0.0 copy-done
  17.8 0.5 columns_first.1
  18.4 3.9 %collective-permute-start.2 = (f32[584,128]{1,0:T(8,128)S(1)}, f32[584,128]{1,0:T(8,128)S(1)}, u32[]{:S(2)}, u32[]{:S(2)}) collective-permute-start(f32[584,128]{1,0:T(8,128)S(1)} %get-tuple-element.31), channel_id=1, source_target_pairs={{0,16},{16,32},{32,48},{48,64},{64,80},{80,96},{96,112},{112,128},... | collective-permute-start | bytes 897032 | tf_op jit(solution)/shard_map/ppermute | solution.py:647
  22.3 0.0 collective-permute-start.3
  22.3 1.6 %collective-permute-done.4.from_left = f32[656,128]{1,0:T(8,128)S(1)} collective-permute-done((f32[656,128]{1,0:T(8,128)S(1)}, f32[656,128]{1,0:T(8,128)S(1)}, u32[]{:S(2)}, u32[]{:S(2)}) %collective-permute-start.4) | collective-permute-done | bytes 335904 | tf_op jit(solution)/shard_map/ppermute | solution.py:647
  23.9 0.0 collective-permute-done.5.from_right
  23.9 0.6 columns_second.1
  24.5 4.4 %collective-permute-start.6 = (f32[664,128]{1,0:T(8,128)S(1)}, f32[664,128]{1,0:T(8,128)S(1)}, u32[]{:S(2)}, u32[]{:S(2)}) collective-permute-start(f32[664,128]{1,0:T(8,128)S(1)} %get-tuple-element.46), channel_id=1, source_target_pairs={{0,16},{16,32},{32,48},{48,64},{64,80},{80,96},{96,112},{112,128},... | collective-permute-start | bytes 1019912 | tf_op jit(solution)/shard_map/ppermute | solution.py:647
  28.9 0.0 collective-permute-start.7
  28.9 0.3 rows_own.1
  29.1 0.0 collective-permute-done.2.from_up.from_up1
  29.1 4.4 %collective-permute-done.3.from_down.from_down1 = f32[584,128]{1,0:T(8,128)S(1)} collective-permute-done((f32[584,128]{1,0:T(8,128)S(1)}, f32[584,128]{1,0:T(8,128)S(1)}, u32[]{:S(2)}, u32[]{:S(2)}) %collective-permute-start.3) | collective-permute-done | bytes 299040 | tf_op jit(solution)/shard_map/ppermute | solution.py:647
  33.5 0.3 rows_first.1
  33.9 0.4 collective-permute-done.6.from_up2
  34.3 6.3 %collective-permute-done.7.from_down2 = f32[664,128]{1,0:T(8,128)S(1)} collective-permute-done((f32[664,128]{1,0:T(8,128)S(1)}, f32[664,128]{1,0:T(8,128)S(1)}, u32[]{:S(2)}, u32[]{:S(2)}) %collective-permute-start.7) | collective-permute-done | bytes 340000 | tf_op jit(solution)/shard_map/ppermute | solution.py:647
  40.6 8.8 %powers.1 = (f32[16,128,128]{2,1,0:T(8,128)}, f32[16,128,128]{2,1,0:T(8,128)}, f32[16,128,128]{2,1,0:T(8,128)}, f32[256,128]{1,0:T(8,128)S(1)}) custom-call(f32[8,144,128]{2,1,0:T(8,128)S(1)} %get-tuple-element.33.logperm1, f32[8,128]{1,0:T(8,128)S(1)} %get-tuple-element.34.largest1, f32[9,144,128]{2,1,0:T(8,128)S(1)} %get-tuple-element.42.partial, ...), custom_call_target="tpu_custom_call" | custom-call | flops 1000000 | bytes 1000000 | tf_op jit(solution)/shard_map/powers/pallas_call | solution.py:716
  49.4 21.4 %all_to_all.11 = f32[256,1,128]{2,1,0:T(1,128)S(1)} all-to-all(f32[256,1,128]{2,1,0:T(1,128)S(1)} %bitcast.4), channel_id=1, replica_groups=mesh['gx'=16,'gy'=16] {'gx','gy'}, dimensions={0} | all-to-all | bytes 262144 | tf_op jit(solution)/shard_map/all_to_all | solution.py:729
  70.8 3.3 %combine.1 = (f32[16,128,128]{2,1,0:T(8,128)}, f32[16,128,128]{2,1,0:T(8,128)}) custom-call(f32[256,128]{1,0:T(8,128)S(1)} %bitcast.5, f32[256,128]{1,0:T(8,128)S(1)} %get-tuple-element.48.own, f32[16,128,128]{2,1,0:T(8,128)} %source_in.3, f32[16,128,128]{2,1,0:T(8,128)} %get-tuple-element.49.power1_in, f32[16,128,128]{2,1,0:T(8,128)} %get-tuple-element.50.power2_in, ...), custom_call_target="tpu_custom_call" | custom-call | flops 1000000 | bytes 1000000 | tf_op jit(solution)/shard_map/combine/pallas_call | solution.py:731
Async XLA Ops:
  2.0 15.8 %collective-permute-start = (f32[512,128]{1,0:T(8,128)S(1)}, f32[512,128]{1,0:T(8,128)S(1)}, u32[]{:S(2)}, u32[]{:S(2)}) collective-permute-start(f32[512,128]{1,0:T(8,128)S(1)} %get-tuple-element.28), channel_id=1, source_target_pairs={{0,1},{1,2},{2,3},{3,4},{4,5},{5,6},{6,7},{7,8},{8,9},{9,10},{10,1... | collective-permute-start | bytes 786440 | tf_op jit(solution)/shard_map/ppermute | solution.py:647
  4.5 12.4 %copy-start.1 = (s32[16,128,128]{2,1,0:T(8,128)S(1)}, s32[16,128,128]{2,1,0:T(8,128)}, u32[]{:S(2)}) copy-start(s32[16,128,128]{2,1,0:T(8,128)} %biofilm.5) | copy-start | bytes 3145732
  4.5 12.4 %copy-start.2 = (f32[16,128,128]{2,1,0:T(8,128)S(1)}, f32[16,128,128]{2,1,0:T(8,128)}, u32[]{:S(2)}) copy-start(f32[16,128,128]{2,1,0:T(8,128)} %noise_in.3) | copy-start | bytes 3145732
  4.5 13.3 %collective-permute-start.1 = (f32[512,128]{1,0:T(8,128)S(1)}, f32[512,128]{1,0:T(8,128)S(1)}, u32[]{:S(2)}, u32[]{:S(2)}) collective-permute-start(f32[512,128]{1,0:T(8,128)S(1)} %get-tuple-element.29), channel_id=1, source_target_pairs={{1,0},{2,1},{3,2},{4,3},{5,4},{6,5},{7,6},{8,7},{9,8},{10,9},{11,1... | collective-permute-start | bytes 786440 | tf_op jit(solution)/shard_map/ppermute | solution.py:647
  13.3 10.6 %collective-permute-start.4 = (f32[656,128]{1,0:T(8,128)S(1)}, f32[656,128]{1,0:T(8,128)S(1)}, u32[]{:S(2)}, u32[]{:S(2)}) collective-permute-start(f32[656,128]{1,0:T(8,128)S(1)} %get-tuple-element.37), channel_id=1, source_target_pairs={{0,1},{1,2},{2,3},{3,4},{4,5},{5,6},{6,7},{7,8},{8,9},{9,10},{10,1... | collective-permute-start | bytes 1007624 | tf_op jit(solution)/shard_map/ppermute | solution.py:647
  13.4 4.5 %copy-start = (f32[16,128,128]{2,1,0:T(8,128)S(1)}, f32[16,128,128]{2,1,0:T(8,128)}, u32[]{:S(2)}) copy-start(f32[16,128,128]{2,1,0:T(8,128)} %source_in.3) | copy-start | bytes 3145732
  13.4 10.5 %collective-permute-start.5 = (f32[656,128]{1,0:T(8,128)S(1)}, f32[656,128]{1,0:T(8,128)S(1)}, u32[]{:S(2)}, u32[]{:S(2)}) collective-permute-start(f32[656,128]{1,0:T(8,128)S(1)} %get-tuple-element.38), channel_id=1, source_target_pairs={{1,0},{2,1},{3,2},{4,3},{5,4},{6,5},{7,6},{8,7},{9,8},{10,9},{11,1... | collective-permute-start | bytes 1007624 | tf_op jit(solution)/shard_map/ppermute | solution.py:647
  18.4 10.8 %collective-permute-start.2 = (f32[584,128]{1,0:T(8,128)S(1)}, f32[584,128]{1,0:T(8,128)S(1)}, u32[]{:S(2)}, u32[]{:S(2)}) collective-permute-start(f32[584,128]{1,0:T(8,128)S(1)} %get-tuple-element.31), channel_id=1, source_target_pairs={{0,16},{16,32},{32,48},{48,64},{64,80},{80,96},{96,112},{112,128},... | collective-permute-start | bytes 897032 | tf_op jit(solution)/shard_map/ppermute | solution.py:647
  22.3 11.2 %collective-permute-start.3 = (f32[584,128]{1,0:T(8,128)S(1)}, f32[584,128]{1,0:T(8,128)S(1)}, u32[]{:S(2)}, u32[]{:S(2)}) collective-permute-start(f32[584,128]{1,0:T(8,128)S(1)} %get-tuple-element.32), channel_id=1, source_target_pairs={{16,0},{32,16},{48,32},{64,48},{80,64},{96,80},{112,96},{128,112},... | collective-permute-start | bytes 897032 | tf_op jit(solution)/shard_map/ppermute | solution.py:647
  24.5 9.8 %collective-permute-start.6 = (f32[664,128]{1,0:T(8,128)S(1)}, f32[664,128]{1,0:T(8,128)S(1)}, u32[]{:S(2)}, u32[]{:S(2)}) collective-permute-start(f32[664,128]{1,0:T(8,128)S(1)} %get-tuple-element.46), channel_id=1, source_target_pairs={{0,16},{16,32},{32,48},{48,64},{64,80},{80,96},{96,112},{112,128},... | collective-permute-start | bytes 1019912 | tf_op jit(solution)/shard_map/ppermute | solution.py:647
  28.9 11.7 %collective-permute-start.7 = (f32[664,128]{1,0:T(8,128)S(1)}, f32[664,128]{1,0:T(8,128)S(1)}, u32[]{:S(2)}, u32[]{:S(2)}) collective-permute-start(f32[664,128]{1,0:T(8,128)S(1)} %get-tuple-element.47), channel_id=1, source_target_pairs={{16,0},{32,16},{48,32},{64,48},{80,64},{96,80},{112,96},{128,112},... | collective-permute-start | bytes 1019912 | tf_op jit(solution)/shard_map/ppermute | solution.py:647

commit v4 on v3

--- a/solution.py
+++ b/solution.py
@@ -17,7 +17,9 @@
 ROWS = 160
 OWN = 16
 HUGE = 1e30
-U1, U2, U3, U5, U6 = 16, 4, 2, 4, 2
+U1, U2, U3, U5, U6 = 16, 4, 4, 16, 8
+V2, V3 = 4, 1
+C2, C3 = 144, 64
 
 
 def iota(shape, dim):
@@ -69,12 +71,12 @@
         to_left[q * N : q * N + N, :] = jnp.where(low, even, roll(odd, 64, 1))
 
 
-def pack_second(noise_in, source_in, biofilm_in, to_right, to_left, noise, source, biofilm, arrived):
+def pack_second(noise, source_in, biofilm_in, to_right, to_left, source, biofilm, arrived):
     def arrivals(g):
         rows = slice(16 * g, 16 * g + 16)
         return [
             pltpu.make_async_copy(far.at[:, rows, :], near.at[:, rows, :], arrived.at[k, g])
-            for k, (far, near) in enumerate(((noise_in, noise), (source_in, source), (biofilm_in, biofilm)))
+            for k, (far, near) in enumerate(((source_in, source), (biofilm_in, biofilm)))
         ]
 
     for g in range(8):
@@ -83,8 +85,11 @@
 
     lane = iota((16, N), 1)
     slot = lane % 8
-    group = lane // 8
     low = lane < 64
+    outer = (lane < 32) | (lane >= 96)
+
+    def six(k):
+        return ((lane - (8 * k + 5)) & 127) < 6
 
     third_right = jnp.zeros((16, N), F32)
     third_left = jnp.zeros((16, N), F32)
@@ -92,32 +97,29 @@
         for copy in arrivals(g):
             copy.wait()
         rows = slice(16 * g, 16 * g + 16)
-        zero = jnp.zeros((16, N), F32)
-        nr, sr, nl, sl = zero, zero, zero, zero
-        br = jnp.zeros((16, N), jnp.int32)
-        bl = br
-        for q in range(8):
-            even = noise[2 * q, rows, :]
-            odd = noise[2 * q + 1, rows, :]
-            if q >= 4:
-                first = (q - 4) * N + 16 * g
-                to_right[first : first + 16, :] = jnp.where(low, roll(even, 64, 1), odd)
-                to_left[first : first + 16, :] = jnp.where(low, even, roll(odd, 64, 1))
-            for z, n in ((2 * q, even), (2 * q + 1, odd)):
-                here = group == z
-                s = source[z, rows, :]
-                b = biofilm[z, rows, :]
-                nr = jnp.where(here, roll(n, 8 * z - 61, 1), nr)
-                nl = jnp.where(here, roll(n, 8 * z + 5 - 64, 1), nl)
-                sr = jnp.where(here, roll(s, 8 * z + 8, 1), sr)
-                sl = jnp.where(here, roll(s, 8 * z, 1), sl)
-                br = jnp.where(here, roll(b, 8 * z + 8, 1), br)
-                bl = jnp.where(here, roll(b, 8 * z, 1), bl)
-        br = br.astype(F32)
-        bl = bl.astype(F32)
+        sources = jnp.zeros((16, N), F32)
+        noises = jnp.zeros((16, N), F32)
+        levels = jnp.zeros((16, N), jnp.int32)
+        for z in range(16):
+            n = noise[z, rows, :]
+            both = roll(jnp.where(outer, source[z, rows, :], n), 8 * z + 8, 1)
+            sources = jnp.where(six(z), both, sources)
+            noises = jnp.where(six((z + 8) % 16), both, noises)
+            levels = jnp.where(six(z), roll(biofilm[z, rows, :], 8 * z + 8, 1), levels)
+            if z >= 8 and z % 2 == 1:
+                even = noise[z - 1, rows, :]
+                first = (z - 9) // 2 * N + 16 * g
+                to_right[first : first + 16, :] = jnp.where(low, roll(even, 64, 1), n)
+                to_left[first : first + 16, :] = jnp.where(low, even, roll(n, 64, 1))
+        br = levels.astype(F32)
+        bl = roll(br, -8, 1)
         first = 4 * N + 16 * g
-        to_right[first : first + 16, :] = jnp.where(slot < 3, nr, jnp.where(slot < 5, roll(br, -3, 1), sr))
-        to_left[first : first + 16, :] = jnp.where(slot < 3, sl, jnp.where(slot < 5, roll(bl, 3, 1), nl))
+        to_right[first : first + 16, :] = jnp.where(
+            slot < 3, roll(noises, -69, 1), jnp.where(slot < 5, roll(br, -3, 1), sources)
+        )
+        to_left[first : first + 16, :] = jnp.where(
+            slot < 3, roll(sources, -8, 1), jnp.where(slot < 5, roll(bl, 3, 1), roll(noises, -67, 1))
+        )
         third_right = third_right + roll(jnp.where(slot == 5, br, 0.0), g, 1)
         third_left = third_left + roll(jnp.where(slot == 2, bl, 0.0), g, 1)
     to_right[5 * N :, :] = third_right
@@ -167,7 +169,19 @@
     return dot(high, w) + dot(low, w)
 
 
-def half_columns(first_layer, own_middle, from_left, from_right, middle, to_down, to_up):
+def on_even():
+    return lax.axis_index("gx") % 2 == 0
+
+
+class Chosen:
+    def __init__(self, first, a, b):
+        self.first, self.a, self.b = first, a, b
+
+    def __getitem__(self, index):
+        return jnp.where(self.first, self.a[index], self.b[index])
+
+
+def half_columns(first_layer, own_middle, from_left, from_right, middle):
     _, left, right, _, _ = column_weights()
     both = jnp.concatenate([left, right], axis=0)
     total = jnp.zeros((N, N), F32)
@@ -177,31 +191,43 @@
         total = total + roll(halo[:, 2 * N :], 8 * first_layer + 16 * q, 1)
         for k in (0, 1):
             z = 2 * q + k
-            field = own_middle[first_layer + z] + halo[:, k * N : k * N + N]
-            middle[z] = field
-            to_down[z * 72 : z * 72 + 72, :] = field[56:, :]
-            to_up[z * 72 : z * 72 + 72, :] = field[:72, :]
+            middle[z] = own_middle[first_layer + z] + halo[:, k * N : k * N + N]
     return total
 
 
-def outer_rows(to_down, to_up, z, tail, s, b):
-    to_down[z * 72 : z * 72 + 3, :] = s[125:128, :]
-    to_down[z * 72 + 3 : z * 72 + 5, :] = b[126:128, :].astype(F32)
-    to_down[tail + z : tail + z + 1, :] = b[125:126, :].astype(F32)
-    to_up[z * 72 + 67 : z * 72 + 70, :] = s[0:3, :]
-    to_up[z * 72 + 70 : z * 72 + 72, :] = b[0:2, :].astype(F32)
-    to_up[tail + z : tail + z + 1, :] = b[2:3, :].astype(F32)
-
-
-def columns_first(own_middle, source, biofilm, from_left, from_right, middle, edge, to_down, to_up):
-    edge[...] = half_columns(0, own_middle, from_left, from_right, middle, to_down, to_up)
-    for z in range(8):
-        outer_rows(to_down, to_up, z, 8 * 72, source.at[z], biofilm.at[z])
+def fill_messages(sums, sources, levels, tail, outer, inner):
+    def fill(to_down, to_up):
+        for z in range(len(sums)):
+            to_down[z * 72 : z * 72 + 72, :] = sums[z][56:128, :]
+            to_up[z * 72 : z * 72 + 72, :] = sums[z][0:72, :]
+        for z, (s, b) in enumerate(zip(sources, levels)):
+            to_down[z * 72 : z * 72 + 3, :] = s[125:128, :]
+            to_down[z * 72 + 3 : z * 72 + 5, :] = b[126:128, :].astype(F32)
+            to_down[tail + z : tail + z + 1, :] = b[125:126, :].astype(F32)
+            to_up[z * 72 + 67 : z * 72 + 70, :] = s[0:3, :]
+            to_up[z * 72 + 70 : z * 72 + 72, :] = b[0:2, :].astype(F32)
+            to_up[tail + z : tail + z + 1, :] = b[2:3, :].astype(F32)
+
+    even = on_even()
+
+    @pl.when(even)
+    def _():
+        fill(inner, outer)
+
+    @pl.when(jnp.logical_not(even))
+    def _():
+        fill(outer, inner)
+
+
+def columns_first(own_middle, source, biofilm, from_left, from_right, middle, edge, outer, inner):
+    edge[...] = half_columns(0, own_middle, from_left, from_right, middle)
+    planes = [[ref.at[z] for z in range(8)] for ref in (middle, source, biofilm)]
+    fill_messages(*planes, 8 * 72, outer, inner)
 
 
 def columns_second(
     own_middle, own_edge, first_edge, source, biofilm, from_left, from_right,
-    middle, edge, edge_source, edge_biofilm, to_down, to_up,
+    middle, edge, edge_source, edge_biofilm, outer, inner,
 ):
     _, _, _, left_extra, right_extra = column_weights()
     slot = iota((N, N), 1) % 8
@@ -209,10 +235,7 @@
     extra_right = from_right[4 * N : 5 * N, :]
     total = own_edge[...] + first_edge[...]
     total = total + sums_beside(extra_left, extra_right, jnp.concatenate([left_extra, right_extra], axis=0))
-    total = total + half_columns(8, own_middle, from_left, from_right, middle, to_down, to_up)
-    edge[...] = total
-    to_down[8 * 72 : 9 * 72, :] = total[56:, :]
-    to_up[8 * 72 : 9 * 72, :] = total[:72, :]
+    edge[...] = total + half_columns(8, own_middle, from_left, from_right, middle)
 
     edge_source[...] = jnp.where(slot >= 5, extra_left, jnp.where(slot <= 2, extra_right, 0.0))
     third_left = from_left[5 * N :, :]
@@ -225,11 +248,17 @@
             slot16 == 5, roll(third_left, -g, 1), jnp.where(slot16 == 2, roll(third_right, -g, 1), levels[rows, :])
         )
 
-    to_down[9 * 72 :, :] = jnp.zeros((16, N), F32)
-    to_up[9 * 72 :, :] = jnp.zeros((16, N), F32)
-    for z in range(8):
-        outer_rows(to_down, to_up, z, 9 * 72, source.at[8 + z], biofilm.at[8 + z])
-    outer_rows(to_down, to_up, 8, 9 * 72, edge_source, edge_biofilm)
+    outer[9 * 72 :, :] = jnp.zeros((16, N), F32)
+    inner[9 * 72 :, :] = jnp.zeros((16, N), F32)
+    planes = [[ref.at[8 + z] for z in range(8)] for ref in (source, biofilm)]
+    fill_messages(
+        [middle.at[z] for z in range(8)] + [edge],
+        planes[0] + [edge_source],
+        planes[1] + [edge_biofilm],
+        9 * 72,
+        outer,
+        inner,
+    )
 
 
 def row_weights():
@@ -268,16 +297,16 @@
     return jnp.max(jnp.where(real, total, -HUGE).reshape(18, 8, N), axis=0)
 
 
-def rows_first(middle, from_up, from_down, logperm, largest):
+def rows_first(middle, outer, inner, logperm, largest):
+    even = on_even()
+    from_up, from_down = Chosen(even, outer, inner), Chosen(even, inner, outer)
     own, halo = row_weights()
     most = jnp.full((8, N), -HUGE, F32)
     for z in range(0, 8, 2):
-        inner = row_sums(own, middle[z], middle[z + 1])
-        outer = row_sums(halo, *[halo_rows(from_up, from_down, z + i) for i in (0, 1)])
+        near = row_sums(own, middle[z], middle[z + 1])
+        far = row_sums(halo, *[halo_rows(from_up, from_down, z + i) for i in (0, 1)])
         for i in (0, 1):
-            most = jnp.maximum(
-                most, finish_sums(from_up, from_down, z + i, inner[i] + outer[i], logperm.at[z + i])
-            )
+            most = jnp.maximum(most, finish_sums(from_up, from_down, z + i, near[i] + far[i], logperm.at[z + i]))
     largest[...] = most
 
 
@@ -304,18 +333,22 @@
     return guess * (2.0 - x * guess)
 
 
-WIDE = ((8, 48), (56, 48), (104, 48))
-OWN_ROWS = ((16, 64), (80, 64))
+WIDE = tuple((start, C2) for start in range(8, 152, C2))
+OWN_ROWS = tuple((start, C3) for start in range(16, 144, C3))
 
 
 def operate_powers(
-    logperm1, largest1, partial, factor, edge_factor, edge_source, source, from_up1, from_down1, from_up2, from_down2,
+    logperm1, largest1, partial, factor, edge_factor, edge_source, source, outer1, inner1, outer2, inner2,
     power1, power2, power3, table,
     resist, across_x, across_y, across_z, flow, field0, field1, field2, field3, logperm2, plane_resist, plane_field,
     side_resist, side_x, side_y, side_z, side0, side1, side2, side_flux, done,
 ):
     lane = iota((8, N), 1)
     row8 = iota((8, N), 0)
+
+    even = on_even()
+    from_up1, from_down1 = Chosen(even, outer1, inner1), Chosen(even, inner1, outer1)
+    from_up2, from_down2 = Chosen(even, outer2, inner2), Chosen(even, inner2, outer2)
 
     _, halo = row_weights()
     edge_lane = (iota((144, N), 1) % 8 <= 2) | (iota((144, N), 1) % 8 >= 5)
@@ -465,30 +498,36 @@
 
         lax.fori_loop(0, 16, layer, 0, unroll=U1)
 
-    def apply_rows(field, z, start, size):
+    def apply_layers(field, first, count, start, size):
         rows = slice(start, start + size)
         lanes = iota((size, N), 1)
-        here = field[z, rows, :]
-        inward = flow[z, rows, :]
-        value = inward - roll(inward, -1, 1)
-        beside = roll(side_flux[z // 8, rows, :], 115 - 16 * (z % 8), 1)
-        value = value + jnp.where((lanes == 0) | (lanes == 127), beside, 0.0)
-        value = value + across_x[z, rows, :] * (here - field[z, start - 1 : start - 1 + size, :])
-        value = value - across_x[z, start + 1 : start + 1 + size, :] * (
-            field[z, start + 1 : start + 1 + size, :] - here
-        )
-        value = value + across_z[z, rows, :] * (here - field[jnp.maximum(z - 1, 0), rows, :])
-        return value - across_z[z + 1, rows, :] * (field[jnp.minimum(z + 1, 15), rows, :] - here)
+        ends = (lanes == 0) | (lanes == 127)
+        here = field[first, rows, :]
+        from_last = across_z[first, rows, :] * (here - field[jnp.maximum(first - 1, 0), rows, :])
+        for k in range(count):
+            z = first + k
+            after = field[jnp.minimum(z + 1, 15) if k == count - 1 else z + 1, rows, :]
+            to_next = across_z[z + 1, rows, :] * (after - here)
+            inward = flow[z, rows, :]
+            beside = roll(side_flux[z // 8, rows, :], 115 - 16 * (z % 8), 1)
+            value = inward - roll(inward, -1, 1) + jnp.where(ends, beside, 0.0)
+            value = value + across_x[z, rows, :] * (here - field[z, start - 1 : start - 1 + size, :])
+            value = value - across_x[z, start + 1 : start + 1 + size, :] * (
+                field[z, start + 1 : start + 1 + size, :] - here
+            )
+            yield z, here, value + from_last - to_next
+            here, from_last = after, to_next
 
     def apply(field, image):
         flow_along_y(field)
 
-        def layer(z, carry):
+        def layers(k, carry):
             for start, size in WIDE:
-                image[z, start : start + size, :] = apply_rows(field, z, start, size)
+                for z, _, value in apply_layers(field, k * U2, U2, start, size):
+                    image[z, start : start + size, :] = value
             return carry
 
-        lax.fori_loop(0, 16, layer, 0, unroll=U2)
+        lax.fori_loop(0, 16 // U2, layers, 0, unroll=V2)
 
     def hand_out(field, power, k):
         return pltpu.make_async_copy(field.at[:, 16:144, :], power, done.at[k])
@@ -502,20 +541,20 @@
     apply_sides(side2, None)
     flow_along_y(field2)
 
-    def last(z, sums):
+    def last(k, sums):
         for start, size in OWN_ROWS:
             rows = slice(start, start + size)
-            f3 = apply_rows(field2, z, start, size)
-            field3[z, start - 16 : start - 16 + size, :] = f3
-            f0 = field0[z, rows, :]
-            f1 = field1[z, rows, :]
-            f2 = field2[z, rows, :]
-            terms = (f0 * f0, f0 * f1, f1 * f1, f1 * f2, f2 * f2, f2 * f3)
-            sums = tuple(s + jnp.sum(t.reshape(size // 8, 8, N), axis=0) for s, t in zip(sums, terms))
-        pltpu.make_async_copy(field3.at[z], power3.at[z], done.at[2]).start()
+            for z, f2, f3 in apply_layers(field2, k * U3, U3, start, size):
+                field3[z, start - 16 : start - 16 + size, :] = f3
+                f0 = field0[z, rows, :]
+                f1 = field1[z, rows, :]
+                terms = (f0 * f0, f0 * f1, f1 * f1, f1 * f2, f2 * f2, f2 * f3)
+                sums = tuple(s + jnp.sum(t.reshape(size // 8, 8, N), axis=0) for s, t in zip(sums, terms))
+        part = pl.ds(k * U3, U3)
+        pltpu.make_async_copy(field3.at[part], power3.at[part], done.at[2]).start()
         return sums
 
-    sums = lax.fori_loop(0, 16, last, tuple(jnp.zeros((8, N), F32) for _ in range(6)), unroll=U3)
+    sums = lax.fori_loop(0, 16 // U3, last, tuple(jnp.zeros((8, N), F32) for _ in range(6)), unroll=V3)
     line = jnp.where((lane[:1] >= 8) & (lane[:1] < 16), top, 0.0)
     for k, s in enumerate(sums):
         amount = jnp.sum(jnp.sum(s, axis=0, keepdims=True), axis=1, keepdims=True)
@@ -647,6 +686,12 @@
     return lax.ppermute(to_next, axis, forward), lax.ppermute(to_previous, axis, backward)
 
 
+def exchange_pairs(outer, inner, axis):
+    count = lax.axis_size(axis)
+    across = [(i, (i + 1 if i % 2 else i - 1) % count) for i in range(count)]
+    return lax.ppermute(outer, axis, across), lax.ppermute(inner, axis, [(i, i ^ 1) for i in range(count)])
+
+
 def local(noise, biofilm, source):
     block = pltpu.VMEM((NZ, N, N), F32)
     to_right, to_left = call(
@@ -660,13 +705,13 @@
     beside1 = exchange(to_right, to_left, "gy")
     to_right, to_left = call(
         pack_second,
-        hbm(3),
+        vmem(1) + hbm(2),
         [shape(Y_ROWS[1], N)] * 2,
         vmem(2),
-        [block, block, pltpu.VMEM((NZ, N, N), jnp.int32), pltpu.SemaphoreType.DMA((3, 8))],
+        [block, pltpu.VMEM((NZ, N, N), jnp.int32), pltpu.SemaphoreType.DMA((2, 8))],
         name="pack_second",
         cost=2e10,
-    )(in_hbm(noise), in_hbm(source), in_hbm(biofilm))
+    )(noise, in_hbm(source), in_hbm(biofilm))
     beside2 = exchange(to_right, to_left, "gy")
     own_middle, own_edge, factor = call(
         column_sums_own,
@@ -676,15 +721,15 @@
         name="columns_own",
         cost=2e10,
     )(noise, biofilm)
-    middle1, first_edge, to_down, to_up = call(
+    middle1, first_edge, outer, inner = call(
         columns_first,
         vmem(5),
         [shape(8, N, N), shape(N, N)] + [shape(X_ROWS[0], N)] * 2,
         vmem(4),
         name="columns_first",
     )(own_middle, source, biofilm, *beside1)
-    above_below1 = exchange(to_down, to_up, "gx")
-    middle2, edge, edge_source, edge_biofilm, to_down, to_up = call(
+    above_below1 = exchange_pairs(outer, inner, "gx")
+    middle2, edge, edge_source, edge_biofilm, outer, inner = call(
         columns_second,
         vmem(7),
         [shape(8, N, N), shape(N, N), shape(N, N), shape(N, N)] + [shape(X_ROWS[1], N)] * 2,
@@ -692,7 +737,7 @@
         name="columns_second",
         cost=2e10,
     )(own_middle, own_edge, first_edge, source, biofilm, *beside2)
-    above_below2 = exchange(to_down, to_up, "gx")
+    above_below2 = exchange_pairs(outer, inner, "gx")
     partial, edge_factor = call(
         row_sums_own,
         vmem(3),

time: 74.4 us -> 71.9 us (0.966)
  waiting for transfers between devices: 12.7 us -> 10 us
  starting transfers between devices: 19.5 us -> 21.9 us
  Pallas kernels: 19.7 us -> 17.4 us
    ppermute x0 -> x4, starting transfers between devices: none -> 10.8 us  [the longest x2 8.29 us: exchange_pairs(): lax.ppermute(outer, axis, across)]
    ppermute x4 -> x2, waiting for transfers between devices: 10.6 us -> 0.01 us  [exchange(): lax.ppermute(to_previous, axis, backward)]
    ppermute x0 -> x4, waiting for transfers between devices: none -> 9.92 us  [the longest x2 9.91 us: exchange_pairs(): lax.ppermute(outer, axis, across)]
    ppermute x4 -> x2, starting transfers between devices: 10.9 us -> 2.63 us  [exchange(): lax.ppermute(to_next, axis, forward)]
    ppermute x4 -> x2, waiting for transfers between devices: 2.03 us -> 0.07 us  [exchange(): lax.ppermute(to_next, axis, forward)]
    pallas_call x1, Pallas kernels: 8.78 us -> 6.92 us  [local(): call(operate_powers, vmem(11), [pltpu.HBM((NZ, N, N), F32)] * 3 + [shape(...]
    ppermute x4 -> x2, starting transfers between devices: 8.53 us -> 8.52 us  [exchange(): lax.ppermute(to_previous, axis, backward)]
  transfers between devices with their start and end apart: 8 -> 8, of which waited for: 4 -> 3; matrix products, arithmetic and copies ran while one was open for 0% -> 0% of each run, Pallas kernels for 9% -> 8%
where the time goes in v4:
time: 71.9 us; the launch traced here: 71.7 us
  starting transfers between devices  21.9 us (30%)
  blocking collectives  21.5 us (30%)
  Pallas kernels  17.4 us (24%)
  waiting for transfers between devices  10 us (14%)
  between operations  0.9 us (1%)
    all_to_all x1, blocking collectives, local(): everyone = lax.all_to_all(table, ('gx', 'gy'), 0, 0, tiled=True)  21.5 us
    ppermute x2, waiting for transfers between devices, exchange_pairs(): lax.ppermute(outer, axis, across)  9.91 us
    ppermute x2, starting transfers between devices, exchange(): lax.ppermute(to_previous, axis, backward)  8.52 us
    ppermute x2, starting transfers between devices, exchange_pairs(): lax.ppermute(outer, axis, across)  8.29 us
    pallas_call x1, Pallas kernels, local(): call(operate_powers, vmem(11), [pltpu.HBM((NZ, N, N), F32)] * 3 + [shape(...  6.92 us
    pallas_call x1, Pallas kernels, local(): call(combine, vmem(2) + hbm(4), [pltpu.HBM((NZ, N, N), F32)] * 2, hbm(2),...  3.25 us
    pallas_call x1, Pallas kernels, local(): call(pack_second, vmem(1) + hbm(2), [shape(Y_ROWS[1], N)] * 2, vmem(2), [...  3.04 us
    ppermute x2, starting transfers between devices, exchange(): lax.ppermute(to_next, axis, forward)  2.63 us
  transfers between devices with their start and end apart: 8, of which 3 were waited for; matrix products, arithmetic and copies ran while one was open for 0% of the time, Pallas kernels for 8%

profile of v4, /device:TPU:1, one launch (start us, length us, event | category | flops | bytes accessed | tf_op | source)
XLA Modules:
  0.0 71.7 jit_solution(2485140195656239498)
XLA Ops:
  0.6 0.0 copy-start.2
  0.6 1.4 %pack_first.1 = (f32[512,128]{1,0:T(8,128)S(1)}, f32[512,128]{1,0:T(8,128)S(1)}) custom-call(f32[16,128,128]{2,1,0:T(8,128)} %noise.3), custom_call_target="tpu_custom_call" | custom-call | flops 1000000 | bytes 1000000 | tf_op jit(solution)/shard_map/pack_first/pallas_call | solution.py:697
  2.1 2.5 %collective-permute-start = (f32[512,128]{1,0:T(8,128)S(1)}, f32[512,128]{1,0:T(8,128)S(1)}, u32[]{:S(2)}, u32[]{:S(2)}) collective-permute-start(f32[512,128]{1,0:T(8,128)S(1)} %get-tuple-element.28), channel_id=1, source_target_pairs={{0,1},{1,2},{2,3},{3,4},{4,5},{5,6},{6,7},{7,8},{8,9},{9,10},{10,1... | collective-permute-start | bytes 786440 | tf_op jit(solution)/shard_map/ppermute | solution.py:686
  4.6 0.0 copy-start.1
  4.6 5.0 %collective-permute-start.1 = (f32[512,128]{1,0:T(8,128)S(1)}, f32[512,128]{1,0:T(8,128)S(1)}, u32[]{:S(2)}, u32[]{:S(2)}) collective-permute-start(f32[512,128]{1,0:T(8,128)S(1)} %get-tuple-element.29), channel_id=1, source_target_pairs={{1,0},{2,1},{3,2},{4,3},{5,4},{6,5},{7,6},{8,7},{9,8},{10,9},{11,1... | collective-permute-start | bytes 786440 | tf_op jit(solution)/shard_map/ppermute | solution.py:686
  9.6 0.0 copy-done.2
  9.6 3.0 %pack_second.1 = (f32[656,128]{1,0:T(8,128)S(1)}, f32[656,128]{1,0:T(8,128)S(1)}) custom-call(f32[16,128,128]{2,1,0:T(8,128)S(1)} %copy-done.2, f32[16,128,128]{2,1,0:T(8,128)} %source_in.3, s32[16,128,128]{2,1,0:T(8,128)} %biofilm.5), custom_call_target="tpu_custom_call" | custom-call | flops 20000000000 | bytes 20000000000 | tf_op jit(solution)/shard_map/pack_second/pallas_call | solution.py:706
  12.6 0.1 collective-permute-start.4
  12.7 0.0 copy-start
  12.7 3.6 %collective-permute-start.5 = (f32[656,128]{1,0:T(8,128)S(1)}, f32[656,128]{1,0:T(8,128)S(1)}, u32[]{:S(2)}, u32[]{:S(2)}) collective-permute-start(f32[656,128]{1,0:T(8,128)S(1)} %get-tuple-element.38), channel_id=1, source_target_pairs={{1,0},{2,1},{3,2},{4,3},{5,4},{6,5},{7,6},{8,7},{9,8},{10,9},{11,1... | collective-permute-start | bytes 1007624 | tf_op jit(solution)/shard_map/ppermute | solution.py:686
  16.3 0.0 copy-done.1
  16.3 0.9 %columns_own.1 = (f32[16,128,128]{2,1,0:T(8,128)S(1)}, f32[128,128]{1,0:T(8,128)S(1)}, f32[16,128,128]{2,1,0:T(8,128)S(1)}) custom-call(f32[16,128,128]{2,1,0:T(8,128)S(1)} %copy-done.2, s32[16,128,128]{2,1,0:T(8,128)S(1)} %copy-done.1), custom_call_target="tpu_custom_call" | custom-call | flops 20000000000 | bytes 20000000000 | tf_op jit(solution)/shard_map/columns_own/pallas_call | solution.py:716
  17.2 0.0 collective-permute-done.from_left
  17.2 0.0 collective-permute-done.1.from_right
  17.2 0.0 copy-done
  17.2 0.6 columns_first.1
  17.8 3.9 %collective-permute-start.2 = (f32[584,128]{1,0:T(8,128)S(1)}, f32[584,128]{1,0:T(8,128)S(1)}, u32[]{:S(2)}, u32[]{:S(2)}) collective-permute-start(f32[584,128]{1,0:T(8,128)S(1)} %get-tuple-element.31), channel_id=1, source_target_pairs={{0,240},{16,32},{32,16},{48,64},{64,48},{80,96},{96,80},{112,128},... | collective-permute-start | bytes 897032 | tf_op jit(solution)/shard_map/ppermute | solution.py:692
  21.7 1.5 %collective-permute-start.3 = (f32[584,128]{1,0:T(8,128)S(1)}, f32[584,128]{1,0:T(8,128)S(1)}, u32[]{:S(2)}, u32[]{:S(2)}) collective-permute-start(f32[584,128]{1,0:T(8,128)S(1)} %get-tuple-element.32), channel_id=1, source_target_pairs={{0,16},{16,0},{32,48},{48,32},{64,80},{80,64},{96,112},{112,96},{1... | collective-permute-start | bytes 897032 | tf_op jit(solution)/shard_map/ppermute | solution.py:692
  23.2 0.1 collective-permute-done.4.from_left
  23.3 0.0 collective-permute-done.5.from_right
  23.3 0.6 columns_second.1
  23.9 4.4 %collective-permute-start.6 = (f32[664,128]{1,0:T(8,128)S(1)}, f32[664,128]{1,0:T(8,128)S(1)}, u32[]{:S(2)}, u32[]{:S(2)}) collective-permute-start(f32[664,128]{1,0:T(8,128)S(1)} %get-tuple-element.46), channel_id=1, source_target_pairs={{0,240},{16,32},{32,16},{48,64},{64,48},{80,96},{96,80},{112,128},... | collective-permute-start | bytes 1019912 | tf_op jit(solution)/shard_map/ppermute | solution.py:692
  28.3 1.0 %collective-permute-start.7 = (f32[664,128]{1,0:T(8,128)S(1)}, f32[664,128]{1,0:T(8,128)S(1)}, u32[]{:S(2)}, u32[]{:S(2)}) collective-permute-start(f32[664,128]{1,0:T(8,128)S(1)} %get-tuple-element.47), channel_id=1, source_target_pairs={{0,16},{16,0},{32,48},{48,32},{64,80},{80,64},{96,112},{112,96},{1... | collective-permute-start | bytes 1019912 | tf_op jit(solution)/shard_map/ppermute | solution.py:692
  29.3 0.3 rows_own.1
  29.6 3.0 %collective-permute-done.2.outer.outer1 = f32[584,128]{1,0:T(8,128)S(1)} collective-permute-done((f32[584,128]{1,0:T(8,128)S(1)}, f32[584,128]{1,0:T(8,128)S(1)}, u32[]{:S(2)}, u32[]{:S(2)}) %collective-permute-start.2) | collective-permute-done | bytes 299040 | tf_op jit(solution)/shard_map/ppermute | solution.py:692
  32.6 0.0 collective-permute-done.3.inner.inner1
  32.6 0.4 rows_first.1
  32.9 6.9 %collective-permute-done.6.outer2 = f32[664,128]{1,0:T(8,128)S(1)} collective-permute-done((f32[664,128]{1,0:T(8,128)S(1)}, f32[664,128]{1,0:T(8,128)S(1)}, u32[]{:S(2)}, u32[]{:S(2)}) %collective-permute-start.6) | collective-permute-done | bytes 340000 | tf_op jit(solution)/shard_map/ppermute | solution.py:692
  39.9 0.0 collective-permute-done.7.inner2
  39.9 6.9 %powers.1 = (f32[16,128,128]{2,1,0:T(8,128)}, f32[16,128,128]{2,1,0:T(8,128)}, f32[16,128,128]{2,1,0:T(8,128)}, f32[256,128]{1,0:T(8,128)S(1)}) custom-call(f32[8,144,128]{2,1,0:T(8,128)S(1)} %get-tuple-element.33.logperm1, f32[8,128]{1,0:T(8,128)S(1)} %get-tuple-element.34.largest1, f32[9,144,128]{2,1,0:T(8,128)S(1)} %get-tuple-element.42.partial, ...), custom_call_target="tpu_custom_call" | custom-call | flops 1000000 | bytes 1000000 | tf_op jit(solution)/shard_map/powers/pallas_call | solution.py:761
  46.8 21.5 %all_to_all.11 = f32[256,1,128]{2,1,0:T(1,128)S(1)} all-to-all(f32[256,1,128]{2,1,0:T(1,128)S(1)} %bitcast.4), channel_id=1, replica_groups=mesh['gx'=16,'gy'=16] {'gx','gy'}, dimensions={0} | all-to-all | bytes 262144 | tf_op jit(solution)/shard_map/all_to_all | solution.py:774
  68.3 3.3 %combine.1 = (f32[16,128,128]{2,1,0:T(8,128)}, f32[16,128,128]{2,1,0:T(8,128)}) custom-call(f32[256,128]{1,0:T(8,128)S(1)} %bitcast.5, f32[256,128]{1,0:T(8,128)S(1)} %get-tuple-element.48.own, f32[16,128,128]{2,1,0:T(8,128)} %source_in.3, f32[16,128,128]{2,1,0:T(8,128)} %get-tuple-element.49.power1_in, f32[16,128,128]{2,1,0:T(8,128)} %get-tuple-element.50.power2_in, ...), custom_call_target="tpu_custom_call" | custom-call | flops 1000000 | bytes 1000000 | tf_op jit(solution)/shard_map/combine/pallas_call | solution.py:776
Async XLA Ops:
  0.6 9.0 %copy-start.2 = (f32[16,128,128]{2,1,0:T(8,128)S(1)}, f32[16,128,128]{2,1,0:T(8,128)}, u32[]{:S(2)}) copy-start(f32[16,128,128]{2,1,0:T(8,128)} %noise.3) | copy-start | bytes 3145732
  2.1 15.1 %collective-permute-start = (f32[512,128]{1,0:T(8,128)S(1)}, f32[512,128]{1,0:T(8,128)S(1)}, u32[]{:S(2)}, u32[]{:S(2)}) collective-permute-start(f32[512,128]{1,0:T(8,128)S(1)} %get-tuple-element.28), channel_id=1, source_target_pairs={{0,1},{1,2},{2,3},{3,4},{4,5},{5,6},{6,7},{7,8},{8,9},{9,10},{10,1... | collective-permute-start | bytes 786440 | tf_op jit(solution)/shard_map/ppermute | solution.py:686
  4.6 11.7 %copy-start.1 = (s32[16,128,128]{2,1,0:T(8,128)S(1)}, s32[16,128,128]{2,1,0:T(8,128)}, u32[]{:S(2)}) copy-start(s32[16,128,128]{2,1,0:T(8,128)} %biofilm.5) | copy-start | bytes 3145732
  4.6 12.6 %collective-permute-start.1 = (f32[512,128]{1,0:T(8,128)S(1)}, f32[512,128]{1,0:T(8,128)S(1)}, u32[]{:S(2)}, u32[]{:S(2)}) collective-permute-start(f32[512,128]{1,0:T(8,128)S(1)} %get-tuple-element.29), channel_id=1, source_target_pairs={{1,0},{2,1},{3,2},{4,3},{5,4},{6,5},{7,6},{8,7},{9,8},{10,9},{11,1... | collective-permute-start | bytes 786440 | tf_op jit(solution)/shard_map/ppermute | solution.py:686
  12.6 10.6 %collective-permute-start.4 = (f32[656,128]{1,0:T(8,128)S(1)}, f32[656,128]{1,0:T(8,128)S(1)}, u32[]{:S(2)}, u32[]{:S(2)}) collective-permute-start(f32[656,128]{1,0:T(8,128)S(1)} %get-tuple-element.37), channel_id=1, source_target_pairs={{0,1},{1,2},{2,3},{3,4},{4,5},{5,6},{6,7},{7,8},{8,9},{9,10},{10,1... | collective-permute-start | bytes 1007624 | tf_op jit(solution)/shard_map/ppermute | solution.py:686
  12.7 4.5 %copy-start = (f32[16,128,128]{2,1,0:T(8,128)S(1)}, f32[16,128,128]{2,1,0:T(8,128)}, u32[]{:S(2)}) copy-start(f32[16,128,128]{2,1,0:T(8,128)} %source_in.3) | copy-start | bytes 3145732
  12.7 10.5 %collective-permute-start.5 = (f32[656,128]{1,0:T(8,128)S(1)}, f32[656,128]{1,0:T(8,128)S(1)}, u32[]{:S(2)}, u32[]{:S(2)}) collective-permute-start(f32[656,128]{1,0:T(8,128)S(1)} %get-tuple-element.38), channel_id=1, source_target_pairs={{1,0},{2,1},{3,2},{4,3},{5,4},{6,5},{7,6},{8,7},{9,8},{10,9},{11,1... | collective-permute-start | bytes 1007624 | tf_op jit(solution)/shard_map/ppermute | solution.py:686
  17.8 14.8 %collective-permute-start.2 = (f32[584,128]{1,0:T(8,128)S(1)}, f32[584,128]{1,0:T(8,128)S(1)}, u32[]{:S(2)}, u32[]{:S(2)}) collective-permute-start(f32[584,128]{1,0:T(8,128)S(1)} %get-tuple-element.31), channel_id=1, source_target_pairs={{0,240},{16,32},{32,16},{48,64},{64,48},{80,96},{96,80},{112,128},... | collective-permute-start | bytes 897032 | tf_op jit(solution)/shard_map/ppermute | solution.py:692
  21.7 10.9 %collective-permute-start.3 = (f32[584,128]{1,0:T(8,128)S(1)}, f32[584,128]{1,0:T(8,128)S(1)}, u32[]{:S(2)}, u32[]{:S(2)}) collective-permute-start(f32[584,128]{1,0:T(8,128)S(1)} %get-tuple-element.32), channel_id=1, source_target_pairs={{0,16},{16,0},{32,48},{48,32},{64,80},{80,64},{96,112},{112,96},{1... | collective-permute-start | bytes 897032 | tf_op jit(solution)/shard_map/ppermute | solution.py:692
  23.9 15.9 %collective-permute-start.6 = (f32[664,128]{1,0:T(8,128)S(1)}, f32[664,128]{1,0:T(8,128)S(1)}, u32[]{:S(2)}, u32[]{:S(2)}) collective-permute-start(f32[664,128]{1,0:T(8,128)S(1)} %get-tuple-element.46), channel_id=1, source_target_pairs={{0,240},{16,32},{32,16},{48,64},{64,48},{80,96},{96,80},{112,128},... | collective-permute-start | bytes 1019912 | tf_op jit(solution)/shard_map/ppermute | solution.py:692
  28.3 11.6 %collective-permute-start.7 = (f32[664,128]{1,0:T(8,128)S(1)}, f32[664,128]{1,0:T(8,128)S(1)}, u32[]{:S(2)}, u32[]{:S(2)}) collective-permute-start(f32[664,128]{1,0:T(8,128)S(1)} %get-tuple-element.47), channel_id=1, source_target_pairs={{0,16},{16,0},{32,48},{48,32},{64,80},{80,64},{96,112},{112,96},{1... | collective-permute-start | bytes 1019912 | tf_op jit(solution)/shard_map/ppermute | solution.py:692

commit v5 on v4

--- a/solution.py
+++ b/solution.py
@@ -12,12 +12,15 @@
 F32 = jnp.float32
 BF16 = jnp.bfloat16
 
-Y_ROWS = (4 * N, 4 * N + N + 16)
-X_ROWS = (8 * 72 + 8, 9 * 72 + 16)
+H = 10
+G = NZ - H
+Y_ROWS = (H // 2 * N, G // 2 * N + N + 16)
+X_TAIL = (H * 72, (G + 1) * 72)
+X_ROWS = (X_TAIL[0] + (H + 7) // 8 * 8, X_TAIL[1] + (G + 8) // 8 * 8)
 ROWS = 160
 OWN = 16
 HUGE = 1e30
-U1, U2, U3, U5, U6 = 16, 4, 4, 16, 8
+U1, U2, U3, U5 = 16, 4, 4, 16
 V2, V3 = 4, 1
 C2, C3 = 144, 64
 
@@ -59,11 +62,11 @@
     low = iota((N, N), 1) < 64
     copies = [
         pltpu.make_async_copy(noise_in.at[2 * q : 2 * q + 2], noise.at[2 * q : 2 * q + 2], arrived.at[q])
-        for q in range(4)
+        for q in range(H // 2)
     ]
     for copy in copies:
         copy.start()
-    for q in range(4):
+    for q in range(H // 2):
         copies[q].wait()
         even = noise[2 * q]
         odd = noise[2 * q + 1]
@@ -71,7 +74,7 @@
         to_left[q * N : q * N + N, :] = jnp.where(low, even, roll(odd, 64, 1))
 
 
-def pack_second(noise, source_in, biofilm_in, to_right, to_left, source, biofilm, arrived):
+def pack_second(after, noise, source_in, biofilm_in, to_right, to_left, source, biofilm, arrived):
     def arrivals(g):
         rows = slice(16 * g, 16 * g + 16)
         return [
@@ -79,6 +82,7 @@
             for k, (far, near) in enumerate(((source_in, source), (biofilm_in, biofilm)))
         ]
 
+    del after
     for g in range(8):
         for copy in arrivals(g):
             copy.start()
@@ -106,14 +110,14 @@
             sources = jnp.where(six(z), both, sources)
             noises = jnp.where(six((z + 8) % 16), both, noises)
             levels = jnp.where(six(z), roll(biofilm[z, rows, :], 8 * z + 8, 1), levels)
-            if z >= 8 and z % 2 == 1:
+            if z >= H and z % 2 == 1:
                 even = noise[z - 1, rows, :]
-                first = (z - 9) // 2 * N + 16 * g
+                first = (z - 1 - H) // 2 * N + 16 * g
                 to_right[first : first + 16, :] = jnp.where(low, roll(even, 64, 1), n)
                 to_left[first : first + 16, :] = jnp.where(low, even, roll(n, 64, 1))
         br = levels.astype(F32)
         bl = roll(br, -8, 1)
-        first = 4 * N + 16 * g
+        first = G // 2 * N + 16 * g
         to_right[first : first + 16, :] = jnp.where(
             slot < 3, roll(noises, -69, 1), jnp.where(slot < 5, roll(br, -3, 1), sources)
         )
@@ -122,8 +126,8 @@
         )
         third_right = third_right + roll(jnp.where(slot == 5, br, 0.0), g, 1)
         third_left = third_left + roll(jnp.where(slot == 2, bl, 0.0), g, 1)
-    to_right[5 * N :, :] = third_right
-    to_left[5 * N :, :] = third_left
+    to_right[G // 2 * N + N :, :] = third_right
+    to_left[G // 2 * N + N :, :] = third_left
 
 
 def column_weights():
@@ -181,11 +185,11 @@
         return jnp.where(self.first, self.a[index], self.b[index])
 
 
-def half_columns(first_layer, own_middle, from_left, from_right, middle):
+def part_columns(first_layer, count, own_middle, from_left, from_right, middle):
     _, left, right, _, _ = column_weights()
     both = jnp.concatenate([left, right], axis=0)
     total = jnp.zeros((N, N), F32)
-    for q in range(4):
+    for q in range(count // 2):
         rows = slice(q * N, q * N + N)
         halo = sums_beside(from_left[rows, :], from_right[rows, :], both)
         total = total + roll(halo[:, 2 * N :], 8 * first_layer + 16 * q, 1)
@@ -197,6 +201,8 @@
 
 def fill_messages(sums, sources, levels, tail, outer, inner):
     def fill(to_down, to_up):
+        for ref in (to_down, to_up):
+            ref[tail:, :] = jnp.zeros((ref.shape[0] - tail, N), F32)
         for z in range(len(sums)):
             to_down[z * 72 : z * 72 + 72, :] = sums[z][56:128, :]
             to_up[z * 72 : z * 72 + 72, :] = sums[z][0:72, :]
@@ -220,9 +226,9 @@
 
 
 def columns_first(own_middle, source, biofilm, from_left, from_right, middle, edge, outer, inner):
-    edge[...] = half_columns(0, own_middle, from_left, from_right, middle)
-    planes = [[ref.at[z] for z in range(8)] for ref in (middle, source, biofilm)]
-    fill_messages(*planes, 8 * 72, outer, inner)
+    edge[...] = part_columns(0, H, own_middle, from_left, from_right, middle)
+    planes = [[ref.at[z] for z in range(H)] for ref in (middle, source, biofilm)]
+    fill_messages(*planes, X_TAIL[0], outer, inner)
 
 
 def columns_second(
@@ -231,15 +237,16 @@
 ):
     _, _, _, left_extra, right_extra = column_weights()
     slot = iota((N, N), 1) % 8
-    extra_left = from_left[4 * N : 5 * N, :]
-    extra_right = from_right[4 * N : 5 * N, :]
+    first = G // 2 * N
+    extra_left = from_left[first : first + N, :]
+    extra_right = from_right[first : first + N, :]
     total = own_edge[...] + first_edge[...]
     total = total + sums_beside(extra_left, extra_right, jnp.concatenate([left_extra, right_extra], axis=0))
-    edge[...] = total + half_columns(8, own_middle, from_left, from_right, middle)
+    edge[...] = total + part_columns(H, G, own_middle, from_left, from_right, middle)
 
     edge_source[...] = jnp.where(slot >= 5, extra_left, jnp.where(slot <= 2, extra_right, 0.0))
-    third_left = from_left[5 * N :, :]
-    third_right = from_right[5 * N :, :]
+    third_left = from_left[first + N :, :]
+    third_right = from_right[first + N :, :]
     levels = jnp.where(slot >= 6, roll(extra_left, 3, 1), jnp.where(slot <= 1, roll(extra_right, -3, 1), 0.0))
     slot16 = iota((16, N), 1) % 8
     for g in range(8):
@@ -248,14 +255,12 @@
             slot16 == 5, roll(third_left, -g, 1), jnp.where(slot16 == 2, roll(third_right, -g, 1), levels[rows, :])
         )
 
-    outer[9 * 72 :, :] = jnp.zeros((16, N), F32)
-    inner[9 * 72 :, :] = jnp.zeros((16, N), F32)
-    planes = [[ref.at[8 + z] for z in range(8)] for ref in (source, biofilm)]
+    planes = [[ref.at[H + z] for z in range(G)] for ref in (source, biofilm)]
     fill_messages(
-        [middle.at[z] for z in range(8)] + [edge],
+        [middle.at[z] for z in range(G)] + [edge],
         planes[0] + [edge_source],
         planes[1] + [edge_biofilm],
-        9 * 72,
+        X_TAIL[1],
         outer,
         inner,
     )
@@ -302,7 +307,7 @@
     from_up, from_down = Chosen(even, outer, inner), Chosen(even, inner, outer)
     own, halo = row_weights()
     most = jnp.full((8, N), -HUGE, F32)
-    for z in range(0, 8, 2):
+    for z in range(0, H, 2):
         near = row_sums(own, middle[z], middle[z + 1])
         far = row_sums(halo, *[halo_rows(from_up, from_down, z + i) for i in (0, 1)])
         for i in (0, 1):
@@ -312,9 +317,9 @@
 
 def row_sums_own(middle, edge, edge_biofilm, partial, factor):
     own, _ = row_weights()
-    for z in range(0, 8, 2):
+    for z in range(0, G, 2):
         partial[z], partial[z + 1] = row_sums(own, middle[z], middle[z + 1])
-    partial[8] = row_sums(own, edge[...])[0]
+    partial[G] = row_sums(own, edge[...])[0]
     factor[...] = resistance_factor(edge_biofilm[...])
 
 
@@ -354,18 +359,18 @@
     edge_lane = (iota((144, N), 1) % 8 <= 2) | (iota((144, N), 1) % 8 >= 5)
     second = (from_up2, from_down2)
     largest = largest1[...]
-    for z in (0, 2, 4, 6):
+    for z in range(0, G, 2):
         pair = row_sums(halo, halo_rows(*second, z), halo_rows(*second, z + 1))
         for i in (0, 1):
             sums = partial[z + i] + pair[i]
             largest = jnp.maximum(largest, finish_sums(*second, z + i, sums, logperm2.at[z + i]))
-    sums = partial[8] + row_sums(halo, halo_rows(*second, 8))[0]
-    largest = jnp.maximum(largest, finish_sums(*second, 8, sums, logperm2.at[8], edge_lane))
+    sums = partial[G] + row_sums(halo, halo_rows(*second, G))[0]
+    largest = jnp.maximum(largest, finish_sums(*second, G, sums, logperm2.at[G], edge_lane))
     top = jnp.max(jnp.max(largest, axis=0, keepdims=True), axis=1, keepdims=True)
     top = jnp.maximum(top, -60.0)
 
-    def halo_tiles(half, z):
-        from_up, from_down, tail = half
+    def halo_tiles(part, z):
+        from_up, from_down, tail = part
         first = pl.multiple_of(z * 72, 8)
         above = from_up[pl.ds(first, 8), :]
         below = from_down[pl.ds(first + 64, 8), :]
@@ -377,11 +382,11 @@
         biofilm_below = jnp.where(row8 == 2, third_below, jnp.where(row8 <= 1, roll(below, 2, 0), 0.0))
         return source_above, source_below, biofilm_above, biofilm_below
 
-    first_half = (from_up1, from_down1, 8 * 72)
-    second_half = (from_up2, from_down2, 9 * 72)
-
-    def prepare(half, z, logperm, out, field, own_source, own_factor):
-        source_above, source_below, biofilm_above, biofilm_below = halo_tiles(half, z)
+    first_part = (from_up1, from_down1, X_TAIL[0])
+    second_part = (from_up2, from_down2, X_TAIL[1])
+
+    def prepare(part, z, logperm, out, field, own_source, own_factor):
+        source_above, source_below, biofilm_above, biofilm_below = halo_tiles(part, z)
         field[8:16, :] = source_above
         field[16:144, :] = own_source
         field[144:152, :] = source_below
@@ -395,19 +400,19 @@
         field[0:8, :] = none
         field[152:160, :] = none
 
-    prepare(second_half, 8, logperm2.at[8], plane_resist, plane_field, edge_source[...], edge_factor[...])
-    for base, half, logperm in ((0, first_half, logperm1), (8, second_half, logperm2)):
-
-        def prepare_layer(k, carry, base=base, half=half, logperm=logperm):
+    prepare(second_part, G, logperm2.at[G], plane_resist, plane_field, edge_source[...], edge_factor[...])
+    for base, count, part, logperm in ((0, H, first_part, logperm1), (H, G, second_part, logperm2)):
+
+        def prepare_layer(k, carry, base=base, part=part, logperm=logperm):
             z = base + k
-            prepare(half, k, logperm.at[k], resist.at[z], field0.at[z], source[z], factor[z])
+            prepare(part, k, logperm.at[k], resist.at[z], field0.at[z], source[z], factor[z])
             none = jnp.zeros((8, N), F32)
             for ref in (field1, field2, across_x):
                 ref[z, 0:8, :] = none
                 ref[z, 152:160, :] = none
             return carry
 
-        lax.fori_loop(0, 8, prepare_layer, 0, unroll=U6)
+        lax.fori_loop(0, count, prepare_layer, 0, unroll=count)
 
     a = iota((N, 2 * N), 0)
     o = iota((N, 2 * N), 1)
@@ -699,19 +704,19 @@
         hbm(1),
         [shape(Y_ROWS[0], N)] * 2,
         vmem(2),
-        [pltpu.VMEM((8, N, N), F32), pltpu.SemaphoreType.DMA((4,))],
+        [pltpu.VMEM((H, N, N), F32), pltpu.SemaphoreType.DMA((H // 2,))],
         name="pack_first",
     )(in_hbm(noise))
     beside1 = exchange(to_right, to_left, "gy")
     to_right, to_left = call(
         pack_second,
-        vmem(1) + hbm(2),
+        vmem(2) + hbm(2),
         [shape(Y_ROWS[1], N)] * 2,
         vmem(2),
         [block, pltpu.VMEM((NZ, N, N), jnp.int32), pltpu.SemaphoreType.DMA((2, 8))],
         name="pack_second",
         cost=2e10,
-    )(noise, in_hbm(source), in_hbm(biofilm))
+    )(to_left, noise, in_hbm(source), in_hbm(biofilm))
     beside2 = exchange(to_right, to_left, "gy")
     own_middle, own_edge, factor = call(
         column_sums_own,
@@ -724,7 +729,7 @@
     middle1, first_edge, outer, inner = call(
         columns_first,
         vmem(5),
-        [shape(8, N, N), shape(N, N)] + [shape(X_ROWS[0], N)] * 2,
+        [shape(H, N, N), shape(N, N)] + [shape(X_ROWS[0], N)] * 2,
         vmem(4),
         name="columns_first",
     )(own_middle, source, biofilm, *beside1)
@@ -732,7 +737,7 @@
     middle2, edge, edge_source, edge_biofilm, outer, inner = call(
         columns_second,
         vmem(7),
-        [shape(8, N, N), shape(N, N), shape(N, N), shape(N, N)] + [shape(X_ROWS[1], N)] * 2,
+        [shape(G, N, N), shape(N, N), shape(N, N), shape(N, N)] + [shape(X_ROWS[1], N)] * 2,
         vmem(6),
         name="columns_second",
         cost=2e10,
@@ -741,7 +746,7 @@
     partial, edge_factor = call(
         row_sums_own,
         vmem(3),
-        [shape(9, 144, N), shape(N, N)],
+        [shape(G + 1, 144, N), shape(N, N)],
         vmem(2),
         name="rows_own",
         cost=1,
@@ -749,7 +754,7 @@
     logperm1, largest1 = call(
         rows_first,
         vmem(3),
-        [shape(8, 144, N), shape(8, N)],
+        [shape(H, 144, N), shape(8, N)],
         vmem(2),
         name="rows_first",
         cost=2e10,
@@ -766,7 +771,7 @@
         [layers] * 3
         + [pltpu.VMEM((NZ + 1, ROWS, N), F32)]
         + [layers] * 4
-        + [block, pltpu.VMEM((9, 144, N), F32), plane, plane]
+        + [block, pltpu.VMEM((G + 1, 144, N), F32), plane, plane]
         + [sides] * 8
         + [pltpu.SemaphoreType.DMA((3,))],
         name="powers",

time: 71.9 us -> 70.9 us (0.986)
  starting transfers between devices: 21.9 us -> 21 us
    ppermute x2, starting transfers between devices: 8.29 us -> 7.12 us  [exchange_pairs(): lax.ppermute(outer, axis, across)]
  transfers between devices with their start and end apart: 8 -> 8, of which waited for: 3 -> 2; matrix products, arithmetic and copies ran while one was open for 0% -> 0% of each run, Pallas kernels for 8% -> 8%
where the time goes in v5:
time: 70.9 us; the launch traced here: 70.7 us
  blocking collectives  21.6 us (30%)
  starting transfers between devices  21 us (30%)
  Pallas kernels  17.4 us (25%)
  waiting for transfers between devices  9.79 us (14%)
  between operations  0.9 us (1%)
    all_to_all x1, blocking collectives, local(): everyone = lax.all_to_all(table, ('gx', 'gy'), 0, 0, tiled=True)  21.6 us
    ppermute x2, waiting for transfers between devices, exchange_pairs(): lax.ppermute(outer, axis, across)  9.78 us
    ppermute x2, starting transfers between devices, exchange(): lax.ppermute(to_previous, axis, backward)  8.52 us
    ppermute x2, starting transfers between devices, exchange_pairs(): lax.ppermute(outer, axis, across)  7.12 us
    pallas_call x1, Pallas kernels, local(): call(operate_powers, vmem(11), [pltpu.HBM((NZ, N, N), F32)] * 3 + [shape(...  6.86 us
    pallas_call x1, Pallas kernels, local(): call(combine, vmem(2) + hbm(4), [pltpu.HBM((NZ, N, N), F32)] * 2, hbm(2),...  3.25 us
    pallas_call x1, Pallas kernels, local(): call(pack_second, vmem(2) + hbm(2), [shape(Y_ROWS[1], N)] * 2, vmem(2), [...  3.04 us
    ppermute x2, starting transfers between devices, exchange_pairs(): lax.ppermute(inner, axis, [(i, i ^ 1) for i in range(count)])  2.71 us
  transfers between devices with their start and end apart: 8, of which 2 were waited for; matrix products, arithmetic and copies ran while one was open for 0% of the time, Pallas kernels for 8%

profile of v5, /device:TPU:1, one launch (start us, length us, event | category | flops | bytes accessed | tf_op | source)
XLA Modules:
  0.0 70.7 jit_solution(5335117882328649221)
XLA Ops:
  0.6 0.0 copy-start.1
  0.6 1.5 %pack_first.1 = (f32[640,128]{1,0:T(8,128)S(1)}, f32[640,128]{1,0:T(8,128)S(1)}) custom-call(f32[16,128,128]{2,1,0:T(8,128)} %noise.3), custom_call_target="tpu_custom_call" | custom-call | flops 1000000 | bytes 1000000 | tf_op jit(solution)/shard_map/pack_first/pallas_call | solution.py:702
  2.2 2.5 %collective-permute-start = (f32[640,128]{1,0:T(8,128)S(1)}, f32[640,128]{1,0:T(8,128)S(1)}, u32[]{:S(2)}, u32[]{:S(2)}) collective-permute-start(f32[640,128]{1,0:T(8,128)S(1)} %get-tuple-element.28), channel_id=1, source_target_pairs={{0,1},{1,2},{2,3},{3,4},{4,5},{5,6},{6,7},{7,8},{8,9},{9,10},{10,1... | collective-permute-start | bytes 983048 | tf_op jit(solution)/shard_map/ppermute | solution.py:691
  4.7 0.0 copy-start.2
  4.7 5.0 %collective-permute-start.1 = (f32[640,128]{1,0:T(8,128)S(1)}, f32[640,128]{1,0:T(8,128)S(1)}, u32[]{:S(2)}, u32[]{:S(2)}) collective-permute-start(f32[640,128]{1,0:T(8,128)S(1)} %get-tuple-element.29.after), channel_id=1, source_target_pairs={{1,0},{2,1},{3,2},{4,3},{5,4},{6,5},{7,6},{8,7},{9,8},{10,9},{11,1... | collective-permute-start | bytes 983048 | tf_op jit(solution)/shard_map/ppermute | solution.py:691
  9.7 0.0 copy-done.1
  9.7 3.0 %pack_second.1 = (f32[528,128]{1,0:T(8,128)S(1)}, f32[528,128]{1,0:T(8,128)S(1)}) custom-call(f32[640,128]{1,0:T(8,128)S(1)} %get-tuple-element.29.after, f32[16,128,128]{2,1,0:T(8,128)S(1)} %copy-done.1, f32[16,128,128]{2,1,0:T(8,128)} %source_in.3, s32[16,128,128]{2,1,0:T(8,128)} %biofilm.5), custom_call_target="tpu_custom_call" | custom-call | flops 20000000000 | bytes 20000000000 | tf_op jit(solution)/shard_map/pack_second/pallas_call | solution.py:711
  12.7 0.1 collective-permute-start.4
  12.8 0.0 copy-start
  12.9 3.6 %collective-permute-start.5 = (f32[528,128]{1,0:T(8,128)S(1)}, f32[528,128]{1,0:T(8,128)S(1)}, u32[]{:S(2)}, u32[]{:S(2)}) collective-permute-start(f32[528,128]{1,0:T(8,128)S(1)} %get-tuple-element.38), channel_id=1, source_target_pairs={{1,0},{2,1},{3,2},{4,3},{5,4},{6,5},{7,6},{8,7},{9,8},{10,9},{11,1... | collective-permute-start | bytes 811016 | tf_op jit(solution)/shard_map/ppermute | solution.py:691
  16.4 0.0 copy-done.2
  16.4 0.9 %columns_own.1 = (f32[16,128,128]{2,1,0:T(8,128)S(1)}, f32[128,128]{1,0:T(8,128)S(1)}, f32[16,128,128]{2,1,0:T(8,128)S(1)}) custom-call(f32[16,128,128]{2,1,0:T(8,128)S(1)} %copy-done.1, s32[16,128,128]{2,1,0:T(8,128)S(1)} %copy-done.2), custom_call_target="tpu_custom_call" | custom-call | flops 20000000000 | bytes 20000000000 | tf_op jit(solution)/shard_map/columns_own/pallas_call | solution.py:721
  17.3 0.0 collective-permute-done.from_left
  17.3 0.0 collective-permute-done.1.from_right
  17.3 0.0 copy-done
  17.3 0.7 columns_first.1
  18.0 3.9 %collective-permute-start.2 = (f32[736,128]{1,0:T(8,128)S(1)}, f32[736,128]{1,0:T(8,128)S(1)}, u32[]{:S(2)}, u32[]{:S(2)}) collective-permute-start(f32[736,128]{1,0:T(8,128)S(1)} %get-tuple-element.31), channel_id=1, source_target_pairs={{0,240},{16,32},{32,16},{48,64},{64,48},{80,96},{96,80},{112,128},... | collective-permute-start | bytes 1130504 | tf_op jit(solution)/shard_map/ppermute | solution.py:697
  21.9 1.5 %collective-permute-start.3 = (f32[736,128]{1,0:T(8,128)S(1)}, f32[736,128]{1,0:T(8,128)S(1)}, u32[]{:S(2)}, u32[]{:S(2)}) collective-permute-start(f32[736,128]{1,0:T(8,128)S(1)} %get-tuple-element.32), channel_id=1, source_target_pairs={{0,16},{16,0},{32,48},{48,32},{64,80},{80,64},{96,112},{112,96},{1... | collective-permute-start | bytes 1130504 | tf_op jit(solution)/shard_map/ppermute | solution.py:697
  23.4 0.0 collective-permute-done.4.from_left
  23.4 0.0 collective-permute-done.5.from_right
  23.4 0.5 columns_second.1
  23.9 3.2 %collective-permute-start.6 = (f32[512,128]{1,0:T(8,128)S(1)}, f32[512,128]{1,0:T(8,128)S(1)}, u32[]{:S(2)}, u32[]{:S(2)}) collective-permute-start(f32[512,128]{1,0:T(8,128)S(1)} %get-tuple-element.46), channel_id=1, source_target_pairs={{0,240},{16,32},{32,16},{48,64},{64,48},{80,96},{96,80},{112,128},... | collective-permute-start | bytes 786440 | tf_op jit(solution)/shard_map/ppermute | solution.py:697
  27.1 1.2 %collective-permute-start.7 = (f32[512,128]{1,0:T(8,128)S(1)}, f32[512,128]{1,0:T(8,128)S(1)}, u32[]{:S(2)}, u32[]{:S(2)}) collective-permute-start(f32[512,128]{1,0:T(8,128)S(1)} %get-tuple-element.47), channel_id=1, source_target_pairs={{0,16},{16,0},{32,48},{48,32},{64,80},{80,64},{96,112},{112,96},{1... | collective-permute-start | bytes 786440 | tf_op jit(solution)/shard_map/ppermute | solution.py:697
  28.4 0.2 rows_own.1
  28.6 4.6 %collective-permute-done.2.outer.outer1 = f32[736,128]{1,0:T(8,128)S(1)} collective-permute-done((f32[736,128]{1,0:T(8,128)S(1)}, f32[736,128]{1,0:T(8,128)S(1)}, u32[]{:S(2)}, u32[]{:S(2)}) %collective-permute-start.2) | collective-permute-done | bytes 376864 | tf_op jit(solution)/shard_map/ppermute | solution.py:697
  33.2 0.0 collective-permute-done.3.inner.inner1
  33.2 0.4 rows_first.1
  33.6 5.2 %collective-permute-done.6.outer2 = f32[512,128]{1,0:T(8,128)S(1)} collective-permute-done((f32[512,128]{1,0:T(8,128)S(1)}, f32[512,128]{1,0:T(8,128)S(1)}, u32[]{:S(2)}, u32[]{:S(2)}) %collective-permute-start.6) | collective-permute-done | bytes 262176 | tf_op jit(solution)/shard_map/ppermute | solution.py:697
  38.8 0.0 collective-permute-done.7.inner2
  38.8 6.9 %powers.1 = (f32[16,128,128]{2,1,0:T(8,128)}, f32[16,128,128]{2,1,0:T(8,128)}, f32[16,128,128]{2,1,0:T(8,128)}, f32[256,128]{1,0:T(8,128)S(1)}) custom-call(f32[10,144,128]{2,1,0:T(8,128)S(1)} %get-tuple-element.33.logperm1, f32[8,128]{1,0:T(8,128)S(1)} %get-tuple-element.34.largest1, f32[7,144,128]{2,1,0:T(8,128)S(1)} %get-tuple-element.42.partial, ...), custom_call_target="tpu_custom_call" | custom-call | flops 1000000 | bytes 1000000 | tf_op jit(solution)/shard_map/powers/pallas_call | solution.py:766
  45.7 21.6 %all_to_all.11 = f32[256,1,128]{2,1,0:T(1,128)S(1)} all-to-all(f32[256,1,128]{2,1,0:T(1,128)S(1)} %bitcast.4), channel_id=1, replica_groups=mesh['gx'=16,'gy'=16] {'gx','gy'}, dimensions={0} | all-to-all | bytes 262144 | tf_op jit(solution)/shard_map/all_to_all | solution.py:779
  67.3 3.3 %combine.1 = (f32[16,128,128]{2,1,0:T(8,128)}, f32[16,128,128]{2,1,0:T(8,128)}) custom-call(f32[256,128]{1,0:T(8,128)S(1)} %bitcast.5, f32[256,128]{1,0:T(8,128)S(1)} %get-tuple-element.48.own, f32[16,128,128]{2,1,0:T(8,128)} %source_in.3, f32[16,128,128]{2,1,0:T(8,128)} %get-tuple-element.49.power1_in, f32[16,128,128]{2,1,0:T(8,128)} %get-tuple-element.50.power2_in, ...), custom_call_target="tpu_custom_call" | custom-call | flops 1000000 | bytes 1000000 | tf_op jit(solution)/shard_map/combine/pallas_call | solution.py:781
Async XLA Ops:
  0.6 9.1 %copy-start.1 = (f32[16,128,128]{2,1,0:T(8,128)S(1)}, f32[16,128,128]{2,1,0:T(8,128)}, u32[]{:S(2)}) copy-start(f32[16,128,128]{2,1,0:T(8,128)} %noise.3) | copy-start | bytes 3145732
  2.2 15.1 %collective-permute-start = (f32[640,128]{1,0:T(8,128)S(1)}, f32[640,128]{1,0:T(8,128)S(1)}, u32[]{:S(2)}, u32[]{:S(2)}) collective-permute-start(f32[640,128]{1,0:T(8,128)S(1)} %get-tuple-element.28), channel_id=1, source_target_pairs={{0,1},{1,2},{2,3},{3,4},{4,5},{5,6},{6,7},{7,8},{8,9},{9,10},{10,1... | collective-permute-start | bytes 983048 | tf_op jit(solution)/shard_map/ppermute | solution.py:691
  4.7 11.7 %copy-start.2 = (s32[16,128,128]{2,1,0:T(8,128)S(1)}, s32[16,128,128]{2,1,0:T(8,128)}, u32[]{:S(2)}) copy-start(s32[16,128,128]{2,1,0:T(8,128)} %biofilm.5) | copy-start | bytes 3145732
  4.7 12.6 %collective-permute-start.1 = (f32[640,128]{1,0:T(8,128)S(1)}, f32[640,128]{1,0:T(8,128)S(1)}, u32[]{:S(2)}, u32[]{:S(2)}) collective-permute-start(f32[640,128]{1,0:T(8,128)S(1)} %get-tuple-element.29.after), channel_id=1, source_target_pairs={{1,0},{2,1},{3,2},{4,3},{5,4},{6,5},{7,6},{8,7},{9,8},{10,9},{11,1... | collective-permute-start | bytes 983048 | tf_op jit(solution)/shard_map/ppermute | solution.py:691
  12.7 10.6 %collective-permute-start.4 = (f32[528,128]{1,0:T(8,128)S(1)}, f32[528,128]{1,0:T(8,128)S(1)}, u32[]{:S(2)}, u32[]{:S(2)}) collective-permute-start(f32[528,128]{1,0:T(8,128)S(1)} %get-tuple-element.37), channel_id=1, source_target_pairs={{0,1},{1,2},{2,3},{3,4},{4,5},{5,6},{6,7},{7,8},{8,9},{9,10},{10,1... | collective-permute-start | bytes 811016 | tf_op jit(solution)/shard_map/ppermute | solution.py:691
  12.8 4.5 %copy-start = (f32[16,128,128]{2,1,0:T(8,128)S(1)}, f32[16,128,128]{2,1,0:T(8,128)}, u32[]{:S(2)}) copy-start(f32[16,128,128]{2,1,0:T(8,128)} %source_in.3) | copy-start | bytes 3145732
  12.9 10.5 %collective-permute-start.5 = (f32[528,128]{1,0:T(8,128)S(1)}, f32[528,128]{1,0:T(8,128)S(1)}, u32[]{:S(2)}, u32[]{:S(2)}) collective-permute-start(f32[528,128]{1,0:T(8,128)S(1)} %get-tuple-element.38), channel_id=1, source_target_pairs={{1,0},{2,1},{3,2},{4,3},{5,4},{6,5},{7,6},{8,7},{9,8},{10,9},{11,1... | collective-permute-start | bytes 811016 | tf_op jit(solution)/shard_map/ppermute | solution.py:691
  18.0 15.2 %collective-permute-start.2 = (f32[736,128]{1,0:T(8,128)S(1)}, f32[736,128]{1,0:T(8,128)S(1)}, u32[]{:S(2)}, u32[]{:S(2)}) collective-permute-start(f32[736,128]{1,0:T(8,128)S(1)} %get-tuple-element.31), channel_id=1, source_target_pairs={{0,240},{16,32},{32,16},{48,64},{64,48},{80,96},{96,80},{112,128},... | collective-permute-start | bytes 1130504 | tf_op jit(solution)/shard_map/ppermute | solution.py:697
  21.9 11.3 %collective-permute-start.3 = (f32[736,128]{1,0:T(8,128)S(1)}, f32[736,128]{1,0:T(8,128)S(1)}, u32[]{:S(2)}, u32[]{:S(2)}) collective-permute-start(f32[736,128]{1,0:T(8,128)S(1)} %get-tuple-element.32), channel_id=1, source_target_pairs={{0,16},{16,0},{32,48},{48,32},{64,80},{80,64},{96,112},{112,96},{1... | collective-permute-start | bytes 1130504 | tf_op jit(solution)/shard_map/ppermute | solution.py:697
  23.9 14.9 %collective-permute-start.6 = (f32[512,128]{1,0:T(8,128)S(1)}, f32[512,128]{1,0:T(8,128)S(1)}, u32[]{:S(2)}, u32[]{:S(2)}) collective-permute-start(f32[512,128]{1,0:T(8,128)S(1)} %get-tuple-element.46), channel_id=1, source_target_pairs={{0,240},{16,32},{32,16},{48,64},{64,48},{80,96},{96,80},{112,128},... | collective-permute-start | bytes 786440 | tf_op jit(solution)/shard_map/ppermute | solution.py:697
  27.1 11.7 %collective-permute-start.7 = (f32[512,128]{1,0:T(8,128)S(1)}, f32[512,128]{1,0:T(8,128)S(1)}, u32[]{:S(2)}, u32[]{:S(2)}) collective-permute-start(f32[512,128]{1,0:T(8,128)S(1)} %get-tuple-element.47), channel_id=1, source_target_pairs={{0,16},{16,0},{32,48},{48,32},{64,80},{80,64},{96,112},{112,96},{1... | collective-permute-start | bytes 786440 | tf_op jit(solution)/shard_map/ppermute | solution.py:697

commit v6 on v5

--- a/solution.py
+++ b/solution.py
@@ -20,9 +20,7 @@
 ROWS = 160
 OWN = 16
 HUGE = 1e30
-U1, U2, U3, U5 = 16, 4, 4, 16
-V2, V3 = 4, 1
-C2, C3 = 144, 64
+C3 = 64
 
 
 def iota(shape, dim):
@@ -302,9 +300,99 @@
     return jnp.max(jnp.where(real, total, -HUGE).reshape(18, 8, N), axis=0)
 
 
-def rows_first(middle, outer, inner, logperm, largest):
+def row_sums_own(middle, edge, edge_biofilm, partial, factor):
+    own, _ = row_weights()
+    for z in range(0, G, 2):
+        partial[z], partial[z + 1] = row_sums(own, middle[z], middle[z + 1])
+    partial[G] = row_sums(own, edge[...])[0]
+    factor[...] = resistance_factor(edge_biofilm[...])
+
+
+def resistance_factor(biofilm):
+    open_part = 1.0 - 0.06 * biofilm
+    solid = (1.0 - 0.35 * open_part) * (1.0 / (1.0 - 0.35))
+    return (0.5 * solid * solid) / (open_part * open_part * open_part)
+
+
+def resistance(logperm, factor, top):
+    return jnp.minimum(jnp.exp(top - logperm) * factor, HUGE)
+
+
+def reciprocal(x):
+    guess = pl.reciprocal(x, approx=True)
+    return guess * (2.0 - x * guess)
+
+
+MAIN = slice(8, 152)
+BEFORE = slice(7, 151)
+AFTER = slice(9, 153)
+OWN_ROWS = tuple((start, C3) for start in range(16, 144, C3))
+
+
+def largest_of(tile):
+    return jnp.maximum(jnp.max(jnp.max(tile, axis=0, keepdims=True), axis=1, keepdims=True), -60.0)
+
+
+def halo_tiles(part, z):
+    from_up, from_down, tail = part
+    row8 = iota((8, N), 0)
+    first = pl.multiple_of(z * 72, 8)
+    above = from_up[pl.ds(first, 8), :]
+    below = from_down[pl.ds(first + 64, 8), :]
+    third_above = from_up[pl.ds(tail + z, 1), :]
+    third_below = from_down[pl.ds(tail + z, 1), :]
+    source_above = jnp.where(row8 >= 5, roll(above, 5, 0), 0.0)
+    source_below = jnp.where(row8 <= 2, roll(below, 5, 0), 0.0)
+    biofilm_above = jnp.where(row8 == 5, third_above, jnp.where(row8 >= 6, roll(above, 3, 0), 0.0))
+    biofilm_below = jnp.where(row8 == 2, third_below, jnp.where(row8 <= 1, roll(below, 2, 0), 0.0))
+    return source_above, source_below, biofilm_above, biofilm_below
+
+
+def prepare(part, z, top, logperm, out, field, own_source, own_factor):
+    row8 = iota((8, N), 0)
+    source_above, source_below, biofilm_above, biofilm_below = halo_tiles(part, z)
+    field[8:16, :] = source_above
+    field[16:144, :] = own_source
+    field[144:152, :] = source_below
+    out[8:16, :] = jnp.where(row8 >= 5, resistance(logperm[0:8, :], resistance_factor(biofilm_above), top), HUGE)
+    out[144:152, :] = jnp.where(row8 <= 2, resistance(logperm[136:144, :], resistance_factor(biofilm_below), top), HUGE)
+    out[16:144, :] = resistance(logperm[8:136, :], own_factor, top)
+    empty = jnp.full((8, N), HUGE, F32)
+    none = jnp.zeros((8, N), F32)
+    out[0:8, :] = empty
+    out[152:160, :] = empty
+    field[0:8, :] = none
+    field[152:160, :] = none
+
+
+def block_faces(here_ref, last_ref, across_x, across_y, across_z):
+    here = here_ref[MAIN, :]
+    across_x[MAIN, :] = reciprocal(here + here_ref[BEFORE, :])
+    across_x[152:160, :] = jnp.zeros((8, N), F32)
+    across_y[MAIN, :] = jnp.where(iota((144, N), 1) == 0, 0.0, reciprocal(here + roll(here, 1, 1)))
+    if last_ref is None:
+        across_z[MAIN, :] = jnp.zeros((144, N), F32)
+    else:
+        across_z[MAIN, :] = reciprocal(here + last_ref[MAIN, :])
+
+
+def pack_inner(p, layers):
+    group = iota((ROWS, N), 1) // 16
+    packed = jnp.zeros((ROWS, N), F32)
+    for z, ref in layers:
+        if z // 8 == p:
+            packed = jnp.where(group == z % 8, roll(ref[...], 16 * (z % 8) + 3, 1), packed)
+    return packed
+
+
+def rows_first(
+    middle, factor, source, outer, inner,
+    largest, field0, across_x, across_y, across_z, image, last_resist, packed_resist, packed_field,
+    logperm, resist, flow,
+):
     even = on_even()
     from_up, from_down = Chosen(even, outer, inner), Chosen(even, inner, outer)
+    part = (from_up, from_down, X_TAIL[0])
     own, halo = row_weights()
     most = jnp.full((8, N), -HUGE, F32)
     for z in range(0, H, 2):
@@ -312,107 +400,75 @@
         far = row_sums(halo, *[halo_rows(from_up, from_down, z + i) for i in (0, 1)])
         for i in (0, 1):
             most = jnp.maximum(most, finish_sums(from_up, from_down, z + i, near[i] + far[i], logperm.at[z + i]))
-    largest[...] = most
-
-
-def row_sums_own(middle, edge, edge_biofilm, partial, factor):
-    own, _ = row_weights()
-    for z in range(0, G, 2):
-        partial[z], partial[z + 1] = row_sums(own, middle[z], middle[z + 1])
-    partial[G] = row_sums(own, edge[...])[0]
-    factor[...] = resistance_factor(edge_biofilm[...])
-
-
-def resistance_factor(biofilm):
-    open_part = 1.0 - 0.06 * biofilm
-    solid = (1.0 - 0.35 * open_part) * (1.0 / (1.0 - 0.35))
-    return (0.5 * solid * solid) / (open_part * open_part * open_part)
-
-
-def resistance(logperm, factor, top):
-    return jnp.minimum(jnp.exp(top - logperm) * factor, HUGE)
-
-
-def reciprocal(x):
-    guess = pl.reciprocal(x, approx=True)
-    return guess * (2.0 - x * guess)
-
-
-WIDE = tuple((start, C2) for start in range(8, 152, C2))
-OWN_ROWS = tuple((start, C3) for start in range(16, 144, C3))
+    top = largest_of(most)
+    largest[...] = jnp.broadcast_to(top, (8, N))
+    for z in range(H):
+        prepare(part, z, top, logperm.at[z], resist.at[z], field0.at[z], source[z], factor[z])
+    for z in range(H):
+        block_faces(
+            resist.at[z], resist.at[z - 1] if z else None, across_x.at[z], across_y.at[z], across_z.at[z]
+        )
+    last_resist[...] = resist[H - 1]
+    for packed, ref in ((packed_resist, resist), (packed_field, field0)):
+        for p in range(2):
+            packed[p] = pack_inner(p, [(z, ref.at[z]) for z in range(H)])
+    for z in range(H):
+        here = field0[z, MAIN, :]
+        flow[z, MAIN, :] = across_y[z, MAIN, :] * (here - roll(here, 1, 1))
+    from_last = jnp.zeros((144, N), F32)
+    for z in range(H):
+        here = field0[z, MAIN, :]
+        inward = flow[z, MAIN, :]
+        value = inward - roll(inward, -1, 1) + from_last
+        value = value + across_x[z, MAIN, :] * (here - field0[z, BEFORE, :])
+        value = value - across_x[z, AFTER, :] * (field0[z, AFTER, :] - here)
+        if z < H - 1:
+            from_last = across_z[z + 1, MAIN, :] * (field0[z + 1, MAIN, :] - here)
+            value = value - from_last
+        image[z] = value
 
 
 def operate_powers(
-    logperm1, largest1, partial, factor, edge_factor, edge_source, source, outer1, inner1, outer2, inner2,
+    largest1, field0_1, across_x1, across_y1, across_z1, image1, last_resist, packed_resist, packed_field,
+    partial, factor, edge_factor, edge_source, source, outer2, inner2,
     power1, power2, power3, table,
-    resist, across_x, across_y, across_z, flow, field0, field1, field2, field3, logperm2, plane_resist, plane_field,
+    resist, across_x2, across_y2, across_z2, flow, field0_2, field1, field2, field3,
+    logperm2, plane_resist, plane_field,
     side_resist, side_x, side_y, side_z, side0, side1, side2, side_flux, done,
 ):
     lane = iota((8, N), 1)
-    row8 = iota((8, N), 0)
-
     even = on_even()
-    from_up1, from_down1 = Chosen(even, outer1, inner1), Chosen(even, inner1, outer1)
     from_up2, from_down2 = Chosen(even, outer2, inner2), Chosen(even, inner2, outer2)
+    part = (from_up2, from_down2, X_TAIL[1])
 
     _, halo = row_weights()
     edge_lane = (iota((144, N), 1) % 8 <= 2) | (iota((144, N), 1) % 8 >= 5)
-    second = (from_up2, from_down2)
     largest = largest1[...]
+    top1 = largest[:1, :1]
     for z in range(0, G, 2):
-        pair = row_sums(halo, halo_rows(*second, z), halo_rows(*second, z + 1))
+        pair = row_sums(halo, halo_rows(from_up2, from_down2, z), halo_rows(from_up2, from_down2, z + 1))
         for i in (0, 1):
             sums = partial[z + i] + pair[i]
-            largest = jnp.maximum(largest, finish_sums(*second, z + i, sums, logperm2.at[z + i]))
-    sums = partial[G] + row_sums(halo, halo_rows(*second, G))[0]
-    largest = jnp.maximum(largest, finish_sums(*second, G, sums, logperm2.at[G], edge_lane))
-    top = jnp.max(jnp.max(largest, axis=0, keepdims=True), axis=1, keepdims=True)
-    top = jnp.maximum(top, -60.0)
-
-    def halo_tiles(part, z):
-        from_up, from_down, tail = part
-        first = pl.multiple_of(z * 72, 8)
-        above = from_up[pl.ds(first, 8), :]
-        below = from_down[pl.ds(first + 64, 8), :]
-        third_above = from_up[pl.ds(tail + z, 1), :]
-        third_below = from_down[pl.ds(tail + z, 1), :]
-        source_above = jnp.where(row8 >= 5, roll(above, 5, 0), 0.0)
-        source_below = jnp.where(row8 <= 2, roll(below, 5, 0), 0.0)
-        biofilm_above = jnp.where(row8 == 5, third_above, jnp.where(row8 >= 6, roll(above, 3, 0), 0.0))
-        biofilm_below = jnp.where(row8 == 2, third_below, jnp.where(row8 <= 1, roll(below, 2, 0), 0.0))
-        return source_above, source_below, biofilm_above, biofilm_below
-
-    first_part = (from_up1, from_down1, X_TAIL[0])
-    second_part = (from_up2, from_down2, X_TAIL[1])
-
-    def prepare(part, z, logperm, out, field, own_source, own_factor):
-        source_above, source_below, biofilm_above, biofilm_below = halo_tiles(part, z)
-        field[8:16, :] = source_above
-        field[16:144, :] = own_source
-        field[144:152, :] = source_below
-        out[8:16, :] = jnp.where(row8 >= 5, resistance(logperm[0:8, :], resistance_factor(biofilm_above), top), HUGE)
-        out[144:152, :] = jnp.where(row8 <= 2, resistance(logperm[136:144, :], resistance_factor(biofilm_below), top), HUGE)
-        out[16:144, :] = resistance(logperm[8:136, :], own_factor, top)
-        empty = jnp.full((8, N), HUGE, F32)
-        none = jnp.zeros((8, N), F32)
-        out[0:8, :] = empty
-        out[152:160, :] = empty
-        field[0:8, :] = none
-        field[152:160, :] = none
-
-    prepare(second_part, G, logperm2.at[G], plane_resist, plane_field, edge_source[...], edge_factor[...])
-    for base, count, part, logperm in ((0, H, first_part, logperm1), (H, G, second_part, logperm2)):
-
-        def prepare_layer(k, carry, base=base, part=part, logperm=logperm):
-            z = base + k
-            prepare(part, k, logperm.at[k], resist.at[z], field0.at[z], source[z], factor[z])
-            none = jnp.zeros((8, N), F32)
-            for ref in (field1, field2, across_x):
-                ref[z, 0:8, :] = none
-                ref[z, 152:160, :] = none
-            return carry
-
-        lax.fori_loop(0, count, prepare_layer, 0, unroll=count)
+            largest = jnp.maximum(largest, finish_sums(from_up2, from_down2, z + i, sums, logperm2.at[z + i]))
+    sums = partial[G] + row_sums(halo, halo_rows(from_up2, from_down2, G))[0]
+    largest = jnp.maximum(largest, finish_sums(from_up2, from_down2, G, sums, logperm2.at[G], edge_lane))
+    top = largest_of(largest)
+    shrink = jnp.exp(top1 - top)
+    grow = jnp.exp(top - top1)
+
+    prepare(part, G, top, logperm2.at[G], plane_resist, plane_field, edge_source[...], edge_factor[...])
+    for k in range(G):
+        prepare(part, k, top, logperm2.at[k], resist.at[1 + k], field0_2.at[k], source[H + k], factor[H + k])
+    resist[0] = jnp.minimum(last_resist[...] * grow, HUGE)
+    none = jnp.zeros((8, N), F32)
+    for ref in (field1, field2):
+        for z in range(NZ):
+            ref[z, 0:8, :] = none
+            ref[z, 152:160, :] = none
+    for ref in (side1, side2, side_x):
+        for p in range(2):
+            ref[p, 0:8, :] = none
+            ref[p, 152:160, :] = none
 
     a = iota((N, 2 * N), 0)
     o = iota((N, 2 * N), 1)
@@ -421,22 +477,25 @@
         (a // 8 == o // 16)
         & (((t >= 3) & (t <= 5) & (a % 8 == t - 3)) | ((t >= 10) & (t <= 12) & (a % 8 == t - 5)))
     )
-    lane160 = iota((ROWS, N), 1)
-    slot160 = lane160 % 16
-    for plane, field, side, fill in ((plane_resist, resist, side_resist, HUGE), (plane_field, field0, side0, 0.0)):
+    slot160 = iota((ROWS, N), 1) % 16
+    second_resist = [(H + k, resist.at[1 + k]) for k in range(G)]
+    second_field = [(H + k, field0_2.at[k]) for k in range(G)]
+    first_group = iota((ROWS, N), 1) // 16
+    for plane, packed, second, side, fill in (
+        (plane_resist, packed_resist, second_resist, side_resist, HUGE),
+        (plane_field, packed_field, second_field, side0, 0.0),
+    ):
         high, mid, low = split3(plane[...])
-        outer = dot(high, spread) + dot(mid, spread) + dot(low, spread)
+        beyond = dot(high, spread) + dot(mid, spread) + dot(low, spread)
         for p in range(2):
-            inner = jnp.zeros((ROWS, N), F32)
-            for k in range(8):
-                inner = jnp.where(lane160 // 16 == k, roll(field[8 * p + k], 16 * k + 3, 1), inner)
-            value = jnp.where(slot160 <= 2, inner, jnp.where(slot160 >= 13, roll(inner, 10, 1), outer[:, p * N : p * N + N]))
+            inside = packed[p]
+            if fill:
+                inside = jnp.minimum(inside * grow, HUGE)
+            inside = jnp.where(first_group + 8 * p < H, inside, pack_inner(p, second))
+            value = jnp.where(
+                slot160 <= 2, inside, jnp.where(slot160 >= 13, roll(inside, 10, 1), beyond[:, p * N : p * N + N])
+            )
             side[p] = jnp.where((slot160 <= 5) | (slot160 >= 10), value, fill)
-    none = jnp.zeros((8, N), F32)
-    for p in range(2):
-        for ref in (side1, side2, side_x):
-            ref[p, 0:8, :] = none
-            ref[p, 152:160, :] = none
 
     def next_layer(first, second):
         lanes = iota(first.shape, 1)
@@ -449,117 +508,115 @@
             jnp.where(lanes >= 16, roll(second, 16, 1), roll(first, 16, 1)),
         )
 
-    for start, size in WIDE:
+    here = [side_resist[p, MAIN, :] for p in range(2)]
+    after = next_layer(*here)
+    for p in range(2):
+        side_x[p, MAIN, :] = reciprocal(here[p] + side_resist[p, BEFORE, :])
+        side_y[p, MAIN, :] = reciprocal(here[p] + roll(here[p], 1, 1))
+        value = reciprocal(here[p] + after[p])
+        side_z[p, MAIN, :] = value if p == 0 else jnp.where(iota((144, N), 1) < 112, value, 0.0)
+    for k in range(G):
+        block_faces(resist.at[1 + k], resist.at[k], across_x2.at[k], across_y2.at[k], across_z2.at[k])
+
+    def layer_of(first, second, z):
+        return first.at[z] if z < H else second.at[z - H]
+
+    field0 = [layer_of(field0_1, field0_2, z) for z in range(NZ)]
+    across_x = [layer_of(across_x1, across_x2, z) for z in range(NZ)]
+    across_y = [layer_of(across_y1, across_y2, z) for z in range(NZ)]
+    across_z = [layer_of(across_z1, across_z2, z) for z in range(NZ)]
+
+    def apply_sides(field, image):
+        slot = iota((144, N), 1) % 16
+        here = [field[p, MAIN, :] for p in range(2)]
+        inward = [side_y[p, MAIN, :] * (here[p] - roll(here[p], 1, 1)) for p in range(2)]
+        for p in range(2):
+            side_flux[p, MAIN, :] = jnp.where(slot == 13, inward[p], -roll(inward[p], 9, 1))
+        if image is None:
+            return
+        after = next_layer(*here)
+        through = [side_z[p, MAIN, :] * (after[p] - here[p]) for p in range(2)]
+        back = last_layer(*through)
+        for p in range(2):
+            value = inward[p] - roll(inward[p], -1, 1) - through[p] + back[p]
+            value = value + side_x[p, MAIN, :] * (here[p] - field[p, BEFORE, :])
+            value = value - side_x[p, AFTER, :] * (field[p, AFTER, :] - here[p])
+            image[p, MAIN, :] = value
+
+    def flow_along_y(field, layers):
+        for z in layers:
+            here = field[z][MAIN, :]
+            flow[z, MAIN, :] = across_y[z][MAIN, :] * (here - roll(here, 1, 1))
+
+    def from_beside(z, rows, size):
+        lanes = iota((size, N), 1)
+        beside = roll(side_flux[z // 8, rows, :], 115 - 16 * (z % 8), 1)
+        return jnp.where((lanes == 0) | (lanes == 127), beside, 0.0)
+
+    def apply_layers(field, layers, start, size):
         rows = slice(start, start + size)
-        here = [side_resist[p, rows, :] for p in range(2)]
-        after = next_layer(*here)
-        for p in range(2):
-            side_x[p, rows, :] = reciprocal(here[p] + side_resist[p, start - 1 : start - 1 + size, :])
-            side_y[p, rows, :] = reciprocal(here[p] + roll(here[p], 1, 1))
-            value = reciprocal(here[p] + after[p])
-            side_z[p, rows, :] = value if p == 0 else jnp.where(iota((size, N), 1) < 112, value, 0.0)
-
-    def faces(z, carry):
-        for start, size in WIDE:
-            rows = slice(start, start + size)
-            here = resist[z, rows, :]
-            across_x[z, rows, :] = reciprocal(here + resist[z, start - 1 : start - 1 + size, :])
-            across_y[z, rows, :] = jnp.where(iota((size, N), 1) == 0, 0.0, reciprocal(here + roll(here, 1, 1)))
-            above = resist[jnp.maximum(z - 1, 0), rows, :]
-            across_z[z, rows, :] = jnp.where(z > 0, reciprocal(here + above), 0.0)
-        return carry
-
-    lax.fori_loop(0, 16, faces, 0, unroll=U5)
-    across_z[16] = jnp.zeros((ROWS, N), F32)
-
-    def apply_sides(field, image):
-        for start, size in WIDE:
-            rows = slice(start, start + size)
-            slot = iota((size, N), 1) % 16
-            here = [field[p, rows, :] for p in range(2)]
-            inward = [side_y[p, rows, :] * (here[p] - roll(here[p], 1, 1)) for p in range(2)]
-            for p in range(2):
-                side_flux[p, rows, :] = jnp.where(slot == 13, inward[p], -roll(inward[p], 9, 1))
-            if image is None:
-                continue
-            after = next_layer(*here)
-            through = [side_z[p, rows, :] * (after[p] - here[p]) for p in range(2)]
-            back = last_layer(*through)
-            for p in range(2):
-                value = inward[p] - roll(inward[p], -1, 1) - through[p] + back[p]
-                value = value + side_x[p, rows, :] * (here[p] - field[p, start - 1 : start - 1 + size, :])
-                value = value - side_x[p, start + 1 : start + 1 + size, :] * (
-                    field[p, start + 1 : start + 1 + size, :] - here[p]
-                )
-                image[p, rows, :] = value
-
-    def flow_along_y(field):
-        def layer(z, carry):
-            for start, size in WIDE:
-                rows = slice(start, start + size)
-                here = field[z, rows, :]
-                flow[z, rows, :] = across_y[z, rows, :] * (here - roll(here, 1, 1))
-            return carry
-
-        lax.fori_loop(0, 16, layer, 0, unroll=U1)
-
-    def apply_layers(field, first, count, start, size):
-        rows = slice(start, start + size)
-        lanes = iota((size, N), 1)
-        ends = (lanes == 0) | (lanes == 127)
-        here = field[first, rows, :]
-        from_last = across_z[first, rows, :] * (here - field[jnp.maximum(first - 1, 0), rows, :])
-        for k in range(count):
-            z = first + k
-            after = field[jnp.minimum(z + 1, 15) if k == count - 1 else z + 1, rows, :]
-            to_next = across_z[z + 1, rows, :] * (after - here)
+        before = slice(start - 1, start - 1 + size)
+        after = slice(start + 1, start + 1 + size)
+        first = layers[0]
+        here = field[first][rows, :]
+        from_last = 0.0 if first == 0 else across_z[first][rows, :] * (here - field[first - 1][rows, :])
+        for z in layers:
             inward = flow[z, rows, :]
-            beside = roll(side_flux[z // 8, rows, :], 115 - 16 * (z % 8), 1)
-            value = inward - roll(inward, -1, 1) + jnp.where(ends, beside, 0.0)
-            value = value + across_x[z, rows, :] * (here - field[z, start - 1 : start - 1 + size, :])
-            value = value - across_x[z, start + 1 : start + 1 + size, :] * (
-                field[z, start + 1 : start + 1 + size, :] - here
-            )
-            yield z, here, value + from_last - to_next
-            here, from_last = after, to_next
-
-    def apply(field, image):
-        flow_along_y(field)
-
-        def layers(k, carry):
-            for start, size in WIDE:
-                for z, _, value in apply_layers(field, k * U2, U2, start, size):
-                    image[z, start : start + size, :] = value
-            return carry
-
-        lax.fori_loop(0, 16 // U2, layers, 0, unroll=V2)
+            value = inward - roll(inward, -1, 1)
+            value = value + across_x[z][rows, :] * (here - field[z][before, :])
+            value = value - across_x[z][after, :] * (field[z][after, :] - here)
+            nearby = from_beside(z, rows, size)
+            if z < NZ - 1:
+                following = field[z + 1][rows, :]
+                to_next = across_z[z + 1][rows, :] * (following - here)
+            else:
+                following, to_next = here, 0.0
+            if z < H - 1:
+                value = shrink * (value + from_last - to_next) + nearby
+            elif z == H - 1:
+                value = shrink * (value + from_last) + nearby - to_next
+            else:
+                value = value + nearby + from_last - to_next
+            yield z, here, value
+            here, from_last = following, to_next
 
     def hand_out(field, power, k):
         return pltpu.make_async_copy(field.at[:, 16:144, :], power, done.at[k])
 
+    def layers_of(ref):
+        return [ref.at[z] for z in range(NZ)]
+
     apply_sides(side0, side1)
-    apply(field0, field1)
+    flow_along_y(field0, range(H, NZ))
+    for z in range(H):
+        value = shrink * image1[z] + from_beside(z, MAIN, 144)
+        if z == H - 1:
+            value = value - across_z[H][MAIN, :] * (field0[H][MAIN, :] - field0[z][MAIN, :])
+        field1[z, MAIN, :] = value
+    for z, _, value in apply_layers(field0, range(H, NZ), 8, 144):
+        field1[z, MAIN, :] = value
     hand_out(field1, power1, 0).start()
     apply_sides(side1, side2)
-    apply(field1, field2)
+    flow_along_y(layers_of(field1), range(NZ))
+    for z, _, value in apply_layers(layers_of(field1), range(NZ), 8, 144):
+        field2[z, MAIN, :] = value
     hand_out(field2, power2, 1).start()
     apply_sides(side2, None)
-    flow_along_y(field2)
-
-    def last(k, sums):
+    flow_along_y(layers_of(field2), range(NZ))
+
+    sums = tuple(jnp.zeros((8, N), F32) for _ in range(6))
+    for group in range(0, NZ, 4):
         for start, size in OWN_ROWS:
             rows = slice(start, start + size)
-            for z, f2, f3 in apply_layers(field2, k * U3, U3, start, size):
+            for z, f2, f3 in apply_layers(layers_of(field2), range(group, group + 4), start, size):
                 field3[z, start - 16 : start - 16 + size, :] = f3
-                f0 = field0[z, rows, :]
+                f0 = field0[z][rows, :]
                 f1 = field1[z, rows, :]
                 terms = (f0 * f0, f0 * f1, f1 * f1, f1 * f2, f2 * f2, f2 * f3)
                 sums = tuple(s + jnp.sum(t.reshape(size // 8, 8, N), axis=0) for s, t in zip(sums, terms))
-        part = pl.ds(k * U3, U3)
+        part = pl.ds(group, 4)
         pltpu.make_async_copy(field3.at[part], power3.at[part], done.at[2]).start()
-        return sums
-
-    sums = lax.fori_loop(0, 16 // U3, last, tuple(jnp.zeros((8, N), F32) for _ in range(6)), unroll=V3)
+
     line = jnp.where((lane[:1] >= 8) & (lane[:1] < 16), top, 0.0)
     for k, s in enumerate(sums):
         amount = jnp.sum(jnp.sum(s, axis=0, keepdims=True), axis=1, keepdims=True)
@@ -694,7 +751,8 @@
 def exchange_pairs(outer, inner, axis):
     count = lax.axis_size(axis)
     across = [(i, (i + 1 if i % 2 else i - 1) % count) for i in range(count)]
-    return lax.ppermute(outer, axis, across), lax.ppermute(inner, axis, [(i, i ^ 1) for i in range(count)])
+    from_partner = lax.ppermute(inner, axis, [(i, i ^ 1) for i in range(count)])
+    return lax.ppermute(outer, axis, across), from_partner
 
 
 def local(noise, biofilm, source):
@@ -751,31 +809,36 @@
         name="rows_own",
         cost=1,
     )(middle2, edge, edge_biofilm)
-    logperm1, largest1 = call(
+    first_layers = shape(H, ROWS, N)
+    sides = pltpu.VMEM((2, ROWS, N), F32)
+    layers = pltpu.VMEM((NZ, ROWS, N), F32)
+    second_layers = pltpu.VMEM((G, ROWS, N), F32)
+    plane = pltpu.VMEM((ROWS, N), F32)
+    first_results = call(
         rows_first,
-        vmem(3),
-        [shape(H, 144, N), shape(8, N)],
-        vmem(2),
+        vmem(5),
+        [shape(8, N)]
+        + [first_layers] * 4
+        + [shape(H, 144, N), shape(ROWS, N), shape(2, ROWS, N), shape(2, ROWS, N)],
+        vmem(9),
+        [pltpu.VMEM((H, 144, N), F32), pltpu.VMEM((H, ROWS, N), F32), pltpu.VMEM((H, ROWS, N), F32)],
         name="rows_first",
         cost=2e10,
-    )(middle1, *above_below1)
+    )(middle1, factor, source, *above_below1)
     devices = lax.axis_size("gx") * lax.axis_size("gy")
-    layers = pltpu.VMEM((NZ, ROWS, N), F32)
-    plane = pltpu.VMEM((ROWS, N), F32)
-    sides = pltpu.VMEM((2, ROWS, N), F32)
     power1, power2, power3, table = call(
         operate_powers,
-        vmem(11),
+        vmem(16),
         [pltpu.HBM((NZ, N, N), F32)] * 3 + [shape(devices, N)],
         hbm(3) + vmem(1),
-        [layers] * 3
-        + [pltpu.VMEM((NZ + 1, ROWS, N), F32)]
-        + [layers] * 4
-        + [block, pltpu.VMEM((G + 1, 144, N), F32), plane, plane]
+        [pltpu.VMEM((G + 1, ROWS, N), F32)]
+        + [second_layers] * 3
+        + [layers, second_layers, layers, layers, block]
+        + [pltpu.VMEM((G + 1, 144, N), F32), plane, plane]
         + [sides] * 8
         + [pltpu.SemaphoreType.DMA((3,))],
         name="powers",
-    )(logperm1, largest1, partial, factor, edge_factor, edge_source, source, *above_below1, *above_below2)
+    )(*first_results, partial, factor, edge_factor, edge_source, source, *above_below2)
     everyone = lax.all_to_all(table, ("gx", "gy"), 0, 0, tiled=True)
     return tuple(
         call(

time: 70.9 us -> 69.5 us (0.980)
  waiting for transfers between devices: 9.79 us -> 8.14 us
    ppermute x4, waiting for transfers between devices: 9.78 us -> 8.13 us  [the longest x2 8.13 us: exchange_pairs(): return (lax.ppermute(outer, axis, across), from_partner)]
  transfers between devices with their start and end apart: 8 -> 8, of which waited for: 2 -> 2; matrix products, arithmetic and copies ran while one was open for 0% -> 0% of each run, Pallas kernels for 8% -> 11%
where the time goes in v6:
time: 69.5 us; the launch traced here: 69.4 us
  blocking collectives  21.6 us (31%)
  starting transfers between devices  21 us (30%)
  Pallas kernels  17.7 us (25%)
  waiting for transfers between devices  8.14 us (12%)
  between operations  0.9 us (1%)
    all_to_all x1, blocking collectives, local(): everyone = lax.all_to_all(table, ('gx', 'gy'), 0, 0, tiled=True)  21.6 us
    ppermute x2, starting transfers between devices, exchange(): lax.ppermute(to_previous, axis, backward)  8.52 us
    ppermute x2, waiting for transfers between devices, exchange_pairs(): return (lax.ppermute(outer, axis, across), from_partner)  8.13 us
    ppermute x2, starting transfers between devices, exchange_pairs(): return (lax.ppermute(outer, axis, across), from_partner)  7.12 us
    pallas_call x1, Pallas kernels, local(): call(operate_powers, vmem(16), [pltpu.HBM((NZ, N, N), F32)] * 3 + [shape(...  5.54 us
    pallas_call x1, Pallas kernels, local(): call(combine, vmem(2) + hbm(4), [pltpu.HBM((NZ, N, N), F32)] * 2, hbm(2),...  3.25 us
    pallas_call x1, Pallas kernels, local(): call(pack_second, vmem(2) + hbm(2), [shape(Y_ROWS[1], N)] * 2, vmem(2), [...  3.04 us
    ppermute x2, starting transfers between devices, exchange_pairs(): from_partner = lax.ppermute(inner, axis, [(i, i ^ 1) for i in range(count)])  2.71 us
  transfers between devices with their start and end apart: 8, of which 2 were waited for; matrix products, arithmetic and copies ran while one was open for 0% of the time, Pallas kernels for 11%

profile of v6, /device:TPU:1, one launch (start us, length us, event | category | flops | bytes accessed | tf_op | source)
XLA Modules:
  0.0 69.4 jit_solution(12229400761633142423)
XLA Ops:
  0.6 0.0 copy-start.1
  0.6 1.5 %pack_first.1 = (f32[640,128]{1,0:T(8,128)S(1)}, f32[640,128]{1,0:T(8,128)S(1)}) custom-call(f32[16,128,128]{2,1,0:T(8,128)} %noise.3), custom_call_target="tpu_custom_call" | custom-call | flops 1000000 | bytes 1000000 | tf_op jit(solution)/shard_map/pack_first/pallas_call | solution.py:760
  2.2 2.5 %collective-permute-start = (f32[640,128]{1,0:T(8,128)S(1)}, f32[640,128]{1,0:T(8,128)S(1)}, u32[]{:S(2)}, u32[]{:S(2)}) collective-permute-start(f32[640,128]{1,0:T(8,128)S(1)} %get-tuple-element.35), channel_id=1, source_target_pairs={{0,1},{1,2},{2,3},{3,4},{4,5},{5,6},{6,7},{7,8},{8,9},{9,10},{10,1... | collective-permute-start | bytes 983048 | tf_op jit(solution)/shard_map/ppermute | solution.py:748
  4.7 0.0 copy-start.2
  4.7 5.0 %collective-permute-start.1 = (f32[640,128]{1,0:T(8,128)S(1)}, f32[640,128]{1,0:T(8,128)S(1)}, u32[]{:S(2)}, u32[]{:S(2)}) collective-permute-start(f32[640,128]{1,0:T(8,128)S(1)} %get-tuple-element.36.after), channel_id=1, source_target_pairs={{1,0},{2,1},{3,2},{4,3},{5,4},{6,5},{7,6},{8,7},{9,8},{10,9},{11,1... | collective-permute-start | bytes 983048 | tf_op jit(solution)/shard_map/ppermute | solution.py:748
  9.7 0.0 copy-done.1
  9.7 3.0 %pack_second.1 = (f32[528,128]{1,0:T(8,128)S(1)}, f32[528,128]{1,0:T(8,128)S(1)}) custom-call(f32[640,128]{1,0:T(8,128)S(1)} %get-tuple-element.36.after, f32[16,128,128]{2,1,0:T(8,128)S(1)} %copy-done.1, f32[16,128,128]{2,1,0:T(8,128)} %source_in.3, s32[16,128,128]{2,1,0:T(8,128)} %biofilm.5), custom_call_target="tpu_custom_call" | custom-call | flops 20000000000 | bytes 20000000000 | tf_op jit(solution)/shard_map/pack_second/pallas_call | solution.py:769
  12.7 0.1 collective-permute-start.4
  12.8 0.0 copy-start
  12.9 3.6 %collective-permute-start.5 = (f32[528,128]{1,0:T(8,128)S(1)}, f32[528,128]{1,0:T(8,128)S(1)}, u32[]{:S(2)}, u32[]{:S(2)}) collective-permute-start(f32[528,128]{1,0:T(8,128)S(1)} %get-tuple-element.53), channel_id=1, source_target_pairs={{1,0},{2,1},{3,2},{4,3},{5,4},{6,5},{7,6},{8,7},{9,8},{10,9},{11,1... | collective-permute-start | bytes 811016 | tf_op jit(solution)/shard_map/ppermute | solution.py:748
  16.4 0.0 copy-done.2
  16.4 0.9 %columns_own.1 = (f32[16,128,128]{2,1,0:T(8,128)S(1)}, f32[128,128]{1,0:T(8,128)S(1)}, f32[16,128,128]{2,1,0:T(8,128)S(1)}) custom-call(f32[16,128,128]{2,1,0:T(8,128)S(1)} %copy-done.1, s32[16,128,128]{2,1,0:T(8,128)S(1)} %copy-done.2), custom_call_target="tpu_custom_call" | custom-call | flops 20000000000 | bytes 20000000000 | tf_op jit(solution)/shard_map/columns_own/pallas_call | solution.py:779
  17.3 0.0 collective-permute-done.from_left
  17.3 0.0 collective-permute-done.1.from_right
  17.3 0.0 copy-done
  17.3 0.7 columns_first.1
  18.0 3.9 %collective-permute-start.2 = (f32[736,128]{1,0:T(8,128)S(1)}, f32[736,128]{1,0:T(8,128)S(1)}, u32[]{:S(2)}, u32[]{:S(2)}) collective-permute-start(f32[736,128]{1,0:T(8,128)S(1)} %get-tuple-element.39), channel_id=1, source_target_pairs={{0,240},{16,32},{32,16},{48,64},{64,48},{80,96},{96,80},{112,128},... | collective-permute-start | bytes 1130504 | tf_op jit(solution)/shard_map/ppermute | solution.py:755
  21.9 1.5 %collective-permute-start.3 = (f32[736,128]{1,0:T(8,128)S(1)}, f32[736,128]{1,0:T(8,128)S(1)}, u32[]{:S(2)}, u32[]{:S(2)}) collective-permute-start(f32[736,128]{1,0:T(8,128)S(1)} %get-tuple-element.40), channel_id=1, source_target_pairs={{0,16},{16,0},{32,48},{48,32},{64,80},{80,64},{96,112},{112,96},{1... | collective-permute-start | bytes 1130504 | tf_op jit(solution)/shard_map/ppermute | solution.py:754
  23.4 0.0 collective-permute-done.4.from_left
  23.4 0.0 collective-permute-done.5.from_right
  23.4 0.5 columns_second.1
  23.9 3.2 %collective-permute-start.6 = (f32[512,128]{1,0:T(8,128)S(1)}, f32[512,128]{1,0:T(8,128)S(1)}, u32[]{:S(2)}, u32[]{:S(2)}) collective-permute-start(f32[512,128]{1,0:T(8,128)S(1)} %get-tuple-element.60), channel_id=1, source_target_pairs={{0,240},{16,32},{32,16},{48,64},{64,48},{80,96},{96,80},{112,128},... | collective-permute-start | bytes 786440 | tf_op jit(solution)/shard_map/ppermute | solution.py:755
  27.1 1.2 %collective-permute-start.7 = (f32[512,128]{1,0:T(8,128)S(1)}, f32[512,128]{1,0:T(8,128)S(1)}, u32[]{:S(2)}, u32[]{:S(2)}) collective-permute-start(f32[512,128]{1,0:T(8,128)S(1)} %get-tuple-element.61), channel_id=1, source_target_pairs={{0,16},{16,0},{32,48},{48,32},{64,80},{80,64},{96,112},{112,96},{1... | collective-permute-start | bytes 786440 | tf_op jit(solution)/shard_map/ppermute | solution.py:754
  28.4 0.2 rows_own.1
  28.6 4.6 %collective-permute-done.2.outer = f32[736,128]{1,0:T(8,128)S(1)} collective-permute-done((f32[736,128]{1,0:T(8,128)S(1)}, f32[736,128]{1,0:T(8,128)S(1)}, u32[]{:S(2)}, u32[]{:S(2)}) %collective-permute-start.2) | collective-permute-done | bytes 376864 | tf_op jit(solution)/shard_map/ppermute | solution.py:755
  33.2 0.0 collective-permute-done.3.inner
  33.2 2.1 %rows_first.1 = (f32[8,128]{1,0:T(8,128)S(1)}, f32[10,160,128]{2,1,0:T(8,128)S(1)}, f32[10,160,128]{2,1,0:T(8,128)S(1)}, f32[10,160,128]{2,1,0:T(8,128)S(1)}, f3...) custom-call(f32[10,128,128]{2,1,0:T(8,128)S(1)} %get-tuple-element.3, ...), custom_call_target="tpu_custom_call" | custom-call | flops 20000000000 | bytes 20000000000 | tf_op jit(solution)/shard_map/rows_first/pallas_call | solution.py:817
  35.2 3.6 %collective-permute-done.6.outer2 = f32[512,128]{1,0:T(8,128)S(1)} collective-permute-done((f32[512,128]{1,0:T(8,128)S(1)}, f32[512,128]{1,0:T(8,128)S(1)}, u32[]{:S(2)}, u32[]{:S(2)}) %collective-permute-start.6) | collective-permute-done | bytes 262176 | tf_op jit(solution)/shard_map/ppermute | solution.py:755
  38.8 0.0 collective-permute-done.7.inner2
  38.8 5.5 %powers.1 = (f32[16,128,128]{2,1,0:T(8,128)}, f32[16,128,128]{2,1,0:T(8,128)}, f32[16,128,128]{2,1,0:T(8,128)}, f32[256,128]{1,0:T(8,128)S(1)}) custom-call(f32[8,128]{1,0:T(8,128)S(1)} %get-tuple-element.41.largest1, f32[10,160,128]{2,1,0:T(8,128)S(1)} %get-tuple-element.42.field0_1, f32[10,160,128]{2,1,0:T(8,128)S(1)} %get-tuple-element.43.across_x1, ...), custom_call_target="tpu_custom_call" | custom-call | flops 1000000 | bytes 1000000 | tf_op jit(solution)/shard_map/powers/pallas_call | solution.py:829
  44.3 21.6 %all_to_all.11 = f32[256,1,128]{2,1,0:T(1,128)S(1)} all-to-all(f32[256,1,128]{2,1,0:T(1,128)S(1)} %bitcast.4), channel_id=1, replica_groups=mesh['gx'=16,'gy'=16] {'gx','gy'}, dimensions={0} | all-to-all | bytes 262144 | tf_op jit(solution)/shard_map/all_to_all | solution.py:842
  66.0 3.3 %combine.1 = (f32[16,128,128]{2,1,0:T(8,128)}, f32[16,128,128]{2,1,0:T(8,128)}) custom-call(f32[256,128]{1,0:T(8,128)S(1)} %bitcast.5, f32[256,128]{1,0:T(8,128)S(1)} %get-tuple-element.62.own, f32[16,128,128]{2,1,0:T(8,128)} %source_in.3, f32[16,128,128]{2,1,0:T(8,128)} %get-tuple-element.63.power1_in, f32[16,128,128]{2,1,0:T(8,128)} %get-tuple-element.64.power2_in, ...), custom_call_target="tpu_custom_call" | custom-call | flops 1000000 | bytes 1000000 | tf_op jit(solution)/shard_map/combine/pallas_call | solution.py:844
Async XLA Ops:
  0.6 9.1 %copy-start.1 = (f32[16,128,128]{2,1,0:T(8,128)S(1)}, f32[16,128,128]{2,1,0:T(8,128)}, u32[]{:S(2)}) copy-start(f32[16,128,128]{2,1,0:T(8,128)} %noise.3) | copy-start | bytes 3145732
  2.2 15.1 %collective-permute-start = (f32[640,128]{1,0:T(8,128)S(1)}, f32[640,128]{1,0:T(8,128)S(1)}, u32[]{:S(2)}, u32[]{:S(2)}) collective-permute-start(f32[640,128]{1,0:T(8,128)S(1)} %get-tuple-element.35), channel_id=1, source_target_pairs={{0,1},{1,2},{2,3},{3,4},{4,5},{5,6},{6,7},{7,8},{8,9},{9,10},{10,1... | collective-permute-start | bytes 983048 | tf_op jit(solution)/shard_map/ppermute | solution.py:748
  4.7 11.7 %copy-start.2 = (s32[16,128,128]{2,1,0:T(8,128)S(1)}, s32[16,128,128]{2,1,0:T(8,128)}, u32[]{:S(2)}) copy-start(s32[16,128,128]{2,1,0:T(8,128)} %biofilm.5) | copy-start | bytes 3145732
  4.7 12.6 %collective-permute-start.1 = (f32[640,128]{1,0:T(8,128)S(1)}, f32[640,128]{1,0:T(8,128)S(1)}, u32[]{:S(2)}, u32[]{:S(2)}) collective-permute-start(f32[640,128]{1,0:T(8,128)S(1)} %get-tuple-element.36.after), channel_id=1, source_target_pairs={{1,0},{2,1},{3,2},{4,3},{5,4},{6,5},{7,6},{8,7},{9,8},{10,9},{11,1... | collective-permute-start | bytes 983048 | tf_op jit(solution)/shard_map/ppermute | solution.py:748
  12.7 10.6 %collective-permute-start.4 = (f32[528,128]{1,0:T(8,128)S(1)}, f32[528,128]{1,0:T(8,128)S(1)}, u32[]{:S(2)}, u32[]{:S(2)}) collective-permute-start(f32[528,128]{1,0:T(8,128)S(1)} %get-tuple-element.52), channel_id=1, source_target_pairs={{0,1},{1,2},{2,3},{3,4},{4,5},{5,6},{6,7},{7,8},{8,9},{9,10},{10,1... | collective-permute-start | bytes 811016 | tf_op jit(solution)/shard_map/ppermute | solution.py:748
  12.8 4.5 %copy-start = (f32[16,128,128]{2,1,0:T(8,128)S(1)}, f32[16,128,128]{2,1,0:T(8,128)}, u32[]{:S(2)}) copy-start(f32[16,128,128]{2,1,0:T(8,128)} %source_in.3) | copy-start | bytes 3145732
  12.9 10.5 %collective-permute-start.5 = (f32[528,128]{1,0:T(8,128)S(1)}, f32[528,128]{1,0:T(8,128)S(1)}, u32[]{:S(2)}, u32[]{:S(2)}) collective-permute-start(f32[528,128]{1,0:T(8,128)S(1)} %get-tuple-element.53), channel_id=1, source_target_pairs={{1,0},{2,1},{3,2},{4,3},{5,4},{6,5},{7,6},{8,7},{9,8},{10,9},{11,1... | collective-permute-start | bytes 811016 | tf_op jit(solution)/shard_map/ppermute | solution.py:748
  18.0 15.2 %collective-permute-start.2 = (f32[736,128]{1,0:T(8,128)S(1)}, f32[736,128]{1,0:T(8,128)S(1)}, u32[]{:S(2)}, u32[]{:S(2)}) collective-permute-start(f32[736,128]{1,0:T(8,128)S(1)} %get-tuple-element.39), channel_id=1, source_target_pairs={{0,240},{16,32},{32,16},{48,64},{64,48},{80,96},{96,80},{112,128},... | collective-permute-start | bytes 1130504 | tf_op jit(solution)/shard_map/ppermute | solution.py:755
  21.9 11.3 %collective-permute-start.3 = (f32[736,128]{1,0:T(8,128)S(1)}, f32[736,128]{1,0:T(8,128)S(1)}, u32[]{:S(2)}, u32[]{:S(2)}) collective-permute-start(f32[736,128]{1,0:T(8,128)S(1)} %get-tuple-element.40), channel_id=1, source_target_pairs={{0,16},{16,0},{32,48},{48,32},{64,80},{80,64},{96,112},{112,96},{1... | collective-permute-start | bytes 1130504 | tf_op jit(solution)/shard_map/ppermute | solution.py:754
  23.9 14.9 %collective-permute-start.6 = (f32[512,128]{1,0:T(8,128)S(1)}, f32[512,128]{1,0:T(8,128)S(1)}, u32[]{:S(2)}, u32[]{:S(2)}) collective-permute-start(f32[512,128]{1,0:T(8,128)S(1)} %get-tuple-element.60), channel_id=1, source_target_pairs={{0,240},{16,32},{32,16},{48,64},{64,48},{80,96},{96,80},{112,128},... | collective-permute-start | bytes 786440 | tf_op jit(solution)/shard_map/ppermute | solution.py:755
  27.1 11.7 %collective-permute-start.7 = (f32[512,128]{1,0:T(8,128)S(1)}, f32[512,128]{1,0:T(8,128)S(1)}, u32[]{:S(2)}, u32[]{:S(2)}) collective-permute-start(f32[512,128]{1,0:T(8,128)S(1)} %get-tuple-element.61), channel_id=1, source_target_pairs={{0,16},{16,0},{32,48},{48,32},{64,80},{80,64},{96,112},{112,96},{1... | collective-permute-start | bytes 786440 | tf_op jit(solution)/shard_map/ppermute | solution.py:754

commit v7 on v6

--- a/solution.py
+++ b/solution.py
@@ -154,7 +154,7 @@
     return [weights(w) for w in (own, left, right, left_extra, right_extra)]
 
 
-def column_sums_own(noise, biofilm, own_middle, own_edge, factor):
+def column_sums_own(noise, own_middle, own_edge):
     own = column_weights()[0]
     twice = jnp.concatenate([own, own], axis=0)
     total = jnp.zeros((N, N), F32)
@@ -162,7 +162,6 @@
         out = dot(jnp.concatenate(split2(noise[z]), axis=1), twice)
         own_middle[z] = out[:, :N]
         total = total + roll(out[:, N:], 8 * z, 1)
-        factor[z] = resistance_factor(biofilm[z].astype(F32))
     own_edge[...] = total
 
 
@@ -300,12 +299,14 @@
     return jnp.max(jnp.where(real, total, -HUGE).reshape(18, 8, N), axis=0)
 
 
-def row_sums_own(middle, edge, edge_biofilm, partial, factor):
+def row_sums_own(middle, edge, biofilm, edge_biofilm, partial, factor, edge_factor):
     own, _ = row_weights()
     for z in range(0, G, 2):
         partial[z], partial[z + 1] = row_sums(own, middle[z], middle[z + 1])
     partial[G] = row_sums(own, edge[...])[0]
-    factor[...] = resistance_factor(edge_biofilm[...])
+    for z in range(NZ):
+        factor[z] = resistance_factor(biofilm[z].astype(F32))
+    edge_factor[...] = resistance_factor(edge_biofilm[...])
 
 
 def resistance_factor(biofilm):
@@ -776,14 +777,14 @@
         cost=2e10,
     )(to_left, noise, in_hbm(source), in_hbm(biofilm))
     beside2 = exchange(to_right, to_left, "gy")
-    own_middle, own_edge, factor = call(
+    own_middle, own_edge = call(
         column_sums_own,
+        vmem(1),
+        [shape(NZ, N, N), shape(N, N)],
         vmem(2),
-        [shape(NZ, N, N), shape(N, N), shape(NZ, N, N)],
-        vmem(3),
         name="columns_own",
         cost=2e10,
-    )(noise, biofilm)
+    )(noise)
     middle1, first_edge, outer, inner = call(
         columns_first,
         vmem(5),
@@ -801,14 +802,14 @@
         cost=2e10,
     )(own_middle, own_edge, first_edge, source, biofilm, *beside2)
     above_below2 = exchange_pairs(outer, inner, "gx")
-    partial, edge_factor = call(
+    partial, factor, edge_factor = call(
         row_sums_own,
+        vmem(4),
+        [shape(G + 1, 144, N), shape(NZ, N, N), shape(N, N)],
         vmem(3),
-        [shape(G + 1, 144, N), shape(N, N)],
-        vmem(2),
         name="rows_own",
         cost=1,
-    )(middle2, edge, edge_biofilm)
+    )(middle2, edge, biofilm, edge_biofilm)
     first_layers = shape(H, ROWS, N)
     sides = pltpu.VMEM((2, ROWS, N), F32)
     layers = pltpu.VMEM((NZ, ROWS, N), F32)

time: 69.5 us -> 69.7 us (level)
  transfers between devices with their start and end apart: 8 -> 8, of which waited for: 2 -> 3; matrix products, arithmetic and copies ran while one was open for 0% -> 0% of each run, Pallas kernels for 11% -> 11%
where the time goes in v7:
time: 69.7 us; the launch traced here: 69.5 us
  blocking collectives  21.6 us (31%)
  starting transfers between devices  21.2 us (30%)
  Pallas kernels  18 us (26%)
  waiting for transfers between devices  7.82 us (11%)
  between operations  0.89 us (1%)
    all_to_all x1, blocking collectives, local(): everyone = lax.all_to_all(table, ('gx', 'gy'), 0, 0, tiled=True)  21.6 us
    ppermute x2, starting transfers between devices, exchange(): lax.ppermute(to_previous, axis, backward)  8.5 us
    ppermute x2, waiting for transfers between devices, exchange_pairs(): return (lax.ppermute(outer, axis, across), from_partner)  7.7 us
    ppermute x2, starting transfers between devices, exchange_pairs(): return (lax.ppermute(outer, axis, across), from_partner)  7.31 us
    pallas_call x1, Pallas kernels, local(): call(operate_powers, vmem(16), [pltpu.HBM((NZ, N, N), F32)] * 3 + [shape(...  5.72 us
    pallas_call x1, Pallas kernels, local(): call(combine, vmem(2) + hbm(4), [pltpu.HBM((NZ, N, N), F32)] * 2, hbm(2),...  3.25 us
    pallas_call x1, Pallas kernels, local(): call(pack_second, vmem(2) + hbm(2), [shape(Y_ROWS[1], N)] * 2, vmem(2), [...  3.04 us
    ppermute x2, starting transfers between devices, exchange_pairs(): from_partner = lax.ppermute(inner, axis, [(i, i ^ 1) for i in range(count)])  2.79 us
  transfers between devices with their start and end apart: 8, of which 3 were waited for; matrix products, arithmetic and copies ran while one was open for 0% of the time, Pallas kernels for 11%

profile of v7, /device:TPU:1, one launch (start us, length us, event | category | flops | bytes accessed | tf_op | source)
XLA Modules:
  0.0 69.5 jit_solution(16538587756837116353)
XLA Ops:
  0.6 0.0 copy-start.2
  0.6 1.5 %pack_first.1 = (f32[640,128]{1,0:T(8,128)S(1)}, f32[640,128]{1,0:T(8,128)S(1)}) custom-call(f32[16,128,128]{2,1,0:T(8,128)} %noise.3), custom_call_target="tpu_custom_call" | custom-call | flops 1000000 | bytes 1000000 | tf_op jit(solution)/shard_map/pack_first/pallas_call | solution.py:761
  2.2 2.5 %collective-permute-start = (f32[640,128]{1,0:T(8,128)S(1)}, f32[640,128]{1,0:T(8,128)S(1)}, u32[]{:S(2)}, u32[]{:S(2)}) collective-permute-start(f32[640,128]{1,0:T(8,128)S(1)} %get-tuple-element.35), channel_id=1, source_target_pairs={{0,1},{1,2},{2,3},{3,4},{4,5},{5,6},{6,7},{7,8},{8,9},{9,10},{10,1... | collective-permute-start | bytes 983048 | tf_op jit(solution)/shard_map/ppermute | solution.py:749
  4.7 5.0 %collective-permute-start.1 = (f32[640,128]{1,0:T(8,128)S(1)}, f32[640,128]{1,0:T(8,128)S(1)}, u32[]{:S(2)}, u32[]{:S(2)}) collective-permute-start(f32[640,128]{1,0:T(8,128)S(1)} %get-tuple-element.36.after), channel_id=1, source_target_pairs={{1,0},{2,1},{3,2},{4,3},{5,4},{6,5},{7,6},{8,7},{9,8},{10,9},{11,1... | collective-permute-start | bytes 983048 | tf_op jit(solution)/shard_map/ppermute | solution.py:749
  9.7 0.0 copy-done.2
  9.7 3.0 %pack_second.1 = (f32[528,128]{1,0:T(8,128)S(1)}, f32[528,128]{1,0:T(8,128)S(1)}) custom-call(f32[640,128]{1,0:T(8,128)S(1)} %get-tuple-element.36.after, f32[16,128,128]{2,1,0:T(8,128)S(1)} %copy-done.2, f32[16,128,128]{2,1,0:T(8,128)} %source_in.3, s32[16,128,128]{2,1,0:T(8,128)} %biofilm.5), custom_call_target="tpu_custom_call" | custom-call | flops 20000000000 | bytes 20000000000 | tf_op jit(solution)/shard_map/pack_second/pallas_call | solution.py:770
  12.7 0.1 collective-permute-start.2
  12.8 0.0 copy-start
  12.8 0.0 copy-start.1
  12.9 3.5 %collective-permute-start.3 = (f32[528,128]{1,0:T(8,128)S(1)}, f32[528,128]{1,0:T(8,128)S(1)}, u32[]{:S(2)}, u32[]{:S(2)}) collective-permute-start(f32[528,128]{1,0:T(8,128)S(1)} %get-tuple-element.41), channel_id=1, source_target_pairs={{1,0},{2,1},{3,2},{4,3},{5,4},{6,5},{7,6},{8,7},{9,8},{10,9},{11,1... | collective-permute-start | bytes 811016 | tf_op jit(solution)/shard_map/ppermute | solution.py:749
  16.4 0.5 columns_own.1
  16.9 0.1 collective-permute-done.from_left
  17.0 0.0 collective-permute-done.1.from_right
  17.0 0.0 copy-done
  17.0 0.0 copy-done.1
  17.0 0.7 columns_first.1
  17.7 3.8 %collective-permute-start.4 = (f32[736,128]{1,0:T(8,128)S(1)}, f32[736,128]{1,0:T(8,128)S(1)}, u32[]{:S(2)}, u32[]{:S(2)}) collective-permute-start(f32[736,128]{1,0:T(8,128)S(1)} %get-tuple-element.46), channel_id=1, source_target_pairs={{0,240},{16,32},{32,16},{48,64},{64,48},{80,96},{96,80},{112,128},... | collective-permute-start | bytes 1130504 | tf_op jit(solution)/shard_map/ppermute | solution.py:756
  21.5 1.5 %collective-permute-start.5 = (f32[736,128]{1,0:T(8,128)S(1)}, f32[736,128]{1,0:T(8,128)S(1)}, u32[]{:S(2)}, u32[]{:S(2)}) collective-permute-start(f32[736,128]{1,0:T(8,128)S(1)} %get-tuple-element.47), channel_id=1, source_target_pairs={{0,16},{16,0},{32,48},{48,32},{64,80},{80,64},{96,112},{112,96},{1... | collective-permute-start | bytes 1130504 | tf_op jit(solution)/shard_map/ppermute | solution.py:755
  23.1 0.0 collective-permute-done.2.from_left
  23.1 0.0 collective-permute-done.3.from_right
  23.1 0.5 columns_second.1
  23.6 3.5 %collective-permute-start.6 = (f32[512,128]{1,0:T(8,128)S(1)}, f32[512,128]{1,0:T(8,128)S(1)}, u32[]{:S(2)}, u32[]{:S(2)}) collective-permute-start(f32[512,128]{1,0:T(8,128)S(1)} %get-tuple-element.60), channel_id=1, source_target_pairs={{0,240},{16,32},{32,16},{48,64},{64,48},{80,96},{96,80},{112,128},... | collective-permute-start | bytes 786440 | tf_op jit(solution)/shard_map/ppermute | solution.py:756
  27.1 1.2 %collective-permute-start.7 = (f32[512,128]{1,0:T(8,128)S(1)}, f32[512,128]{1,0:T(8,128)S(1)}, u32[]{:S(2)}, u32[]{:S(2)}) collective-permute-start(f32[512,128]{1,0:T(8,128)S(1)} %get-tuple-element.61), channel_id=1, source_target_pairs={{0,16},{16,0},{32,48},{48,32},{64,80},{80,64},{96,112},{112,96},{1... | collective-permute-start | bytes 786440 | tf_op jit(solution)/shard_map/ppermute | solution.py:755
  28.4 0.6 rows_own.1
  29.0 4.2 %collective-permute-done.4.outer = f32[736,128]{1,0:T(8,128)S(1)} collective-permute-done((f32[736,128]{1,0:T(8,128)S(1)}, f32[736,128]{1,0:T(8,128)S(1)}, u32[]{:S(2)}, u32[]{:S(2)}) %collective-permute-start.4) | collective-permute-done | bytes 376864 | tf_op jit(solution)/shard_map/ppermute | solution.py:756
  33.2 0.0 collective-permute-done.5.inner
  33.2 2.1 %rows_first.1 = (f32[8,128]{1,0:T(8,128)S(1)}, f32[10,160,128]{2,1,0:T(8,128)S(1)}, f32[10,160,128]{2,1,0:T(8,128)S(1)}, f32[10,160,128]{2,1,0:T(8,128)S(1)}, f3...) custom-call(f32[10,128,128]{2,1,0:T(8,128)S(1)} %get-tuple-element.3, ...), custom_call_target="tpu_custom_call" | custom-call | flops 20000000000 | bytes 20000000000 | tf_op jit(solution)/shard_map/rows_first/pallas_call | solution.py:818
  35.3 3.5 %collective-permute-done.6.outer2 = f32[512,128]{1,0:T(8,128)S(1)} collective-permute-done((f32[512,128]{1,0:T(8,128)S(1)}, f32[512,128]{1,0:T(8,128)S(1)}, u32[]{:S(2)}, u32[]{:S(2)}) %collective-permute-start.6) | collective-permute-done | bytes 262176 | tf_op jit(solution)/shard_map/ppermute | solution.py:756
  38.8 0.0 collective-permute-done.7.inner2
  38.8 5.7 %powers.1 = (f32[16,128,128]{2,1,0:T(8,128)}, f32[16,128,128]{2,1,0:T(8,128)}, f32[16,128,128]{2,1,0:T(8,128)}, f32[256,128]{1,0:T(8,128)S(1)}) custom-call(f32[8,128]{1,0:T(8,128)S(1)} %get-tuple-element.48.largest1, f32[10,160,128]{2,1,0:T(8,128)S(1)} %get-tuple-element.49.field0_1, f32[10,160,128]{2,1,0:T(8,128)S(1)} %get-tuple-element.50.across_x1, ...), custom_call_target="tpu_custom_call" | custom-call | flops 1000000 | bytes 1000000 | tf_op jit(solution)/shard_map/powers/pallas_call | solution.py:830
  44.5 21.6 %all_to_all.11 = f32[256,1,128]{2,1,0:T(1,128)S(1)} all-to-all(f32[256,1,128]{2,1,0:T(1,128)S(1)} %bitcast.4), channel_id=1, replica_groups=mesh['gx'=16,'gy'=16] {'gx','gy'}, dimensions={0} | all-to-all | bytes 262144 | tf_op jit(solution)/shard_map/all_to_all | solution.py:843
  66.1 3.3 %combine.1 = (f32[16,128,128]{2,1,0:T(8,128)}, f32[16,128,128]{2,1,0:T(8,128)}) custom-call(f32[256,128]{1,0:T(8,128)S(1)} %bitcast.5, f32[256,128]{1,0:T(8,128)S(1)} %get-tuple-element.62.own, f32[16,128,128]{2,1,0:T(8,128)} %source_in.3, f32[16,128,128]{2,1,0:T(8,128)} %get-tuple-element.63.power1_in, f32[16,128,128]{2,1,0:T(8,128)} %get-tuple-element.64.power2_in, ...), custom_call_target="tpu_custom_call" | custom-call | flops 1000000 | bytes 1000000 | tf_op jit(solution)/shard_map/combine/pallas_call | solution.py:845
Async XLA Ops:
  0.6 9.1 %copy-start.2 = (f32[16,128,128]{2,1,0:T(8,128)S(1)}, f32[16,128,128]{2,1,0:T(8,128)}, u32[]{:S(2)}) copy-start(f32[16,128,128]{2,1,0:T(8,128)} %noise.3) | copy-start | bytes 3145732
  2.2 14.8 %collective-permute-start = (f32[640,128]{1,0:T(8,128)S(1)}, f32[640,128]{1,0:T(8,128)S(1)}, u32[]{:S(2)}, u32[]{:S(2)}) collective-permute-start(f32[640,128]{1,0:T(8,128)S(1)} %get-tuple-element.35), channel_id=1, source_target_pairs={{0,1},{1,2},{2,3},{3,4},{4,5},{5,6},{6,7},{7,8},{8,9},{9,10},{10,1... | collective-permute-start | bytes 983048 | tf_op jit(solution)/shard_map/ppermute | solution.py:749
  4.7 12.3 %collective-permute-start.1 = (f32[640,128]{1,0:T(8,128)S(1)}, f32[640,128]{1,0:T(8,128)S(1)}, u32[]{:S(2)}, u32[]{:S(2)}) collective-permute-start(f32[640,128]{1,0:T(8,128)S(1)} %get-tuple-element.36.after), channel_id=1, source_target_pairs={{1,0},{2,1},{3,2},{4,3},{5,4},{6,5},{7,6},{8,7},{9,8},{10,9},{11,1... | collective-permute-start | bytes 983048 | tf_op jit(solution)/shard_map/ppermute | solution.py:749
  12.7 10.4 %collective-permute-start.2 = (f32[528,128]{1,0:T(8,128)S(1)}, f32[528,128]{1,0:T(8,128)S(1)}, u32[]{:S(2)}, u32[]{:S(2)}) collective-permute-start(f32[528,128]{1,0:T(8,128)S(1)} %get-tuple-element.40), channel_id=1, source_target_pairs={{0,1},{1,2},{2,3},{3,4},{4,5},{5,6},{6,7},{7,8},{8,9},{9,10},{10,1... | collective-permute-start | bytes 811016 | tf_op jit(solution)/shard_map/ppermute | solution.py:749
  12.8 4.2 %copy-start = (f32[16,128,128]{2,1,0:T(8,128)S(1)}, f32[16,128,128]{2,1,0:T(8,128)}, u32[]{:S(2)}) copy-start(f32[16,128,128]{2,1,0:T(8,128)} %source_in.3) | copy-start | bytes 3145732
  12.8 4.2 %copy-start.1 = (s32[16,128,128]{2,1,0:T(8,128)S(1)}, s32[16,128,128]{2,1,0:T(8,128)}, u32[]{:S(2)}) copy-start(s32[16,128,128]{2,1,0:T(8,128)} %biofilm.5) | copy-start | bytes 3145732
  12.9 10.2 %collective-permute-start.3 = (f32[528,128]{1,0:T(8,128)S(1)}, f32[528,128]{1,0:T(8,128)S(1)}, u32[]{:S(2)}, u32[]{:S(2)}) collective-permute-start(f32[528,128]{1,0:T(8,128)S(1)} %get-tuple-element.41), channel_id=1, source_target_pairs={{1,0},{2,1},{3,2},{4,3},{5,4},{6,5},{7,6},{8,7},{9,8},{10,9},{11,1... | collective-permute-start | bytes 811016 | tf_op jit(solution)/shard_map/ppermute | solution.py:749
  17.7 15.5 %collective-permute-start.4 = (f32[736,128]{1,0:T(8,128)S(1)}, f32[736,128]{1,0:T(8,128)S(1)}, u32[]{:S(2)}, u32[]{:S(2)}) collective-permute-start(f32[736,128]{1,0:T(8,128)S(1)} %get-tuple-element.46), channel_id=1, source_target_pairs={{0,240},{16,32},{32,16},{48,64},{64,48},{80,96},{96,80},{112,128},... | collective-permute-start | bytes 1130504 | tf_op jit(solution)/shard_map/ppermute | solution.py:756
  21.5 11.6 %collective-permute-start.5 = (f32[736,128]{1,0:T(8,128)S(1)}, f32[736,128]{1,0:T(8,128)S(1)}, u32[]{:S(2)}, u32[]{:S(2)}) collective-permute-start(f32[736,128]{1,0:T(8,128)S(1)} %get-tuple-element.47), channel_id=1, source_target_pairs={{0,16},{16,0},{32,48},{48,32},{64,80},{80,64},{96,112},{112,96},{1... | collective-permute-start | bytes 1130504 | tf_op jit(solution)/shard_map/ppermute | solution.py:755
  23.6 15.1 %collective-permute-start.6 = (f32[512,128]{1,0:T(8,128)S(1)}, f32[512,128]{1,0:T(8,128)S(1)}, u32[]{:S(2)}, u32[]{:S(2)}) collective-permute-start(f32[512,128]{1,0:T(8,128)S(1)} %get-tuple-element.60), channel_id=1, source_target_pairs={{0,240},{16,32},{32,16},{48,64},{64,48},{80,96},{96,80},{112,128},... | collective-permute-start | bytes 786440 | tf_op jit(solution)/shard_map/ppermute | solution.py:756
  27.1 11.7 %collective-permute-start.7 = (f32[512,128]{1,0:T(8,128)S(1)}, f32[512,128]{1,0:T(8,128)S(1)}, u32[]{:S(2)}, u32[]{:S(2)}) collective-permute-start(f32[512,128]{1,0:T(8,128)S(1)} %get-tuple-element.61), channel_id=1, source_target_pairs={{0,16},{16,0},{32,48},{48,32},{64,80},{80,64},{96,112},{112,96},{1... | collective-permute-start | bytes 786440 | tf_op jit(solution)/shard_map/ppermute | solution.py:755
